TPU v7x, 32 devices: a whole 2x2x4 slice. The times are simulated.
32 devices in a mesh: tile: 8 (over y, x, core), kern: 4 (over z).
Axes of the slice: x: 2, y: 2, z: 4, core: 2. Of those that a mesh axis runs over, the one named last changes fastest.
Arguments:
- mask_pixels: bfloat16 [1152, 9216], P(None, 'tile'), may hold values from -6 to 6
- orientation: int32 [8, 2], P('tile'), may hold values 0 or 1
- target_pattern: int32 [1152, 9216], P('kern', 'tile'), may hold values 0 or 1
- kernel_real: float32 [4, 64, 64], P('kern'), may hold values from -6 to 6
- kernel_imag: float32 [4, 64, 64], P('kern'), may hold values from -6 to 6
- eigen_weights: float32 [4], P('kern'), may hold values from 0.01 to 0.1
Outputs:
- mask_gradient: float32 [1152, 9216], P('kern', 'tile')
Inputs may be any that keep to these rules, and one draw needn't show every extreme that they name: `orientation`: 1 takes the neighbour's facing strip in order, 0 reversed; the entry for a side without neighbour is unused.
All inputs are finite; a program needn't handle non-finite values. No bound on the sum of `orientation` or of `target_pattern` on one device may be relied on, other than what follows from the above.
Results may differ from a plain program's by a relative error of at most 0.018.
Values may be sent and summed in bfloat16 or wider, within the bound.
No kernel may reach another device: no remote copies, remote signals or barrier semaphores. Data moves between devices by JAX's collectives and lax.ppermute only.
A program may use at most 64 MiB of HBM per device.

v0:
```python
import functools
import math

import jax
import jax.numpy as jnp
import ml_dtypes
import numpy as np
from jax import lax
from jax.experimental import pallas as pl
from jax.experimental.pallas import tpu as pltpu
from jax.sharding import PartitionSpec as P

N = 1152
HALO = 64
KF = 64
NE = 1280
LANES = 128
PAIR = 2 * KF
BLOCKS = N // LANES
EDGE = KF
MARKS = 16
BF16 = jnp.bfloat16
F32 = jnp.float32
VMEM_LIMIT = 32 * 1024 * 1024


def wave_tables():
    position = np.arange(NE)[:, None]
    frequency = np.arange(KF)[None, :] - KF // 2
    phase = np.mod(position * frequency, NE).astype(np.float64) * (2.0 * math.pi / NE)
    return np.cos(phase).astype(np.float32), np.sin(phase).astype(np.float32)


def transform_tables():
    cos, sin = wave_tables()
    full = np.concatenate([cos, sin], 1)
    mid = full[HALO : HALO + N]
    ct, st = cos[HALO : HALO + N].T, sin[HALO : HALO + N].T
    columns = np.concatenate(
        [
            np.stack([ct.reshape(KF, BLOCKS, LANES), st.reshape(KF, BLOCKS, LANES)], 2),
            np.stack([-st.reshape(KF, BLOCKS, LANES), ct.reshape(KF, BLOCKS, LANES)], 2),
        ],
        0,
    )
    to_columns = columns.transpose(1, 0, 2, 3).reshape(BLOCKS, PAIR, 2 * LANES)
    from_columns = to_columns.transpose(0, 2, 1)
    low, high = full[:HALO], full[HALO + N :]
    blank = np.zeros((HALO, PAIR), np.float32)
    rims = np.stack(
        [
            np.concatenate([low[::-1], blank], 0),
            np.concatenate([low, blank], 0),
            np.concatenate([high[::-1], blank], 0),
            np.concatenate([high, blank], 0),
        ]
    )
    back = np.concatenate([cos.T, -sin.T], 0)
    back_low, back_high = back[:, :HALO], back[:, HALO + N :]
    blank = np.zeros((PAIR, HALO), np.float32)
    margins = np.stack(
        [
            np.concatenate([back_high[:, ::-1], blank], 1),
            np.concatenate([back_high, blank], 1),
            np.concatenate([blank, back_low[:, ::-1]], 1),
            np.concatenate([blank, back_low], 1),
        ]
    )
    tables = (mid, mid.T, to_columns, from_columns, rims, back[:, HALO : HALO + N], margins)
    return tuple(np.ascontiguousarray(one).astype(ml_dtypes.bfloat16) for one in tables)


def dot(a, b):
    return jnp.dot(a, b, preferred_element_type=F32)


def in_left_half(shape):
    return lax.broadcasted_iota(jnp.int32, shape, 1) < KF


def swap_halves(pair):
    return pltpu.roll(pair, KF, 1)


def destination(k, step, count):
    return k ^ step if count == 4 else (k - step) % count


def call(
    body, name, outs, args, specs, out_specs=None, scratch=(), flops=0, moved=0
):
    vmem = pl.BlockSpec(memory_space=pltpu.VMEM)
    if out_specs is None:
        out_specs = tuple(vmem for _ in outs) if isinstance(outs, tuple) else vmem
    return pl.pallas_call(
        body,
        name=name,
        out_shape=outs,
        in_specs=specs,
        out_specs=out_specs,
        scratch_shapes=list(scratch),
        compiler_params=pltpu.CompilerParams(vmem_limit_bytes=VMEM_LIMIT),
        cost_estimate=pl.CostEstimate(flops=flops, bytes_accessed=moved, transcendentals=0),
    )(*args)


def edges_body(
    mask, mid, mid_t, real, imag, weight, flags, mate, other, side, held, tall, table, sides_out, pair, marks, sems
):
    odd = lax.rem(lax.axis_index("tile"), 2) == 1
    copies = [
        pltpu.make_async_copy(mid_t, table, sems.at[0]),
        pltpu.make_async_copy(mask.at[:, :LANES], held.at[:, :LANES], sems.at[1]),
        pltpu.make_async_copy(mask.at[:, N - LANES :], held.at[:, N - LANES :], sems.at[2]),
        pltpu.make_async_copy(real.at[0], pair.at[0], sems.at[3]),
        pltpu.make_async_copy(imag.at[0], pair.at[1], sems.at[4]),
        pltpu.make_async_copy(flags, marks, sems.at[5]),
    ]
    inner = pltpu.make_async_copy(
        mask.at[:, LANES : N - LANES], held.at[:, LANES : N - LANES], sems.at[6]
    )
    columns = pltpu.make_async_copy(mid, tall, sems.at[7])
    for copy in copies:
        copy.start()
    inner.start()
    columns.start()
    for copy in copies[3:]:
        copy.wait()
    scale = jnp.sqrt(jnp.full((KF, KF), 2.0 * weight[0], F32)) * (1.0 / (NE * KF))
    kernel = jnp.concatenate([pair[0] * scale, pair[1] * scale], 1).astype(BF16)
    row = lax.broadcasted_iota(jnp.int32, (16, LANES), 0)
    sides = jnp.where(row == 0, marks[0, 0].astype(F32), marks[0, 1].astype(F32)).astype(BF16)
    side[...] = kernel
    mate[EDGE : 2 * EDGE, :] = kernel
    mate[2 * EDGE :, :] = sides
    other[EDGE:, :] = sides
    sides_out[...] = sides
    for copy in copies[:3]:
        copy.wait()
    strips = jnp.concatenate([held[:, :LANES], held[:, N - LANES :]], 1)
    both = dot(table[...], strips)
    left = in_left_half((KF, LANES))
    first, last = both[:, :LANES], both[:, LANES:]
    first = jnp.where(left, first[:KF], swap_halves(first[KF:]))
    last = jnp.where(left, swap_halves(last[:KF]), last[KF:])
    mate[:EDGE, :] = jnp.where(odd, first, last).astype(BF16)
    other[:EDGE, :] = jnp.where(odd, last, first).astype(BF16)
    inner.wait()
    columns.wait()


def middle_body(mask, mid, mid_t, marks, rims, out, tables):
    tile, tiles = lax.axis_index("tile"), lax.axis_size("tile")
    own = marks[...].astype(F32)
    low = jnp.where(own[0:1] == 1.0, rims[1].astype(F32), rims[0].astype(F32))
    high = jnp.where(own[1:2] == 1.0, rims[3].astype(F32), rims[2].astype(F32))
    low = jnp.where(tile == 0, 0.0, low).astype(BF16)
    high = jnp.where(tile == tiles - 1, 0.0, high).astype(BF16)
    odd = lax.rem(tile, 2) == 1
    tables[0] = jnp.where(odd, low, high)
    tables[1] = jnp.where(odd, high, low)
    out[...] = dot(mid_t[...], dot(mask[...], mid[...]).astype(BF16))


def split_kernel(pair):
    left = in_left_half(pair.shape)
    other = swap_halves(pair)
    return jnp.where(left, pair, other), jnp.where(left, other, pair)


def fields_body(count, row_count, *refs):
    (middle, target, mid, to_columns, from_columns, tables, own) = refs[:7]
    near_pack, *others, far_edge = refs[7 : 7 + count]
    out, a_ref, field_a, field_b, bent_a, bent_b, u_ref = refs[7 + count :]
    fields, bent = (field_a, field_b), (bent_a, bent_b)
    left = in_left_half((KF, PAIR))
    blocks = middle[...]
    for pack, table in ((near_pack, tables[0]), (far_edge, tables[1])):
        edge = pack[:EDGE, :].astype(F32)
        edge = jnp.concatenate([edge, swap_halves(edge)], 0).astype(BF16)
        blocks = blocks + dot(edge, table)
    top, bottom = blocks[:KF], swap_halves(blocks[KF:])
    spectrum = jnp.where(left, top - bottom, -(top + bottom))
    turned = swap_halves(spectrum)
    turned = jnp.where(left, -turned, turned)
    kernels = [own[...].astype(F32)]
    kernels.append(near_pack[EDGE : 2 * EDGE, :].astype(F32))
    kernels += [one[...].astype(F32) for one in others]
    kernels = [split_kernel(one) for one in kernels]
    begin = pl.multiple_of(lax.axis_index("kern") * row_count, row_count)
    rows = mid[pl.ds(begin, row_count), :]
    stacks = []
    for real, imag in kernels:
        product = real * spectrum + imag * turned
        other = swap_halves(product)
        other = jnp.where(left, -other, other)
        stacks.append(jnp.concatenate([product, other], 0).astype(BF16))
    waves = dot(rows, jnp.concatenate(stacks, 1)).astype(BF16)
    for index in range(count):
        a_ref[index * row_count : (index + 1) * row_count, :] = waves[:, index * PAIR : (index + 1) * PAIR]
    step = 32 if row_count % 32 == 0 else 16
    halves = (slice(0, LANES), slice(LANES, 2 * LANES))
    fields[0][...] = dot(a_ref[...], to_columns[0])
    for block in range(BLOCKS + 1):
        now = block % 2
        if block + 1 < BLOCKS:
            fields[1 - now][...] = dot(a_ref[...], to_columns[block + 1])
        if block > 0:
            part = dot(bent[1 - now][...], from_columns[block - 1])
            u_ref[...] = part if block == 1 else u_ref[...] + part
        if block == BLOCKS:
            continue
        for r in range(0, row_count, step):
            total = None
            for index in range(count):
                at = index * row_count + r
                real, imag = (fields[now][at : at + step, half] for half in halves)
                term = real * real + imag * imag
                total = term if total is None else total + term
            wanted = target[r : r + step, block * LANES : (block + 1) * LANES].astype(F32)
            decay = jnp.exp(4.0 - 2.0 * total)
            resist = pl.reciprocal(1.0 + decay, approx=True)
            slope = (resist - wanted) * (8.0 * decay) * (resist * resist)
            for index in range(count):
                at = index * row_count + r
                for half in halves:
                    field = fields[now][at : at + step, half] * slope
                    bent[now][at : at + step, half] = field.astype(BF16)
    wide = jnp.concatenate(
        [u_ref[i * row_count : (i + 1) * row_count, :].astype(BF16) for i in range(count)], 1
    )
    waves = lax.dot_general(rows, wide, (((0,), (0,)), ((), ())), preferred_element_type=F32)
    total = None
    for index, (real, imag) in enumerate(kernels):
        wave = waves[:, index * PAIR : (index + 1) * PAIR]
        top, bottom = wave[:KF], swap_halves(wave[KF:])
        wave = jnp.where(left, top + bottom, top - bottom)
        other = swap_halves(wave)
        other = jnp.where(left, other, -other)
        term = real * wave + imag * other
        total = term if total is None else total + term
    out[...] = total.astype(BF16)


def sum_body(count, *refs):
    total = refs[0][...].astype(F32)
    for one in refs[1:count]:
        total = total + one[...].astype(F32)
    refs[count][...] = total.astype(BF16)


def row_waves(rows, pair):
    pair = pair.astype(F32)
    other = swap_halves(pair)
    other = jnp.where(in_left_half(pair.shape), -other, other)
    return dot(rows, jnp.concatenate([pair, other], 0).astype(BF16)).astype(BF16)


def own_rows(mid, row_count):
    begin = pl.multiple_of(lax.axis_index("kern") * row_count, row_count)
    return mid[pl.ds(begin, row_count), :]


def inner_body(row_count, own, mid, back, out):
    out[...] = dot(row_waves(own_rows(mid, row_count), own[...]), back[...])


def outer_body(
    row_count, near, far, near_pack, far_edge, mid, margins, begun, out, held, sems
):
    inner = pltpu.make_async_copy(
        begun.at[:, LANES : N - LANES], out.at[:, LANES : N - LANES], sems.at[2]
    )
    inner.start()
    rows = own_rows(mid, row_count)
    near_wave, far_wave = row_waves(rows, near[...]), row_waves(rows, far[...])
    odd = lax.rem(lax.axis_index("tile"), 2) == 1
    below, above = jnp.where(odd, near_wave, far_wave), jnp.where(odd, far_wave, near_wave)
    near_marks = near_pack[2 * EDGE :, :].astype(F32)
    far_marks = far_edge[EDGE:, :].astype(F32)
    low_mark = jnp.where(odd, near_marks, far_marks)[1:2]
    high_mark = jnp.where(odd, far_marks, near_marks)[0:1]
    low = jnp.where(low_mark == 1.0, margins[1].astype(F32), margins[0].astype(F32)).astype(BF16)
    high = jnp.where(high_mark == 1.0, margins[3].astype(F32), margins[2].astype(F32)).astype(BF16)
    copies = []
    for side, first, wave, table in ((0, 0, below, low), (1, N - LANES, above, high)):
        columns = slice(first, first + LANES)
        held[side] = begun[:, columns] + dot(wave, table)
        copies.append(pltpu.make_async_copy(held.at[side], out.at[:, columns], sems.at[side]))
        copies[-1].start()
    for copy in (inner, *copies):
        copy.wait()


def far_off(array):
    return pltpu.with_memory_space_constraint(array, pltpu.HBM)


def per_device(mask_pixels, orientation, target_pattern, kernel_real, kernel_imag, eigen_weights):
    tables = tuple(jnp.asarray(one) for one in transform_tables())
    mid, mid_t, to_columns, from_columns, rims, back, margins = tables
    tiles, count = lax.axis_size("tile"), lax.axis_size("kern")
    row_count = target_pattern.shape[0]
    vmem = pl.BlockSpec(memory_space=pltpu.VMEM)
    smem = pl.BlockSpec(memory_space=pltpu.SMEM)
    hbm = pl.BlockSpec(memory_space=pltpu.HBM)
    small = jax.ShapeDtypeStruct((KF, PAIR), BF16)

    mate, other, side, held, mid, mid_t, marks = call(
        edges_body,
        "edges",
        (
            pltpu.VMEM((2 * EDGE + MARKS, LANES), BF16),
            pltpu.VMEM((EDGE + MARKS, LANES), BF16),
            pltpu.VMEM((KF, PAIR), BF16),
            pltpu.VMEM((N, N), BF16),
            pltpu.VMEM((N, PAIR), BF16),
            pltpu.VMEM((PAIR, N), BF16),
            pltpu.VMEM((MARKS, LANES), BF16),
        ),
        (
            *(far_off(one) for one in (mask_pixels, mid, mid_t, kernel_real, kernel_imag)),
            eigen_weights,
            far_off(orientation),
        ),
        [hbm] * 5 + [smem, hbm],
        scratch=[
            pltpu.VMEM((2, KF, KF), F32),
            pltpu.SMEM((1, 2), jnp.int32),
            pltpu.SemaphoreType.DMA((8,)),
        ],
        flops=2 * N * LANES * PAIR * 2,
        moved=N * LANES * 4,
    )

    def swapped(move_tile, step):
        pairs = []
        for t in range(tiles):
            for k in range(count):
                pairs.append((t * count + k, move_tile(t) * count + destination(k, step, count)))
        return pairs

    def chip_mate(t):
        return t ^ 1

    def other_side(t):
        return (t + 1 if t % 2 else t - 1) % tiles

    both = ("tile", "kern")
    far_edge = lax.ppermute(other, both, swapped(other_side, 0))
    near_pack = lax.ppermute(mate, both, swapped(chip_mate, 1))
    if count == 4:
        pairs = []
        for t in range(tiles):
            pairs += [(t * count + k, t * count + destination(k, 2 + t % 2, count)) for k in range(count)]
        kernels = [lax.ppermute(side, both, pairs)]
        kernels.append(lax.ppermute(kernels[0], both, swapped(chip_mate, 0)))
    else:
        kernels = [lax.ppermute(side, both, swapped(lambda t: t, step)) for step in range(2, count)]

    middle, edge_tables = call(
        middle_body,
        "middle",
        (pltpu.VMEM((PAIR, PAIR), F32), pltpu.VMEM((2, PAIR, PAIR), BF16)),
        (held, mid, mid_t, marks, rims),
        [vmem] * 5,
        flops=4 * N * N * PAIR,
        moved=N * N * 2,
    )

    part = call(
        functools.partial(fields_body, count, row_count),
        "fields",
        small,
        (middle, target_pattern, mid, to_columns, from_columns, edge_tables, side, near_pack, *kernels, far_edge),
        [vmem] * (7 + count),
        scratch=[
            pltpu.VMEM((count * row_count, PAIR), BF16),
            pltpu.VMEM((count * row_count, 2 * LANES), F32),
            pltpu.VMEM((count * row_count, 2 * LANES), F32),
            pltpu.VMEM((count * row_count, 2 * LANES), BF16),
            pltpu.VMEM((count * row_count, 2 * LANES), BF16),
            pltpu.VMEM((count * row_count, PAIR), F32),
        ],
        flops=8 * count * row_count * N * PAIR,
        moved=4 * row_count * N,
    )

    parts = [part]
    for step in range(1, count):
        pairs = [(k, destination(k, step, count)) for k in range(count)]
        parts.append(lax.ppermute(part, "kern", pairs))
    own = call(functools.partial(sum_body, count), "total", small, tuple(parts), [vmem] * count)
    near = lax.ppermute(own, "tile", [(t, chip_mate(t)) for t in range(tiles)])
    inner = [t for t in range(tiles) if 0 < t < tiles - 1]
    far = lax.ppermute(own, "tile", [(t, other_side(t)) for t in inner])
    begun = call(
        functools.partial(inner_body, row_count),
        "inner",
        pltpu.VMEM((row_count, N), F32),
        (own, mid, back),
        [vmem] * 3,
        flops=2 * row_count * PAIR * N,
        moved=4 * row_count * N,
    )
    return call(
        functools.partial(outer_body, row_count),
        "outer",
        jax.ShapeDtypeStruct((row_count, N), F32),
        (near, far, near_pack, far_edge, mid, margins, begun),
        [vmem] * 7,
        hbm,
        scratch=[
            pltpu.VMEM((2, row_count, LANES), F32),
            pltpu.SemaphoreType.DMA((3,)),
        ],
        flops=2 * row_count * PAIR * 6 * PAIR,
        moved=4 * row_count * 2 * LANES,
    )


def solution(mesh):
    in_specs = (
        P(None, "tile"),
        P("tile", None),
        P("kern", "tile"),
        P("kern", None, None),
        P("kern", None, None),
        P("kern"),
    )
    out_specs = P("kern", "tile")
    return jax.shard_map(
        per_device, mesh=mesh, in_specs=in_specs, out_specs=out_specs, check_vma=False
    )
```

profile of v0, /device:TPU:4, one launch (start us, length us, event | category | flops | bytes accessed | tf_op | source)
XLA Modules:
  0.0 29.0 jit_solution(3972581442169789542)
XLA Ops:
  0.7 0.0 copy-start.2
  0.7 2.0 %edges.1 = (bf16[144,128]{1,0:T(8,128)(2,1)S(1)}, bf16[80,128]{1,0:T(8,128)(2,1)S(1)}, bf16[64,128]{1,0:T(8,128)(2,1)S(1)}, bf16[1152,1152]{1,0:T(8,128)(2,1)S(1...) custom-call(bf16[1152,1152]{1,0:T(8,128)(2,1)} %mask.1, ...), custom_call_target="tpu_custom_call" | custom-call | flops 75497472 | bytes 589824 | tf_op jit(solution)/shard_map/edges/pallas_call | solution.py:95
  2.7 2.7 %collective-permute-start.1 = (bf16[64,128]{1,0:T(8,128)(2,1)S(1)}, bf16[64,128]{1,0:T(8,128)(2,1)S(1)}, u32[]{:S(2)}, u32[]{:S(2)}) collective-permute-start(bf16[64,128]{1,0:T(8,128)(2,1)S(1)} %get-tuple-element.20.refs_6_), channel_id=1, source_target_pairs={{0,2},{1,3},{2,0},{3,1},{4,7},{5,6},{6,5},{7,4},{8,10},{9,11},{10,... | collective-permute-start | bytes 49160 | tf_op jit(solution)/shard_map/ppermute | solution.py:356
  5.4 1.6 %collective-permute-start.3 = (bf16[80,128]{1,0:T(8,128)(2,1)S(1)}, bf16[80,128]{1,0:T(8,128)(2,1)S(1)}, u32[]{:S(2)}, u32[]{:S(2)}) collective-permute-start(bf16[80,128]{1,0:T(8,128)(2,1)S(1)} %get-tuple-element.22), channel_id=1, source_target_pairs={{0,28},{1,29},{2,30},{3,31},{4,8},{5,9},{6,10},{7,11},{8,4},{9,5},... | collective-permute-start | bytes 61448 | tf_op jit(solution)/shard_map/ppermute | solution.py:350
  7.0 1.2 %collective-permute-start = (bf16[144,128]{1,0:T(8,128)(2,1)S(1)}, bf16[144,128]{1,0:T(8,128)(2,1)S(1)}, u32[]{:S(2)}, u32[]{:S(2)}) collective-permute-start(bf16[144,128]{1,0:T(8,128)(2,1)S(1)} %get-tuple-element.21), channel_id=1, source_target_pairs={{0,5},{1,4},{2,7},{3,6},{4,1},{5,0},{6,3},{7,2},{8,13},{9,12},{10,... | collective-permute-start | bytes 110600 | tf_op jit(solution)/shard_map/ppermute | solution.py:351
  8.1 0.0 collective-permute-done.1.refs_8_
  8.1 0.0 collective-permute-start.2
  8.1 0.0 copy-done.2
  8.2 0.0 copy-start.3
  8.2 0.0 copy-start.4
  8.2 0.0 copy-start.5
  8.2 1.1 %middle.1 = (f32[128,128]{1,0:T(8,128)S(1)}, bf16[2,128,128]{2,1,0:T(8,128)(2,1)S(1)}) custom-call(bf16[1152,1152]{1,0:T(8,128)(2,1)S(1)} %get-tuple-element.14.mask, bf16[1152,128]{1,0:T(8,128)(2,1)S(1)} %get-tuple-element.15.mid.refs_2_, bf16[128,1152]{1,0:T(8,128)(2,1)S(1)} %get-tuple-element.16.mid_t, bf16[16,128]{1,0:T(8,128)(2,1)S(1)} %get-tuple-element.17.marks, ...), custom_call_target="tpu_custom_call" | custom-call | flops 679477248 | bytes 2654208 | tf_op jit(solution)/shard_map/middle/pallas_call | solution.py:95
  9.3 0.2 collective-permute-done.3.refs_10_.far_edge
  9.5 0.0 collective-permute-done.2.refs_9_
  9.5 1.1 %collective-permute-done.refs_7_.near_pack = bf16[144,128]{1,0:T(8,128)(2,1)S(1)} collective-permute-done((bf16[144,128]{1,0:T(8,128)(2,1)S(1)}, bf16[144,128]{1,0:T(8,128)(2,1)S(1)}, u32[]{:S(2)}, u32[]{:S(2)}) %collective-permute-start) | collective-permute-done | bytes 36896 | tf_op jit(solution)/shard_map/ppermute | solution.py:351
  10.6 0.0 copy-done.5
  10.6 0.0 copy-start
  10.6 4.4 %fields.1.refs_0_ = bf16[64,128]{1,0:T(8,128)(2,1)S(1)} custom-call(f32[128,128]{1,0:T(8,128)S(1)} %get-tuple-element.18.refs_0_, s32[288,1152]{1,0:T(8,128)S(1)} %copy-done.3, bf16[1152,128]{1,0:T(8,128)(2,1)S(1)} %get-tuple-element.15.mid.refs_2_, bf16[9,128,256]{2,1,0:T(8,128)(2,1)S(1)} %copy-done.5, bf16[9,256,128]{2,1,0:T(8,128)(2,1)S(1)} %copy-done.4, ...), custom_call_target="tpu_custom_call" | custom-call | flops 1358954496 | bytes 1327104 | tf_op jit(solution)/shard_map/fields/pallas_call | solution.py:95
  15.0 0.0 copy-start.1
  15.0 2.3 %collective-permute-start.6 = (bf16[64,128]{1,0:T(8,128)(2,1)S(1)}, bf16[64,128]{1,0:T(8,128)(2,1)S(1)}, u32[]{:S(2)}, u32[]{:S(2)}) collective-permute-start(bf16[64,128]{1,0:T(8,128)(2,1)S(1)} %fields.1.refs_0_), channel_id=1, source_target_pairs={{0,3},{1,2},{2,1},{3,0},{4,7},{5,6},{6,5},{7,4},{8,11},{9,10},{10,... | collective-permute-start | bytes 49160 | tf_op jit(solution)/shard_map/ppermute | solution.py:392
  17.3 0.0 collective-permute-start.5
  17.3 2.2 %collective-permute-start.4 = (bf16[64,128]{1,0:T(8,128)(2,1)S(1)}, bf16[64,128]{1,0:T(8,128)(2,1)S(1)}, u32[]{:S(2)}, u32[]{:S(2)}) collective-permute-start(bf16[64,128]{1,0:T(8,128)(2,1)S(1)} %fields.1.refs_0_), channel_id=1, source_target_pairs={{0,1},{1,0},{2,3},{3,2},{4,5},{5,4},{6,7},{7,6},{8,9},{9,8},{10,11... | collective-permute-start | bytes 49160 | tf_op jit(solution)/shard_map/ppermute | solution.py:392
  19.5 1.1 %collective-permute-done.6.refs_3_ = bf16[64,128]{1,0:T(8,128)(2,1)S(1)} collective-permute-done((bf16[64,128]{1,0:T(8,128)(2,1)S(1)}, bf16[64,128]{1,0:T(8,128)(2,1)S(1)}, u32[]{:S(2)}, u32[]{:S(2)}) %collective-permute-start.6) | collective-permute-done | bytes 16416 | tf_op jit(solution)/shard_map/ppermute | solution.py:392
  20.6 1.3 %collective-permute-done.5.refs_2_ = bf16[64,128]{1,0:T(8,128)(2,1)S(1)} collective-permute-done((bf16[64,128]{1,0:T(8,128)(2,1)S(1)}, bf16[64,128]{1,0:T(8,128)(2,1)S(1)}, u32[]{:S(2)}, u32[]{:S(2)}) %collective-permute-start.5) | collective-permute-done | bytes 16416 | tf_op jit(solution)/shard_map/ppermute | solution.py:392
  21.9 0.0 collective-permute-done.4.refs_1_
  21.9 2.0 %collective-permute-start.8 = (bf16[64,128]{1,0:T(8,128)(2,1)S(1)}, bf16[64,128]{1,0:T(8,128)(2,1)S(1)}, u32[]{:S(2)}, u32[]{:S(2)}) collective-permute-start(bf16[64,128]{1,0:T(8,128)(2,1)S(1)} %total.1.own), channel_id=1, source_target_pairs={{4,8},{8,4},{12,16},{16,12},{20,24},{24,20},{5,9},{9,5},{13,17},{1... | collective-permute-start | bytes 49160 | tf_op jit(solution)/shard_map/ppermute | solution.py:396
  24.0 1.6 %collective-permute-start.7 = (bf16[64,128]{1,0:T(8,128)(2,1)S(1)}, bf16[64,128]{1,0:T(8,128)(2,1)S(1)}, u32[]{:S(2)}, u32[]{:S(2)}) collective-permute-start(bf16[64,128]{1,0:T(8,128)(2,1)S(1)} %total.1.own), channel_id=1, source_target_pairs={{0,4},{4,0},{8,12},{12,8},{16,20},{20,16},{24,28},{28,24},{1,5},{5... | collective-permute-start | bytes 49160 | tf_op jit(solution)/shard_map/ppermute | solution.py:394
  25.5 0.5 %inner.1.begun = f32[288,1152]{1,0:T(8,128)S(1)} custom-call(bf16[64,128]{1,0:T(8,128)(2,1)S(1)} %total.1.own, bf16[1152,128]{1,0:T(8,128)(2,1)S(1)} %get-tuple-element.15.mid.refs_2_, bf16[128,1152]{1,0:T(8,128)(2,1)S(1)} %copy-done), custom_call_target="tpu_custom_call" | custom-call | flops 84934656 | bytes 1327104 | tf_op jit(solution)/shard_map/inner/pallas_call | solution.py:95
  26.1 1.8 %collective-permute-done.8.far = bf16[64,128]{1,0:T(8,128)(2,1)S(1)} collective-permute-done((bf16[64,128]{1,0:T(8,128)(2,1)S(1)}, bf16[64,128]{1,0:T(8,128)(2,1)S(1)}, u32[]{:S(2)}, u32[]{:S(2)}) %collective-permute-start.8) | collective-permute-done | bytes 16416 | tf_op jit(solution)/shard_map/ppermute | solution.py:396
  27.9 0.0 collective-permute-done.7.near
  27.9 0.0 copy-done.1
  27.9 1.1 %outer.1 = f32[288,1152]{1,0:T(8,128)} custom-call(bf16[64,128]{1,0:T(8,128)(2,1)S(1)} %collective-permute-done.7.near, bf16[64,128]{1,0:T(8,128)(2,1)S(1)} %collective-permute-done.8.far, bf16[144,128]{1,0:T(8,128)(2,1)S(1)} %collective-permute-done.refs_7_.near_pack, bf16[80,128]{1,0:T(8,128)(2,1)S(1)} %collective-permute-done.3.refs_10_.far_edge, ...), custom_call_target="tpu_custom_call" | custom-call | flops 56623104 | bytes 294912 | tf_op jit(solution)/shard_map/outer/pallas_call | solution.py:95
  (4 shorter events, 0.0 us)
Async XLA Ops:
  0.7 7.5 %copy-start.2 = (bf16[4,128,128]{2,1,0:T(8,128)(2,1)S(1)}, bf16[4,128,128]{2,1,0:T(8,128)(2,1)}, u32[]{:S(2)}) copy-start(bf16[4,128,128]{2,1,0:T(8,128)(2,1)} %constant.18.clone.rims) | copy-start | bytes 393220
  2.7 5.4 %collective-permute-start.1 = (bf16[64,128]{1,0:T(8,128)(2,1)S(1)}, bf16[64,128]{1,0:T(8,128)(2,1)S(1)}, u32[]{:S(2)}, u32[]{:S(2)}) collective-permute-start(bf16[64,128]{1,0:T(8,128)(2,1)S(1)} %get-tuple-element.20.refs_6_), channel_id=1, source_target_pairs={{0,2},{1,3},{2,0},{3,1},{4,7},{5,6},{6,5},{7,4},{8,10},{9,11},{10,... | collective-permute-start | bytes 49160 | tf_op jit(solution)/shard_map/ppermute | solution.py:356
  5.4 4.1 %collective-permute-start.3 = (bf16[80,128]{1,0:T(8,128)(2,1)S(1)}, bf16[80,128]{1,0:T(8,128)(2,1)S(1)}, u32[]{:S(2)}, u32[]{:S(2)}) collective-permute-start(bf16[80,128]{1,0:T(8,128)(2,1)S(1)} %get-tuple-element.22), channel_id=1, source_target_pairs={{0,28},{1,29},{2,30},{3,31},{4,8},{5,9},{6,10},{7,11},{8,4},{9,5},... | collective-permute-start | bytes 61448 | tf_op jit(solution)/shard_map/ppermute | solution.py:350
  7.0 3.6 %collective-permute-start = (bf16[144,128]{1,0:T(8,128)(2,1)S(1)}, bf16[144,128]{1,0:T(8,128)(2,1)S(1)}, u32[]{:S(2)}, u32[]{:S(2)}) collective-permute-start(bf16[144,128]{1,0:T(8,128)(2,1)S(1)} %get-tuple-element.21), channel_id=1, source_target_pairs={{0,5},{1,4},{2,7},{3,6},{4,1},{5,0},{6,3},{7,2},{8,13},{9,12},{10,... | collective-permute-start | bytes 110600 | tf_op jit(solution)/shard_map/ppermute | solution.py:351
  8.1 1.3 %collective-permute-start.2 = (bf16[64,128]{1,0:T(8,128)(2,1)S(1)}, bf16[64,128]{1,0:T(8,128)(2,1)S(1)}, u32[]{:S(2)}, u32[]{:S(2)}) collective-permute-start(bf16[64,128]{1,0:T(8,128)(2,1)S(1)} %collective-permute-done.1.refs_8_), channel_id=1, source_target_pairs={{0,4},{1,5},{2,6},{3,7},{4,0},{5,1},{6,2},{7,3},{8,12},{9,13},{10,... | collective-permute-start | bytes 49160 | tf_op jit(solution)/shard_map/ppermute | solution.py:357
  8.2 2.4 %copy-start.3 = (s32[288,1152]{1,0:T(8,128)S(1)}, s32[288,1152]{1,0:T(8,128)}, u32[]{:S(2)}) copy-start(s32[288,1152]{1,0:T(8,128)} %refs_1_.1) | copy-start | bytes 3981316
  8.2 2.4 %copy-start.4 = (bf16[9,256,128]{2,1,0:T(8,128)(2,1)S(1)}, bf16[9,256,128]{2,1,0:T(8,128)(2,1)}, u32[]{:S(2)}) copy-start(bf16[9,256,128]{2,1,0:T(8,128)(2,1)} %constant.17.clone.refs_4_) | copy-start | bytes 1769476
  8.2 2.4 %copy-start.5 = (bf16[9,128,256]{2,1,0:T(8,128)(2,1)S(1)}, bf16[9,128,256]{2,1,0:T(8,128)(2,1)}, u32[]{:S(2)}) copy-start(bf16[9,128,256]{2,1,0:T(8,128)(2,1)} %constant.16.clone.refs_3_) | copy-start | bytes 1769476
  10.6 15.0 %copy-start = (bf16[128,1152]{1,0:T(8,128)(2,1)S(1)}, bf16[128,1152]{1,0:T(8,128)(2,1)}, u32[]{:S(2)}) copy-start(bf16[128,1152]{1,0:T(8,128)(2,1)} %constant.19.clone.back) | copy-start | bytes 884740
  15.0 12.9 %copy-start.1 = (bf16[4,128,128]{2,1,0:T(8,128)(2,1)S(1)}, bf16[4,128,128]{2,1,0:T(8,128)(2,1)}, u32[]{:S(2)}) copy-start(bf16[4,128,128]{2,1,0:T(8,128)(2,1)} %constant.20.clone.margins) | copy-start | bytes 393220
  15.0 5.6 %collective-permute-start.6 = (bf16[64,128]{1,0:T(8,128)(2,1)S(1)}, bf16[64,128]{1,0:T(8,128)(2,1)S(1)}, u32[]{:S(2)}, u32[]{:S(2)}) collective-permute-start(bf16[64,128]{1,0:T(8,128)(2,1)S(1)} %fields.1.refs_0_), channel_id=1, source_target_pairs={{0,3},{1,2},{2,1},{3,0},{4,7},{5,6},{6,5},{7,4},{8,11},{9,10},{10,... | collective-permute-start | bytes 49160 | tf_op jit(solution)/shard_map/ppermute | solution.py:392
  17.3 4.6 %collective-permute-start.5 = (bf16[64,128]{1,0:T(8,128)(2,1)S(1)}, bf16[64,128]{1,0:T(8,128)(2,1)S(1)}, u32[]{:S(2)}, u32[]{:S(2)}) collective-permute-start(bf16[64,128]{1,0:T(8,128)(2,1)S(1)} %fields.1.refs_0_), channel_id=1, source_target_pairs={{0,2},{1,3},{2,0},{3,1},{4,6},{5,7},{6,4},{7,5},{8,10},{9,11},{10,... | collective-permute-start | bytes 49160 | tf_op jit(solution)/shard_map/ppermute | solution.py:392
  17.3 4.6 %collective-permute-start.4 = (bf16[64,128]{1,0:T(8,128)(2,1)S(1)}, bf16[64,128]{1,0:T(8,128)(2,1)S(1)}, u32[]{:S(2)}, u32[]{:S(2)}) collective-permute-start(bf16[64,128]{1,0:T(8,128)(2,1)S(1)} %fields.1.refs_0_), channel_id=1, source_target_pairs={{0,1},{1,0},{2,3},{3,2},{4,5},{5,4},{6,7},{7,6},{8,9},{9,8},{10,11... | collective-permute-start | bytes 49160 | tf_op jit(solution)/shard_map/ppermute | solution.py:392
  21.9 6.0 %collective-permute-start.8 = (bf16[64,128]{1,0:T(8,128)(2,1)S(1)}, bf16[64,128]{1,0:T(8,128)(2,1)S(1)}, u32[]{:S(2)}, u32[]{:S(2)}) collective-permute-start(bf16[64,128]{1,0:T(8,128)(2,1)S(1)} %total.1.own), channel_id=1, source_target_pairs={{4,8},{8,4},{12,16},{16,12},{20,24},{24,20},{5,9},{9,5},{13,17},{1... | collective-permute-start | bytes 49160 | tf_op jit(solution)/shard_map/ppermute | solution.py:396
  24.0 3.9 %collective-permute-start.7 = (bf16[64,128]{1,0:T(8,128)(2,1)S(1)}, bf16[64,128]{1,0:T(8,128)(2,1)S(1)}, u32[]{:S(2)}, u32[]{:S(2)}) collective-permute-start(bf16[64,128]{1,0:T(8,128)(2,1)S(1)} %total.1.own), channel_id=1, source_target_pairs={{0,4},{4,0},{8,12},{12,8},{16,20},{20,16},{24,28},{28,24},{1,5},{5... | collective-permute-start | bytes 49160 | tf_op jit(solution)/shard_map/ppermute | solution.py:394
where the time goes:
time: 29.2 us; the launch traced here: 29 us
  starting transfers between devices  13.5 us (46%)
  Pallas kernels  9.19 us (31%)
  waiting for transfers between devices  5.54 us (19%)
  between operations  0.75 us (3%)
    pallas_call x6, Pallas kernels, call(): pl.pallas_call(body, name=name, out_shape=outs, in_specs=specs, out_specs...  9.19 us
    ppermute x3, starting transfers between devices, per_device(): parts.append(lax.ppermute(part, 'kern', pairs))  4.45 us
    ppermute x1, starting transfers between devices, per_device(): kernels = [lax.ppermute(side, both, pairs)]  2.65 us
    ppermute x3, waiting for transfers between devices, per_device(): parts.append(lax.ppermute(part, 'kern', pairs))  2.44 us
    ppermute x1, starting transfers between devices, per_device(): far = lax.ppermute(own, 'tile', [(t, other_side(t)) for t in inner])  2.05 us
    ppermute x1, waiting for transfers between devices, per_device(): far = lax.ppermute(own, 'tile', [(t, other_side(t)) for t in inner])  1.83 us
    ppermute x1, starting transfers between devices, per_device(): far_edge = lax.ppermute(other, both, swapped(other_side, 0))  1.61 us
    ppermute x1, starting transfers between devices, per_device(): near = lax.ppermute(own, 'tile', [(t, chip_mate(t)) for t in range(tiles)])  1.55 us
  transfers between devices with their start and end apart: 9, of which 5 were waited for; matrix products, arithmetic and copies ran while one was open for 0% of the time, Pallas kernels for 6%

commit v1 on v0

--- a/solution.py
+++ b/solution.py
@@ -149,7 +149,8 @@
     columns.wait()
 
 
-def middle_body(mask, mid, mid_t, marks, rims, out, tables):
+def middle_body(row_count, mask, mid, mid_t, marks, rims, out, tables, rows_t):
+    rows_t[...] = own_rows(mid, row_count).astype(F32).T.astype(BF16)
     tile, tiles = lax.axis_index("tile"), lax.axis_size("tile")
     own = marks[...].astype(F32)
     low = jnp.where(own[0:1] == 1.0, rims[1].astype(F32), rims[0].astype(F32))
@@ -162,6 +163,10 @@
     out[...] = dot(mid_t[...], dot(mask[...], mid[...]).astype(BF16))
 
 
+def relay_body(value, ready, out):
+    out[...] = value[...]
+
+
 def split_kernel(pair):
     left = in_left_half(pair.shape)
     other = swap_halves(pair)
@@ -169,9 +174,9 @@
 
 
 def fields_body(count, row_count, *refs):
-    (middle, target, mid, to_columns, from_columns, tables, own) = refs[:7]
-    near_pack, *others, far_edge = refs[7 : 7 + count]
-    out, a_ref, field_a, field_b, bent_a, bent_b, u_ref = refs[7 + count :]
+    (middle, target, mid, rows_t, to_columns, from_columns, tables, own) = refs[:8]
+    near_pack, *others, far_edge = refs[8 : 8 + count]
+    out, a_ref, field_a, field_b, bent_a, bent_b, u_ref = refs[8 + count :]
     fields, bent = (field_a, field_b), (bent_a, bent_b)
     left = in_left_half((KF, PAIR))
     blocks = middle[...]
@@ -229,7 +234,7 @@
     wide = jnp.concatenate(
         [u_ref[i * row_count : (i + 1) * row_count, :].astype(BF16) for i in range(count)], 1
     )
-    waves = lax.dot_general(rows, wide, (((0,), (0,)), ((), ())), preferred_element_type=F32)
+    waves = dot(rows_t[...], wide)
     total = None
     for index, (real, imag) in enumerate(kernels):
         wave = waves[:, index * PAIR : (index + 1) * PAIR]
@@ -354,26 +359,33 @@
         for t in range(tiles):
             pairs += [(t * count + k, t * count + destination(k, 2 + t % 2, count)) for k in range(count)]
         kernels = [lax.ppermute(side, both, pairs)]
-        kernels.append(lax.ppermute(kernels[0], both, swapped(chip_mate, 0)))
     else:
         kernels = [lax.ppermute(side, both, swapped(lambda t: t, step)) for step in range(2, count)]
 
-    middle, edge_tables = call(
-        middle_body,
+    middle, edge_tables, rows_t = call(
+        functools.partial(middle_body, row_count),
         "middle",
-        (pltpu.VMEM((PAIR, PAIR), F32), pltpu.VMEM((2, PAIR, PAIR), BF16)),
+        (
+            pltpu.VMEM((PAIR, PAIR), F32),
+            pltpu.VMEM((2, PAIR, PAIR), BF16),
+            pltpu.VMEM((PAIR, row_count), BF16),
+        ),
         (held, mid, mid_t, marks, rims),
         [vmem] * 5,
         flops=4 * N * N * PAIR,
         moved=N * N * 2,
     )
 
+    if count == 4:
+        relayed = call(relay_body, "relay", small, (kernels[0], middle), [vmem] * 2)
+        kernels.append(lax.ppermute(relayed, both, swapped(chip_mate, 0)))
+
     part = call(
         functools.partial(fields_body, count, row_count),
         "fields",
         small,
-        (middle, target_pattern, mid, to_columns, from_columns, edge_tables, side, near_pack, *kernels, far_edge),
-        [vmem] * (7 + count),
+        (middle, target_pattern, mid, rows_t, to_columns, from_columns, edge_tables, side, near_pack, *kernels, far_edge),
+        [vmem] * (8 + count),
         scratch=[
             pltpu.VMEM((count * row_count, PAIR), BF16),
             pltpu.VMEM((count * row_count, 2 * LANES), F32),
@@ -388,8 +400,11 @@
 
     parts = [part]
     for step in range(1, count):
-        pairs = [(k, destination(k, step, count)) for k in range(count)]
-        parts.append(lax.ppermute(part, "kern", pairs))
+        pairs = []
+        for t in range(tiles):
+            own_step = step if t % 2 else count - step
+            pairs += [(t * count + k, t * count + destination(k, own_step, count)) for k in range(count)]
+        parts.append(lax.ppermute(part, both, pairs))
     own = call(functools.partial(sum_body, count), "total", small, tuple(parts), [vmem] * count)
     near = lax.ppermute(own, "tile", [(t, chip_mate(t)) for t in range(tiles)])
     inner = [t for t in range(tiles) if 0 < t < tiles - 1]

time: 29.2 us -> 30.2 us (1.034)
  waiting for transfers between devices: 5.54 us -> 6.51 us
    ppermute x4, waiting for transfers between devices: 2.44 us -> 4.52 us  [the longest x3 3.47 us: per_device(): parts.append(lax.ppermute(part, both, pairs))]
    ppermute x1, waiting for transfers between devices: 1.08 us -> 0.04 us  [per_device(): near_pack = lax.ppermute(mate, both, swapped(chip_mate, 1))]
    pallas_call x6 -> x7, Pallas kernels: 9.19 us -> 9.18 us  [call(): pl.pallas_call(body, name=name, out_shape=outs, in_specs=specs, out_specs...]
  transfers between devices with their start and end apart: 9 -> 9, of which waited for: 5 -> 5; matrix products, arithmetic and copies ran while one was open for 0% -> 0% of each run, Pallas kernels for 6% -> 5%
where the time goes in v1:
time: 30.2 us; the launch traced here: 30 us
  starting transfers between devices  13.6 us (45%)
  Pallas kernels  9.18 us (30%)
  waiting for transfers between devices  6.51 us (22%)
  between operations  0.75 us (2%)
    pallas_call x7, Pallas kernels, call(): pl.pallas_call(body, name=name, out_shape=outs, in_specs=specs, out_specs...  9.18 us
    ppermute x3, starting transfers between devices, per_device(): parts.append(lax.ppermute(part, both, pairs))  4.45 us
    ppermute x3, waiting for transfers between devices, per_device(): parts.append(lax.ppermute(part, both, pairs))  3.47 us
    ppermute x1, starting transfers between devices, per_device(): kernels = [lax.ppermute(side, both, pairs)]  2.65 us
    ppermute x1, starting transfers between devices, per_device(): far = lax.ppermute(own, 'tile', [(t, other_side(t)) for t in inner])  1.92 us
    ppermute x1, waiting for transfers between devices, per_device(): far = lax.ppermute(own, 'tile', [(t, other_side(t)) for t in inner])  1.82 us
    ppermute x1, starting transfers between devices, per_device(): near = lax.ppermute(own, 'tile', [(t, chip_mate(t)) for t in range(tiles)])  1.68 us
    ppermute x1, starting transfers between devices, per_device(): far_edge = lax.ppermute(other, both, swapped(other_side, 0))  1.61 us
  transfers between devices with their start and end apart: 9, of which 5 were waited for; matrix products, arithmetic and copies ran while one was open for 0% of the time, Pallas kernels for 5%

profile of v1, /device:TPU:4, one launch (start us, length us, event | category | flops | bytes accessed | tf_op | source)
XLA Modules:
  0.0 30.0 jit_solution(12622490246308859842)
XLA Ops:
  0.7 0.0 copy-start.2
  0.7 2.0 %edges.1 = (bf16[144,128]{1,0:T(8,128)(2,1)S(1)}, bf16[80,128]{1,0:T(8,128)(2,1)S(1)}, bf16[64,128]{1,0:T(8,128)(2,1)S(1)}, bf16[1152,1152]{1,0:T(8,128)(2,1)S(1...) custom-call(bf16[1152,1152]{1,0:T(8,128)(2,1)} %mask.1, ...), custom_call_target="tpu_custom_call" | custom-call | flops 75497472 | bytes 589824 | tf_op jit(solution)/shard_map/edges/pallas_call | solution.py:95
  2.7 2.7 %collective-permute-start.1 = (bf16[64,128]{1,0:T(8,128)(2,1)S(1)}, bf16[64,128]{1,0:T(8,128)(2,1)S(1)}, u32[]{:S(2)}, u32[]{:S(2)}) collective-permute-start(bf16[64,128]{1,0:T(8,128)(2,1)S(1)} %get-tuple-element.22.refs_7_), channel_id=1, source_target_pairs={{0,2},{1,3},{2,0},{3,1},{4,7},{5,6},{6,5},{7,4},{8,10},{9,11},{10,... | collective-permute-start | bytes 49160 | tf_op jit(solution)/shard_map/ppermute | solution.py:361
  5.4 1.6 %collective-permute-start.3 = (bf16[80,128]{1,0:T(8,128)(2,1)S(1)}, bf16[80,128]{1,0:T(8,128)(2,1)S(1)}, u32[]{:S(2)}, u32[]{:S(2)}) collective-permute-start(bf16[80,128]{1,0:T(8,128)(2,1)S(1)} %get-tuple-element.24), channel_id=1, source_target_pairs={{0,28},{1,29},{2,30},{3,31},{4,8},{5,9},{6,10},{7,11},{8,4},{9,5},... | collective-permute-start | bytes 61448 | tf_op jit(solution)/shard_map/ppermute | solution.py:355
  7.0 1.2 %collective-permute-start = (bf16[144,128]{1,0:T(8,128)(2,1)S(1)}, bf16[144,128]{1,0:T(8,128)(2,1)S(1)}, u32[]{:S(2)}, u32[]{:S(2)}) collective-permute-start(bf16[144,128]{1,0:T(8,128)(2,1)S(1)} %get-tuple-element.23), channel_id=1, source_target_pairs={{0,5},{1,4},{2,7},{3,6},{4,1},{5,0},{6,3},{7,2},{8,13},{9,12},{10,... | collective-permute-start | bytes 110600 | tf_op jit(solution)/shard_map/ppermute | solution.py:356
  8.1 0.0 copy-done.2
  8.2 1.1 %middle.1 = (f32[128,128]{1,0:T(8,128)S(1)}, bf16[2,128,128]{2,1,0:T(8,128)(2,1)S(1)}, bf16[128,288]{1,0:T(8,128)(2,1)S(1)}) custom-call(bf16[1152,1152]{1,0:T(8,128)(2,1)S(1)} %get-tuple-element.15.mask, bf16[1152,128]{1,0:T(8,128)(2,1)S(1)} %get-tuple-element.16.mid.refs_2_, bf16[128,1152]{1,0:T(8,128)(2,1)S(1)} %get-tuple-element.17.mid_t, ...), custom_call_target="tpu_custom_call" | custom-call | flops 679477248 | bytes 2654208 | tf_op jit(solution)/shard_map/middle/pallas_call | solution.py:95
  9.2 0.0 collective-permute-done.1.value.refs_9_
  9.3 0.1 collective-permute-start.2
  9.3 0.1 collective-permute-done.3.refs_11_.far_edge
  9.5 1.0 %collective-permute-done.2.refs_10_ = bf16[64,128]{1,0:T(8,128)(2,1)S(1)} collective-permute-done((bf16[64,128]{1,0:T(8,128)(2,1)S(1)}, bf16[64,128]{1,0:T(8,128)(2,1)S(1)}, u32[]{:S(2)}, u32[]{:S(2)}) %collective-permute-start.2) | collective-permute-done | bytes 16416 | tf_op jit(solution)/shard_map/ppermute | solution.py:381
  10.5 0.0 collective-permute-done.refs_8_.near_pack
  10.6 0.0 copy-done.3
  10.6 0.0 copy-done.4
  10.6 0.0 copy-done.5
  10.6 0.0 copy-start
  10.6 4.4 %fields.1.refs_0_ = bf16[64,128]{1,0:T(8,128)(2,1)S(1)} custom-call(f32[128,128]{1,0:T(8,128)S(1)} %get-tuple-element.19.ready.refs_0_, s32[288,1152]{1,0:T(8,128)S(1)} %copy-done.3, bf16[1152,128]{1,0:T(8,128)(2,1)S(1)} %get-tuple-element.16.mid.refs_2_, bf16[128,288]{1,0:T(8,128)(2,1)S(1)} %get-tuple-element.20.refs_3_, ...), custom_call_target="tpu_custom_call" | custom-call | flops 1358954496 | bytes 1327104 | tf_op jit(solution)/shard_map/fields/pallas_call | solution.py:95
  15.0 0.0 copy-start.1
  15.0 0.6 %collective-permute-start.6 = (bf16[64,128]{1,0:T(8,128)(2,1)S(1)}, bf16[64,128]{1,0:T(8,128)(2,1)S(1)}, u32[]{:S(2)}, u32[]{:S(2)}) collective-permute-start(bf16[64,128]{1,0:T(8,128)(2,1)S(1)} %fields.1.refs_0_), channel_id=1, source_target_pairs={{0,1},{1,0},{2,3},{3,2},{4,7},{5,6},{6,5},{7,4},{8,9},{9,8},{10,11... | collective-permute-start | bytes 49160 | tf_op jit(solution)/shard_map/ppermute | solution.py:407
  15.7 1.7 %collective-permute-start.5 = (bf16[64,128]{1,0:T(8,128)(2,1)S(1)}, bf16[64,128]{1,0:T(8,128)(2,1)S(1)}, u32[]{:S(2)}, u32[]{:S(2)}) collective-permute-start(bf16[64,128]{1,0:T(8,128)(2,1)S(1)} %fields.1.refs_0_), channel_id=1, source_target_pairs={{0,2},{1,3},{2,0},{3,1},{4,6},{5,7},{6,4},{7,5},{8,10},{9,11},{10,... | collective-permute-start | bytes 49160 | tf_op jit(solution)/shard_map/ppermute | solution.py:407
  17.4 2.1 %collective-permute-start.4 = (bf16[64,128]{1,0:T(8,128)(2,1)S(1)}, bf16[64,128]{1,0:T(8,128)(2,1)S(1)}, u32[]{:S(2)}, u32[]{:S(2)}) collective-permute-start(bf16[64,128]{1,0:T(8,128)(2,1)S(1)} %fields.1.refs_0_), channel_id=1, source_target_pairs={{0,3},{1,2},{2,1},{3,0},{4,5},{5,4},{6,7},{7,6},{8,11},{9,10},{10,... | collective-permute-start | bytes 49160 | tf_op jit(solution)/shard_map/ppermute | solution.py:407
  19.5 0.0 collective-permute-done.6.refs_3_
  19.5 0.9 %collective-permute-done.5.refs_2_ = bf16[64,128]{1,0:T(8,128)(2,1)S(1)} collective-permute-done((bf16[64,128]{1,0:T(8,128)(2,1)S(1)}, bf16[64,128]{1,0:T(8,128)(2,1)S(1)}, u32[]{:S(2)}, u32[]{:S(2)}) %collective-permute-start.5) | collective-permute-done | bytes 16416 | tf_op jit(solution)/shard_map/ppermute | solution.py:407
  20.4 2.6 %collective-permute-done.4.refs_1_ = bf16[64,128]{1,0:T(8,128)(2,1)S(1)} collective-permute-done((bf16[64,128]{1,0:T(8,128)(2,1)S(1)}, bf16[64,128]{1,0:T(8,128)(2,1)S(1)}, u32[]{:S(2)}, u32[]{:S(2)}) %collective-permute-start.4) | collective-permute-done | bytes 16416 | tf_op jit(solution)/shard_map/ppermute | solution.py:407
  23.0 1.9 %collective-permute-start.8 = (bf16[64,128]{1,0:T(8,128)(2,1)S(1)}, bf16[64,128]{1,0:T(8,128)(2,1)S(1)}, u32[]{:S(2)}, u32[]{:S(2)}) collective-permute-start(bf16[64,128]{1,0:T(8,128)(2,1)S(1)} %total.1.own), channel_id=1, source_target_pairs={{4,8},{8,4},{12,16},{16,12},{20,24},{24,20},{5,9},{9,5},{13,17},{1... | collective-permute-start | bytes 49160 | tf_op jit(solution)/shard_map/ppermute | solution.py:411
  24.9 1.7 %collective-permute-start.7 = (bf16[64,128]{1,0:T(8,128)(2,1)S(1)}, bf16[64,128]{1,0:T(8,128)(2,1)S(1)}, u32[]{:S(2)}, u32[]{:S(2)}) collective-permute-start(bf16[64,128]{1,0:T(8,128)(2,1)S(1)} %total.1.own), channel_id=1, source_target_pairs={{0,4},{4,0},{8,12},{12,8},{16,20},{20,16},{24,28},{28,24},{1,5},{5... | collective-permute-start | bytes 49160 | tf_op jit(solution)/shard_map/ppermute | solution.py:409
  26.6 0.0 copy-done
  26.6 0.5 %inner.1.begun = f32[288,1152]{1,0:T(8,128)S(1)} custom-call(bf16[64,128]{1,0:T(8,128)(2,1)S(1)} %total.1.own, bf16[1152,128]{1,0:T(8,128)(2,1)S(1)} %get-tuple-element.16.mid.refs_2_, bf16[128,1152]{1,0:T(8,128)(2,1)S(1)} %copy-done), custom_call_target="tpu_custom_call" | custom-call | flops 84934656 | bytes 1327104 | tf_op jit(solution)/shard_map/inner/pallas_call | solution.py:95
  27.1 1.8 %collective-permute-done.8.far = bf16[64,128]{1,0:T(8,128)(2,1)S(1)} collective-permute-done((bf16[64,128]{1,0:T(8,128)(2,1)S(1)}, bf16[64,128]{1,0:T(8,128)(2,1)S(1)}, u32[]{:S(2)}, u32[]{:S(2)}) %collective-permute-start.8) | collective-permute-done | bytes 16416 | tf_op jit(solution)/shard_map/ppermute | solution.py:411
  28.9 0.0 collective-permute-done.7.near
  28.9 0.0 copy-done.1
  28.9 1.1 %outer.1 = f32[288,1152]{1,0:T(8,128)} custom-call(bf16[64,128]{1,0:T(8,128)(2,1)S(1)} %collective-permute-done.7.near, bf16[64,128]{1,0:T(8,128)(2,1)S(1)} %collective-permute-done.8.far, bf16[144,128]{1,0:T(8,128)(2,1)S(1)} %collective-permute-done.refs_8_.near_pack, bf16[80,128]{1,0:T(8,128)(2,1)S(1)} %collective-permute-done.3.refs_11_.far_edge, ...), custom_call_target="tpu_custom_call" | custom-call | flops 56623104 | bytes 294912 | tf_op jit(solution)/shard_map/outer/pallas_call | solution.py:95
  (5 shorter events, 0.0 us)
Async XLA Ops:
  0.7 7.5 %copy-start.2 = (bf16[4,128,128]{2,1,0:T(8,128)(2,1)S(1)}, bf16[4,128,128]{2,1,0:T(8,128)(2,1)}, u32[]{:S(2)}) copy-start(bf16[4,128,128]{2,1,0:T(8,128)(2,1)} %constant.18.clone.rims) | copy-start | bytes 393220
  2.7 6.5 %collective-permute-start.1 = (bf16[64,128]{1,0:T(8,128)(2,1)S(1)}, bf16[64,128]{1,0:T(8,128)(2,1)S(1)}, u32[]{:S(2)}, u32[]{:S(2)}) collective-permute-start(bf16[64,128]{1,0:T(8,128)(2,1)S(1)} %get-tuple-element.22.refs_7_), channel_id=1, source_target_pairs={{0,2},{1,3},{2,0},{3,1},{4,7},{5,6},{6,5},{7,4},{8,10},{9,11},{10,... | collective-permute-start | bytes 49160 | tf_op jit(solution)/shard_map/ppermute | solution.py:361
  5.4 4.1 %collective-permute-start.3 = (bf16[80,128]{1,0:T(8,128)(2,1)S(1)}, bf16[80,128]{1,0:T(8,128)(2,1)S(1)}, u32[]{:S(2)}, u32[]{:S(2)}) collective-permute-start(bf16[80,128]{1,0:T(8,128)(2,1)S(1)} %get-tuple-element.24), channel_id=1, source_target_pairs={{0,28},{1,29},{2,30},{3,31},{4,8},{5,9},{6,10},{7,11},{8,4},{9,5},... | collective-permute-start | bytes 61448 | tf_op jit(solution)/shard_map/ppermute | solution.py:355
  7.0 3.6 %collective-permute-start = (bf16[144,128]{1,0:T(8,128)(2,1)S(1)}, bf16[144,128]{1,0:T(8,128)(2,1)S(1)}, u32[]{:S(2)}, u32[]{:S(2)}) collective-permute-start(bf16[144,128]{1,0:T(8,128)(2,1)S(1)} %get-tuple-element.23), channel_id=1, source_target_pairs={{0,5},{1,4},{2,7},{3,6},{4,1},{5,0},{6,3},{7,2},{8,13},{9,12},{10,... | collective-permute-start | bytes 110600 | tf_op jit(solution)/shard_map/ppermute | solution.py:356
  8.1 2.4 %copy-start.3 = (s32[288,1152]{1,0:T(8,128)S(1)}, s32[288,1152]{1,0:T(8,128)}, u32[]{:S(2)}) copy-start(s32[288,1152]{1,0:T(8,128)} %refs_1_.1) | copy-start | bytes 3981316
  8.1 2.4 %copy-start.4 = (bf16[9,256,128]{2,1,0:T(8,128)(2,1)S(1)}, bf16[9,256,128]{2,1,0:T(8,128)(2,1)}, u32[]{:S(2)}) copy-start(bf16[9,256,128]{2,1,0:T(8,128)(2,1)} %constant.17.clone.refs_5_) | copy-start | bytes 1769476
  8.1 2.4 %copy-start.5 = (bf16[9,128,256]{2,1,0:T(8,128)(2,1)S(1)}, bf16[9,128,256]{2,1,0:T(8,128)(2,1)}, u32[]{:S(2)}) copy-start(bf16[9,128,256]{2,1,0:T(8,128)(2,1)} %constant.16.clone.refs_4_) | copy-start | bytes 1769476
  9.3 1.2 %collective-permute-start.2 = (bf16[64,128]{1,0:T(8,128)(2,1)S(1)}, bf16[64,128]{1,0:T(8,128)(2,1)S(1)}, u32[]{:S(2)}, u32[]{:S(2)}) collective-permute-start(bf16[64,128]{1,0:T(8,128)(2,1)S(1)} %relay.1), channel_id=1, source_target_pairs={{0,4},{1,5},{2,6},{3,7},{4,0},{5,1},{6,2},{7,3},{8,12},{9,13},{10,... | collective-permute-start | bytes 49160 | tf_op jit(solution)/shard_map/ppermute | solution.py:381
  10.6 16.0 %copy-start = (bf16[128,1152]{1,0:T(8,128)(2,1)S(1)}, bf16[128,1152]{1,0:T(8,128)(2,1)}, u32[]{:S(2)}) copy-start(bf16[128,1152]{1,0:T(8,128)(2,1)} %constant.19.clone.back) | copy-start | bytes 884740
  15.0 13.9 %copy-start.1 = (bf16[4,128,128]{2,1,0:T(8,128)(2,1)S(1)}, bf16[4,128,128]{2,1,0:T(8,128)(2,1)}, u32[]{:S(2)}) copy-start(bf16[4,128,128]{2,1,0:T(8,128)(2,1)} %constant.20.clone.margins) | copy-start | bytes 393220
  15.0 4.5 %collective-permute-start.6 = (bf16[64,128]{1,0:T(8,128)(2,1)S(1)}, bf16[64,128]{1,0:T(8,128)(2,1)S(1)}, u32[]{:S(2)}, u32[]{:S(2)}) collective-permute-start(bf16[64,128]{1,0:T(8,128)(2,1)S(1)} %fields.1.refs_0_), channel_id=1, source_target_pairs={{0,1},{1,0},{2,3},{3,2},{4,7},{5,6},{6,5},{7,4},{8,9},{9,8},{10,11... | collective-permute-start | bytes 49160 | tf_op jit(solution)/shard_map/ppermute | solution.py:407
  15.7 4.7 %collective-permute-start.5 = (bf16[64,128]{1,0:T(8,128)(2,1)S(1)}, bf16[64,128]{1,0:T(8,128)(2,1)S(1)}, u32[]{:S(2)}, u32[]{:S(2)}) collective-permute-start(bf16[64,128]{1,0:T(8,128)(2,1)S(1)} %fields.1.refs_0_), channel_id=1, source_target_pairs={{0,2},{1,3},{2,0},{3,1},{4,6},{5,7},{6,4},{7,5},{8,10},{9,11},{10,... | collective-permute-start | bytes 49160 | tf_op jit(solution)/shard_map/ppermute | solution.py:407
  17.4 5.5 %collective-permute-start.4 = (bf16[64,128]{1,0:T(8,128)(2,1)S(1)}, bf16[64,128]{1,0:T(8,128)(2,1)S(1)}, u32[]{:S(2)}, u32[]{:S(2)}) collective-permute-start(bf16[64,128]{1,0:T(8,128)(2,1)S(1)} %fields.1.refs_0_), channel_id=1, source_target_pairs={{0,3},{1,2},{2,1},{3,0},{4,5},{5,4},{6,7},{7,6},{8,11},{9,10},{10,... | collective-permute-start | bytes 49160 | tf_op jit(solution)/shard_map/ppermute | solution.py:407
  23.0 6.0 %collective-permute-start.8 = (bf16[64,128]{1,0:T(8,128)(2,1)S(1)}, bf16[64,128]{1,0:T(8,128)(2,1)S(1)}, u32[]{:S(2)}, u32[]{:S(2)}) collective-permute-start(bf16[64,128]{1,0:T(8,128)(2,1)S(1)} %total.1.own), channel_id=1, source_target_pairs={{4,8},{8,4},{12,16},{16,12},{20,24},{24,20},{5,9},{9,5},{13,17},{1... | collective-permute-start | bytes 49160 | tf_op jit(solution)/shard_map/ppermute | solution.py:411
  24.9 4.0 %collective-permute-start.7 = (bf16[64,128]{1,0:T(8,128)(2,1)S(1)}, bf16[64,128]{1,0:T(8,128)(2,1)S(1)}, u32[]{:S(2)}, u32[]{:S(2)}) collective-permute-start(bf16[64,128]{1,0:T(8,128)(2,1)S(1)} %total.1.own), channel_id=1, source_target_pairs={{0,4},{4,0},{8,12},{12,8},{16,20},{20,16},{24,28},{28,24},{1,5},{5... | collective-permute-start | bytes 49160 | tf_op jit(solution)/shard_map/ppermute | solution.py:409

commit v2 on v1

--- a/solution.py
+++ b/solution.py
@@ -80,6 +80,10 @@
 
 def swap_halves(pair):
     return pltpu.roll(pair, KF, 1)
+
+
+def sum_step(step, tile, count):
+    return (step, (2, 3, 1)[step - 1])[tile % 2] if count == 4 else step
 
 
 def destination(k, step, count):
@@ -402,7 +406,7 @@
     for step in range(1, count):
         pairs = []
         for t in range(tiles):
-            own_step = step if t % 2 else count - step
+            own_step = sum_step(step, t, count)
             pairs += [(t * count + k, t * count + destination(k, own_step, count)) for k in range(count)]
         parts.append(lax.ppermute(part, both, pairs))
     own = call(functools.partial(sum_body, count), "total", small, tuple(parts), [vmem] * count)

time: 30.2 us -> 28.9 us (0.957)
  waiting for transfers between devices: 6.51 us -> 5.05 us
    ppermute x3, waiting for transfers between devices: 3.47 us -> 2.01 us  [per_device(): parts.append(lax.ppermute(part, both, pairs))]
    ppermute x1, starting transfers between devices: 1.92 us -> 2.28 us  [per_device(): far = lax.ppermute(own, 'tile', [(t, other_side(t)) for t in inner])]
    ppermute x1, starting transfers between devices: 1.68 us -> 1.32 us  [per_device(): near = lax.ppermute(own, 'tile', [(t, chip_mate(t)) for t in range(tiles)])]
  transfers between devices with their start and end apart: 9 -> 9, of which waited for: 5 -> 5; matrix products, arithmetic and copies ran while one was open for 0% -> 0% of each run, Pallas kernels for 5% -> 6%
where the time goes in v2:
time: 28.9 us; the launch traced here: 28.6 us
  starting transfers between devices  13.6 us (47%)
  Pallas kernels  9.18 us (32%)
  waiting for transfers between devices  5.05 us (17%)
  between operations  0.75 us (3%)
    pallas_call x7, Pallas kernels, call(): pl.pallas_call(body, name=name, out_shape=outs, in_specs=specs, out_specs...  9.18 us
    ppermute x3, starting transfers between devices, per_device(): parts.append(lax.ppermute(part, both, pairs))  4.45 us
    ppermute x1, starting transfers between devices, per_device(): kernels = [lax.ppermute(side, both, pairs)]  2.65 us
    ppermute x1, starting transfers between devices, per_device(): far = lax.ppermute(own, 'tile', [(t, other_side(t)) for t in inner])  2.28 us
    ppermute x3, waiting for transfers between devices, per_device(): parts.append(lax.ppermute(part, both, pairs))  2.01 us
    ppermute x1, waiting for transfers between devices, per_device(): far = lax.ppermute(own, 'tile', [(t, other_side(t)) for t in inner])  1.82 us
    ppermute x1, starting transfers between devices, per_device(): far_edge = lax.ppermute(other, both, swapped(other_side, 0))  1.61 us
    ppermute x1, starting transfers between devices, per_device(): near = lax.ppermute(own, 'tile', [(t, chip_mate(t)) for t in range(tiles)])  1.32 us
  transfers between devices with their start and end apart: 9, of which 5 were waited for; matrix products, arithmetic and copies ran while one was open for 0% of the time, Pallas kernels for 6%

profile of v2, /device:TPU:4, one launch (start us, length us, event | category | flops | bytes accessed | tf_op | source)
XLA Modules:
  0.0 28.6 jit_solution(8315943634018482180)
XLA Ops:
  0.7 0.0 copy-start.2
  0.7 2.0 %edges.1 = (bf16[144,128]{1,0:T(8,128)(2,1)S(1)}, bf16[80,128]{1,0:T(8,128)(2,1)S(1)}, bf16[64,128]{1,0:T(8,128)(2,1)S(1)}, bf16[1152,1152]{1,0:T(8,128)(2,1)S(1...) custom-call(bf16[1152,1152]{1,0:T(8,128)(2,1)} %mask.1, ...), custom_call_target="tpu_custom_call" | custom-call | flops 75497472 | bytes 589824 | tf_op jit(solution)/shard_map/edges/pallas_call | solution.py:99
  2.7 2.7 %collective-permute-start.1 = (bf16[64,128]{1,0:T(8,128)(2,1)S(1)}, bf16[64,128]{1,0:T(8,128)(2,1)S(1)}, u32[]{:S(2)}, u32[]{:S(2)}) collective-permute-start(bf16[64,128]{1,0:T(8,128)(2,1)S(1)} %get-tuple-element.22.refs_7_), channel_id=1, source_target_pairs={{0,2},{1,3},{2,0},{3,1},{4,7},{5,6},{6,5},{7,4},{8,10},{9,11},{10,... | collective-permute-start | bytes 49160 | tf_op jit(solution)/shard_map/ppermute | solution.py:365
  5.4 1.6 %collective-permute-start.3 = (bf16[80,128]{1,0:T(8,128)(2,1)S(1)}, bf16[80,128]{1,0:T(8,128)(2,1)S(1)}, u32[]{:S(2)}, u32[]{:S(2)}) collective-permute-start(bf16[80,128]{1,0:T(8,128)(2,1)S(1)} %get-tuple-element.24), channel_id=1, source_target_pairs={{0,28},{1,29},{2,30},{3,31},{4,8},{5,9},{6,10},{7,11},{8,4},{9,5},... | collective-permute-start | bytes 61448 | tf_op jit(solution)/shard_map/ppermute | solution.py:359
  7.0 1.2 %collective-permute-start = (bf16[144,128]{1,0:T(8,128)(2,1)S(1)}, bf16[144,128]{1,0:T(8,128)(2,1)S(1)}, u32[]{:S(2)}, u32[]{:S(2)}) collective-permute-start(bf16[144,128]{1,0:T(8,128)(2,1)S(1)} %get-tuple-element.23), channel_id=1, source_target_pairs={{0,5},{1,4},{2,7},{3,6},{4,1},{5,0},{6,3},{7,2},{8,13},{9,12},{10,... | collective-permute-start | bytes 110600 | tf_op jit(solution)/shard_map/ppermute | solution.py:360
  8.1 0.0 copy-done.2
  8.2 1.1 %middle.1 = (f32[128,128]{1,0:T(8,128)S(1)}, bf16[2,128,128]{2,1,0:T(8,128)(2,1)S(1)}, bf16[128,288]{1,0:T(8,128)(2,1)S(1)}) custom-call(bf16[1152,1152]{1,0:T(8,128)(2,1)S(1)} %get-tuple-element.15.mask, bf16[1152,128]{1,0:T(8,128)(2,1)S(1)} %get-tuple-element.16.mid.refs_2_, bf16[128,1152]{1,0:T(8,128)(2,1)S(1)} %get-tuple-element.17.mid_t, ...), custom_call_target="tpu_custom_call" | custom-call | flops 679477248 | bytes 2654208 | tf_op jit(solution)/shard_map/middle/pallas_call | solution.py:99
  9.2 0.0 collective-permute-done.1.value.refs_9_
  9.3 0.1 collective-permute-start.2
  9.3 0.1 collective-permute-done.3.refs_11_.far_edge
  9.5 1.0 %collective-permute-done.2.refs_10_ = bf16[64,128]{1,0:T(8,128)(2,1)S(1)} collective-permute-done((bf16[64,128]{1,0:T(8,128)(2,1)S(1)}, bf16[64,128]{1,0:T(8,128)(2,1)S(1)}, u32[]{:S(2)}, u32[]{:S(2)}) %collective-permute-start.2) | collective-permute-done | bytes 16416 | tf_op jit(solution)/shard_map/ppermute | solution.py:385
  10.5 0.0 collective-permute-done.refs_8_.near_pack
  10.6 0.0 copy-done.3
  10.6 0.0 copy-done.4
  10.6 0.0 copy-done.5
  10.6 0.0 copy-start
  10.6 4.4 %fields.1.refs_0_ = bf16[64,128]{1,0:T(8,128)(2,1)S(1)} custom-call(f32[128,128]{1,0:T(8,128)S(1)} %get-tuple-element.19.ready.refs_0_, s32[288,1152]{1,0:T(8,128)S(1)} %copy-done.3, bf16[1152,128]{1,0:T(8,128)(2,1)S(1)} %get-tuple-element.16.mid.refs_2_, bf16[128,288]{1,0:T(8,128)(2,1)S(1)} %get-tuple-element.20.refs_3_, ...), custom_call_target="tpu_custom_call" | custom-call | flops 1358954496 | bytes 1327104 | tf_op jit(solution)/shard_map/fields/pallas_call | solution.py:99
  15.0 0.0 copy-start.1
  15.0 1.8 %collective-permute-start.6 = (bf16[64,128]{1,0:T(8,128)(2,1)S(1)}, bf16[64,128]{1,0:T(8,128)(2,1)S(1)}, u32[]{:S(2)}, u32[]{:S(2)}) collective-permute-start(bf16[64,128]{1,0:T(8,128)(2,1)S(1)} %fields.1.refs_0_), channel_id=1, source_target_pairs={{0,3},{1,2},{2,1},{3,0},{4,5},{5,4},{6,7},{7,6},{8,11},{9,10},{10,... | collective-permute-start | bytes 49160 | tf_op jit(solution)/shard_map/ppermute | solution.py:411
  16.9 0.3 collective-permute-start.5
  17.1 2.3 %collective-permute-start.4 = (bf16[64,128]{1,0:T(8,128)(2,1)S(1)}, bf16[64,128]{1,0:T(8,128)(2,1)S(1)}, u32[]{:S(2)}, u32[]{:S(2)}) collective-permute-start(bf16[64,128]{1,0:T(8,128)(2,1)S(1)} %fields.1.refs_0_), channel_id=1, source_target_pairs={{0,1},{1,0},{2,3},{3,2},{4,6},{5,7},{6,4},{7,5},{8,9},{9,8},{10,11... | collective-permute-start | bytes 49160 | tf_op jit(solution)/shard_map/ppermute | solution.py:411
  19.5 1.3 %collective-permute-done.6.refs_3_ = bf16[64,128]{1,0:T(8,128)(2,1)S(1)} collective-permute-done((bf16[64,128]{1,0:T(8,128)(2,1)S(1)}, bf16[64,128]{1,0:T(8,128)(2,1)S(1)}, u32[]{:S(2)}, u32[]{:S(2)}) %collective-permute-start.6) | collective-permute-done | bytes 16416 | tf_op jit(solution)/shard_map/ppermute | solution.py:411
  20.8 0.7 %collective-permute-done.5.refs_2_ = bf16[64,128]{1,0:T(8,128)(2,1)S(1)} collective-permute-done((bf16[64,128]{1,0:T(8,128)(2,1)S(1)}, bf16[64,128]{1,0:T(8,128)(2,1)S(1)}, u32[]{:S(2)}, u32[]{:S(2)}) %collective-permute-start.5) | collective-permute-done | bytes 16416 | tf_op jit(solution)/shard_map/ppermute | solution.py:411
  21.5 0.0 collective-permute-done.4.refs_1_
  21.5 2.3 %collective-permute-start.8 = (bf16[64,128]{1,0:T(8,128)(2,1)S(1)}, bf16[64,128]{1,0:T(8,128)(2,1)S(1)}, u32[]{:S(2)}, u32[]{:S(2)}) collective-permute-start(bf16[64,128]{1,0:T(8,128)(2,1)S(1)} %total.1.own), channel_id=1, source_target_pairs={{4,8},{8,4},{12,16},{16,12},{20,24},{24,20},{5,9},{9,5},{13,17},{1... | collective-permute-start | bytes 49160 | tf_op jit(solution)/shard_map/ppermute | solution.py:415
  23.8 1.3 %collective-permute-start.7 = (bf16[64,128]{1,0:T(8,128)(2,1)S(1)}, bf16[64,128]{1,0:T(8,128)(2,1)S(1)}, u32[]{:S(2)}, u32[]{:S(2)}) collective-permute-start(bf16[64,128]{1,0:T(8,128)(2,1)S(1)} %total.1.own), channel_id=1, source_target_pairs={{0,4},{4,0},{8,12},{12,8},{16,20},{20,16},{24,28},{28,24},{1,5},{5... | collective-permute-start | bytes 49160 | tf_op jit(solution)/shard_map/ppermute | solution.py:413
  25.1 0.0 copy-done
  25.1 0.5 %inner.1.begun = f32[288,1152]{1,0:T(8,128)S(1)} custom-call(bf16[64,128]{1,0:T(8,128)(2,1)S(1)} %total.1.own, bf16[1152,128]{1,0:T(8,128)(2,1)S(1)} %get-tuple-element.16.mid.refs_2_, bf16[128,1152]{1,0:T(8,128)(2,1)S(1)} %copy-done), custom_call_target="tpu_custom_call" | custom-call | flops 84934656 | bytes 1327104 | tf_op jit(solution)/shard_map/inner/pallas_call | solution.py:99
  25.6 1.8 %collective-permute-done.8.far = bf16[64,128]{1,0:T(8,128)(2,1)S(1)} collective-permute-done((bf16[64,128]{1,0:T(8,128)(2,1)S(1)}, bf16[64,128]{1,0:T(8,128)(2,1)S(1)}, u32[]{:S(2)}, u32[]{:S(2)}) %collective-permute-start.8) | collective-permute-done | bytes 16416 | tf_op jit(solution)/shard_map/ppermute | solution.py:415
  27.5 0.0 collective-permute-done.7.near
  27.5 0.0 copy-done.1
  27.5 1.1 %outer.1 = f32[288,1152]{1,0:T(8,128)} custom-call(bf16[64,128]{1,0:T(8,128)(2,1)S(1)} %collective-permute-done.7.near, bf16[64,128]{1,0:T(8,128)(2,1)S(1)} %collective-permute-done.8.far, bf16[144,128]{1,0:T(8,128)(2,1)S(1)} %collective-permute-done.refs_8_.near_pack, bf16[80,128]{1,0:T(8,128)(2,1)S(1)} %collective-permute-done.3.refs_11_.far_edge, ...), custom_call_target="tpu_custom_call" | custom-call | flops 56623104 | bytes 294912 | tf_op jit(solution)/shard_map/outer/pallas_call | solution.py:99
  (5 shorter events, 0.0 us)
Async XLA Ops:
  0.7 7.5 %copy-start.2 = (bf16[4,128,128]{2,1,0:T(8,128)(2,1)S(1)}, bf16[4,128,128]{2,1,0:T(8,128)(2,1)}, u32[]{:S(2)}) copy-start(bf16[4,128,128]{2,1,0:T(8,128)(2,1)} %constant.18.clone.rims) | copy-start | bytes 393220
  2.7 6.5 %collective-permute-start.1 = (bf16[64,128]{1,0:T(8,128)(2,1)S(1)}, bf16[64,128]{1,0:T(8,128)(2,1)S(1)}, u32[]{:S(2)}, u32[]{:S(2)}) collective-permute-start(bf16[64,128]{1,0:T(8,128)(2,1)S(1)} %get-tuple-element.22.refs_7_), channel_id=1, source_target_pairs={{0,2},{1,3},{2,0},{3,1},{4,7},{5,6},{6,5},{7,4},{8,10},{9,11},{10,... | collective-permute-start | bytes 49160 | tf_op jit(solution)/shard_map/ppermute | solution.py:365
  5.4 4.1 %collective-permute-start.3 = (bf16[80,128]{1,0:T(8,128)(2,1)S(1)}, bf16[80,128]{1,0:T(8,128)(2,1)S(1)}, u32[]{:S(2)}, u32[]{:S(2)}) collective-permute-start(bf16[80,128]{1,0:T(8,128)(2,1)S(1)} %get-tuple-element.24), channel_id=1, source_target_pairs={{0,28},{1,29},{2,30},{3,31},{4,8},{5,9},{6,10},{7,11},{8,4},{9,5},... | collective-permute-start | bytes 61448 | tf_op jit(solution)/shard_map/ppermute | solution.py:359
  7.0 3.6 %collective-permute-start = (bf16[144,128]{1,0:T(8,128)(2,1)S(1)}, bf16[144,128]{1,0:T(8,128)(2,1)S(1)}, u32[]{:S(2)}, u32[]{:S(2)}) collective-permute-start(bf16[144,128]{1,0:T(8,128)(2,1)S(1)} %get-tuple-element.23), channel_id=1, source_target_pairs={{0,5},{1,4},{2,7},{3,6},{4,1},{5,0},{6,3},{7,2},{8,13},{9,12},{10,... | collective-permute-start | bytes 110600 | tf_op jit(solution)/shard_map/ppermute | solution.py:360
  8.1 2.4 %copy-start.3 = (s32[288,1152]{1,0:T(8,128)S(1)}, s32[288,1152]{1,0:T(8,128)}, u32[]{:S(2)}) copy-start(s32[288,1152]{1,0:T(8,128)} %refs_1_.1) | copy-start | bytes 3981316
  8.1 2.4 %copy-start.4 = (bf16[9,256,128]{2,1,0:T(8,128)(2,1)S(1)}, bf16[9,256,128]{2,1,0:T(8,128)(2,1)}, u32[]{:S(2)}) copy-start(bf16[9,256,128]{2,1,0:T(8,128)(2,1)} %constant.17.clone.refs_5_) | copy-start | bytes 1769476
  8.1 2.4 %copy-start.5 = (bf16[9,128,256]{2,1,0:T(8,128)(2,1)S(1)}, bf16[9,128,256]{2,1,0:T(8,128)(2,1)}, u32[]{:S(2)}) copy-start(bf16[9,128,256]{2,1,0:T(8,128)(2,1)} %constant.16.clone.refs_4_) | copy-start | bytes 1769476
  9.3 1.2 %collective-permute-start.2 = (bf16[64,128]{1,0:T(8,128)(2,1)S(1)}, bf16[64,128]{1,0:T(8,128)(2,1)S(1)}, u32[]{:S(2)}, u32[]{:S(2)}) collective-permute-start(bf16[64,128]{1,0:T(8,128)(2,1)S(1)} %relay.1), channel_id=1, source_target_pairs={{0,4},{1,5},{2,6},{3,7},{4,0},{5,1},{6,2},{7,3},{8,12},{9,13},{10,... | collective-permute-start | bytes 49160 | tf_op jit(solution)/shard_map/ppermute | solution.py:385
  10.6 14.6 %copy-start = (bf16[128,1152]{1,0:T(8,128)(2,1)S(1)}, bf16[128,1152]{1,0:T(8,128)(2,1)}, u32[]{:S(2)}) copy-start(bf16[128,1152]{1,0:T(8,128)(2,1)} %constant.19.clone.back) | copy-start | bytes 884740
  15.0 12.5 %copy-start.1 = (bf16[4,128,128]{2,1,0:T(8,128)(2,1)S(1)}, bf16[4,128,128]{2,1,0:T(8,128)(2,1)}, u32[]{:S(2)}) copy-start(bf16[4,128,128]{2,1,0:T(8,128)(2,1)} %constant.20.clone.margins) | copy-start | bytes 393220
  15.0 5.7 %collective-permute-start.6 = (bf16[64,128]{1,0:T(8,128)(2,1)S(1)}, bf16[64,128]{1,0:T(8,128)(2,1)S(1)}, u32[]{:S(2)}, u32[]{:S(2)}) collective-permute-start(bf16[64,128]{1,0:T(8,128)(2,1)S(1)} %fields.1.refs_0_), channel_id=1, source_target_pairs={{0,3},{1,2},{2,1},{3,0},{4,5},{5,4},{6,7},{7,6},{8,11},{9,10},{10,... | collective-permute-start | bytes 49160 | tf_op jit(solution)/shard_map/ppermute | solution.py:411
  16.9 4.6 %collective-permute-start.5 = (bf16[64,128]{1,0:T(8,128)(2,1)S(1)}, bf16[64,128]{1,0:T(8,128)(2,1)S(1)}, u32[]{:S(2)}, u32[]{:S(2)}) collective-permute-start(bf16[64,128]{1,0:T(8,128)(2,1)S(1)} %fields.1.refs_0_), channel_id=1, source_target_pairs={{0,2},{1,3},{2,0},{3,1},{4,7},{5,6},{6,5},{7,4},{8,10},{9,11},{10,... | collective-permute-start | bytes 49160 | tf_op jit(solution)/shard_map/ppermute | solution.py:411
  17.1 4.4 %collective-permute-start.4 = (bf16[64,128]{1,0:T(8,128)(2,1)S(1)}, bf16[64,128]{1,0:T(8,128)(2,1)S(1)}, u32[]{:S(2)}, u32[]{:S(2)}) collective-permute-start(bf16[64,128]{1,0:T(8,128)(2,1)S(1)} %fields.1.refs_0_), channel_id=1, source_target_pairs={{0,1},{1,0},{2,3},{3,2},{4,6},{5,7},{6,4},{7,5},{8,9},{9,8},{10,11... | collective-permute-start | bytes 49160 | tf_op jit(solution)/shard_map/ppermute | solution.py:411
  21.5 6.0 %collective-permute-start.8 = (bf16[64,128]{1,0:T(8,128)(2,1)S(1)}, bf16[64,128]{1,0:T(8,128)(2,1)S(1)}, u32[]{:S(2)}, u32[]{:S(2)}) collective-permute-start(bf16[64,128]{1,0:T(8,128)(2,1)S(1)} %total.1.own), channel_id=1, source_target_pairs={{4,8},{8,4},{12,16},{16,12},{20,24},{24,20},{5,9},{9,5},{13,17},{1... | collective-permute-start | bytes 49160 | tf_op jit(solution)/shard_map/ppermute | solution.py:415
  23.8 3.7 %collective-permute-start.7 = (bf16[64,128]{1,0:T(8,128)(2,1)S(1)}, bf16[64,128]{1,0:T(8,128)(2,1)S(1)}, u32[]{:S(2)}, u32[]{:S(2)}) collective-permute-start(bf16[64,128]{1,0:T(8,128)(2,1)S(1)} %total.1.own), channel_id=1, source_target_pairs={{0,4},{4,0},{8,12},{12,8},{16,20},{20,16},{24,28},{28,24},{1,5},{5... | collective-permute-start | bytes 49160 | tf_op jit(solution)/shard_map/ppermute | solution.py:413

commit v3 on v2

--- a/solution.py
+++ b/solution.py
@@ -83,7 +83,7 @@
 
 
 def sum_step(step, tile, count):
-    return (step, (2, 3, 1)[step - 1])[tile % 2] if count == 4 else step
+    return ((2, 3, 1)[step - 1], step)[tile % 2] if count == 4 else step
 
 
 def destination(k, step, count):

time: 28.9 us -> 29.1 us (level)
  waiting for transfers between devices: 5.05 us -> 6.39 us
  starting transfers between devices: 13.6 us -> 12.6 us
    ppermute x3, waiting for transfers between devices: 2.01 us -> 3.32 us  [per_device(): parts.append(lax.ppermute(part, both, pairs))]
    ppermute x3, starting transfers between devices: 4.45 us -> 3.55 us  [per_device(): parts.append(lax.ppermute(part, both, pairs))]
    ppermute x1, starting transfers between devices: 2.28 us -> 1.92 us  [per_device(): far = lax.ppermute(own, 'tile', [(t, other_side(t)) for t in inner])]
    ppermute x1, starting transfers between devices: 1.32 us -> 1.65 us  [per_device(): near = lax.ppermute(own, 'tile', [(t, chip_mate(t)) for t in range(tiles)])]
  transfers between devices with their start and end apart: 9 -> 9, of which waited for: 5 -> 6; matrix products, arithmetic and copies ran while one was open for 0% -> 0% of each run, Pallas kernels for 6% -> 6%
where the time goes in v3:
time: 29.1 us; the launch traced here: 29 us
  starting transfers between devices  12.6 us (43%)
  Pallas kernels  9.18 us (32%)
  waiting for transfers between devices  6.39 us (22%)
  between operations  0.75 us (3%)
    pallas_call x7, Pallas kernels, call(): pl.pallas_call(body, name=name, out_shape=outs, in_specs=specs, out_specs...  9.18 us
    ppermute x3, starting transfers between devices, per_device(): parts.append(lax.ppermute(part, both, pairs))  3.55 us
    ppermute x3, waiting for transfers between devices, per_device(): parts.append(lax.ppermute(part, both, pairs))  3.32 us
    ppermute x1, starting transfers between devices, per_device(): kernels = [lax.ppermute(side, both, pairs)]  2.65 us
    ppermute x1, starting transfers between devices, per_device(): far = lax.ppermute(own, 'tile', [(t, other_side(t)) for t in inner])  1.92 us
    ppermute x1, waiting for transfers between devices, per_device(): far = lax.ppermute(own, 'tile', [(t, other_side(t)) for t in inner])  1.86 us
    ppermute x1, starting transfers between devices, per_device(): near = lax.ppermute(own, 'tile', [(t, chip_mate(t)) for t in range(tiles)])  1.65 us
    ppermute x1, starting transfers between devices, per_device(): far_edge = lax.ppermute(other, both, swapped(other_side, 0))  1.61 us
  transfers between devices with their start and end apart: 9, of which 6 were waited for; matrix products, arithmetic and copies ran while one was open for 0% of the time, Pallas kernels for 6%

profile of v3, /device:TPU:4, one launch (start us, length us, event | category | flops | bytes accessed | tf_op | source)
XLA Modules:
  0.0 29.0 jit_solution(832588455759536759)
XLA Ops:
  0.7 0.0 copy-start.2
  0.7 2.0 %edges.1 = (bf16[144,128]{1,0:T(8,128)(2,1)S(1)}, bf16[80,128]{1,0:T(8,128)(2,1)S(1)}, bf16[64,128]{1,0:T(8,128)(2,1)S(1)}, bf16[1152,1152]{1,0:T(8,128)(2,1)S(1...) custom-call(bf16[1152,1152]{1,0:T(8,128)(2,1)} %mask.1, ...), custom_call_target="tpu_custom_call" | custom-call | flops 75497472 | bytes 589824 | tf_op jit(solution)/shard_map/edges/pallas_call | solution.py:99
  2.7 2.7 %collective-permute-start.1 = (bf16[64,128]{1,0:T(8,128)(2,1)S(1)}, bf16[64,128]{1,0:T(8,128)(2,1)S(1)}, u32[]{:S(2)}, u32[]{:S(2)}) collective-permute-start(bf16[64,128]{1,0:T(8,128)(2,1)S(1)} %get-tuple-element.22.refs_7_), channel_id=1, source_target_pairs={{0,2},{1,3},{2,0},{3,1},{4,7},{5,6},{6,5},{7,4},{8,10},{9,11},{10,... | collective-permute-start | bytes 49160 | tf_op jit(solution)/shard_map/ppermute | solution.py:365
  5.4 1.6 %collective-permute-start.3 = (bf16[80,128]{1,0:T(8,128)(2,1)S(1)}, bf16[80,128]{1,0:T(8,128)(2,1)S(1)}, u32[]{:S(2)}, u32[]{:S(2)}) collective-permute-start(bf16[80,128]{1,0:T(8,128)(2,1)S(1)} %get-tuple-element.24), channel_id=1, source_target_pairs={{0,28},{1,29},{2,30},{3,31},{4,8},{5,9},{6,10},{7,11},{8,4},{9,5},... | collective-permute-start | bytes 61448 | tf_op jit(solution)/shard_map/ppermute | solution.py:359
  7.0 1.2 %collective-permute-start = (bf16[144,128]{1,0:T(8,128)(2,1)S(1)}, bf16[144,128]{1,0:T(8,128)(2,1)S(1)}, u32[]{:S(2)}, u32[]{:S(2)}) collective-permute-start(bf16[144,128]{1,0:T(8,128)(2,1)S(1)} %get-tuple-element.23), channel_id=1, source_target_pairs={{0,5},{1,4},{2,7},{3,6},{4,1},{5,0},{6,3},{7,2},{8,13},{9,12},{10,... | collective-permute-start | bytes 110600 | tf_op jit(solution)/shard_map/ppermute | solution.py:360
  8.1 0.0 copy-done.2
  8.2 1.1 %middle.1 = (f32[128,128]{1,0:T(8,128)S(1)}, bf16[2,128,128]{2,1,0:T(8,128)(2,1)S(1)}, bf16[128,288]{1,0:T(8,128)(2,1)S(1)}) custom-call(bf16[1152,1152]{1,0:T(8,128)(2,1)S(1)} %get-tuple-element.15.mask, bf16[1152,128]{1,0:T(8,128)(2,1)S(1)} %get-tuple-element.16.mid.refs_2_, bf16[128,1152]{1,0:T(8,128)(2,1)S(1)} %get-tuple-element.17.mid_t, ...), custom_call_target="tpu_custom_call" | custom-call | flops 679477248 | bytes 2654208 | tf_op jit(solution)/shard_map/middle/pallas_call | solution.py:99
  9.2 0.0 collective-permute-done.1.value.refs_9_
  9.3 0.1 collective-permute-start.2
  9.3 0.1 collective-permute-done.3.refs_11_.far_edge
  9.5 1.0 %collective-permute-done.2.refs_10_ = bf16[64,128]{1,0:T(8,128)(2,1)S(1)} collective-permute-done((bf16[64,128]{1,0:T(8,128)(2,1)S(1)}, bf16[64,128]{1,0:T(8,128)(2,1)S(1)}, u32[]{:S(2)}, u32[]{:S(2)}) %collective-permute-start.2) | collective-permute-done | bytes 16416 | tf_op jit(solution)/shard_map/ppermute | solution.py:385
  10.5 0.0 collective-permute-done.refs_8_.near_pack
  10.6 0.0 copy-done.3
  10.6 0.0 copy-done.4
  10.6 0.0 copy-done.5
  10.6 0.0 copy-start
  10.6 4.4 %fields.1.refs_0_ = bf16[64,128]{1,0:T(8,128)(2,1)S(1)} custom-call(f32[128,128]{1,0:T(8,128)S(1)} %get-tuple-element.19.ready.refs_0_, s32[288,1152]{1,0:T(8,128)S(1)} %copy-done.3, bf16[1152,128]{1,0:T(8,128)(2,1)S(1)} %get-tuple-element.16.mid.refs_2_, bf16[128,288]{1,0:T(8,128)(2,1)S(1)} %get-tuple-element.20.refs_3_, ...), custom_call_target="tpu_custom_call" | custom-call | flops 1358954496 | bytes 1327104 | tf_op jit(solution)/shard_map/fields/pallas_call | solution.py:99
  15.0 0.0 copy-start.1
  15.0 0.6 %collective-permute-start.6 = (bf16[64,128]{1,0:T(8,128)(2,1)S(1)}, bf16[64,128]{1,0:T(8,128)(2,1)S(1)}, u32[]{:S(2)}, u32[]{:S(2)}) collective-permute-start(bf16[64,128]{1,0:T(8,128)(2,1)S(1)} %fields.1.refs_0_), channel_id=1, source_target_pairs={{0,1},{1,0},{2,3},{3,2},{4,7},{5,6},{6,5},{7,4},{8,9},{9,8},{10,11... | collective-permute-start | bytes 49160 | tf_op jit(solution)/shard_map/ppermute | solution.py:411
  15.7 1.6 %collective-permute-start.5 = (bf16[64,128]{1,0:T(8,128)(2,1)S(1)}, bf16[64,128]{1,0:T(8,128)(2,1)S(1)}, u32[]{:S(2)}, u32[]{:S(2)}) collective-permute-start(bf16[64,128]{1,0:T(8,128)(2,1)S(1)} %fields.1.refs_0_), channel_id=1, source_target_pairs={{0,3},{1,2},{2,1},{3,0},{4,6},{5,7},{6,4},{7,5},{8,11},{9,10},{10,... | collective-permute-start | bytes 49160 | tf_op jit(solution)/shard_map/ppermute | solution.py:411
  17.2 1.3 %collective-permute-start.4 = (bf16[64,128]{1,0:T(8,128)(2,1)S(1)}, bf16[64,128]{1,0:T(8,128)(2,1)S(1)}, u32[]{:S(2)}, u32[]{:S(2)}) collective-permute-start(bf16[64,128]{1,0:T(8,128)(2,1)S(1)} %fields.1.refs_0_), channel_id=1, source_target_pairs={{0,2},{1,3},{2,0},{3,1},{4,5},{5,4},{6,7},{7,6},{8,10},{9,11},{10,... | collective-permute-start | bytes 49160 | tf_op jit(solution)/shard_map/ppermute | solution.py:411
  18.6 0.2 collective-permute-done.6.refs_3_
  18.8 2.4 %collective-permute-done.5.refs_2_ = bf16[64,128]{1,0:T(8,128)(2,1)S(1)} collective-permute-done((bf16[64,128]{1,0:T(8,128)(2,1)S(1)}, bf16[64,128]{1,0:T(8,128)(2,1)S(1)}, u32[]{:S(2)}, u32[]{:S(2)}) %collective-permute-start.5) | collective-permute-done | bytes 16416 | tf_op jit(solution)/shard_map/ppermute | solution.py:411
  21.2 0.7 %collective-permute-done.4.refs_1_ = bf16[64,128]{1,0:T(8,128)(2,1)S(1)} collective-permute-done((bf16[64,128]{1,0:T(8,128)(2,1)S(1)}, bf16[64,128]{1,0:T(8,128)(2,1)S(1)}, u32[]{:S(2)}, u32[]{:S(2)}) %collective-permute-start.4) | collective-permute-done | bytes 16416 | tf_op jit(solution)/shard_map/ppermute | solution.py:411
  21.9 1.9 %collective-permute-start.8 = (bf16[64,128]{1,0:T(8,128)(2,1)S(1)}, bf16[64,128]{1,0:T(8,128)(2,1)S(1)}, u32[]{:S(2)}, u32[]{:S(2)}) collective-permute-start(bf16[64,128]{1,0:T(8,128)(2,1)S(1)} %total.1.own), channel_id=1, source_target_pairs={{4,8},{8,4},{12,16},{16,12},{20,24},{24,20},{5,9},{9,5},{13,17},{1... | collective-permute-start | bytes 49160 | tf_op jit(solution)/shard_map/ppermute | solution.py:415
  23.8 1.6 %collective-permute-start.7 = (bf16[64,128]{1,0:T(8,128)(2,1)S(1)}, bf16[64,128]{1,0:T(8,128)(2,1)S(1)}, u32[]{:S(2)}, u32[]{:S(2)}) collective-permute-start(bf16[64,128]{1,0:T(8,128)(2,1)S(1)} %total.1.own), channel_id=1, source_target_pairs={{0,4},{4,0},{8,12},{12,8},{16,20},{20,16},{24,28},{28,24},{1,5},{5... | collective-permute-start | bytes 49160 | tf_op jit(solution)/shard_map/ppermute | solution.py:413
  25.5 0.0 copy-done
  25.5 0.5 %inner.1.begun = f32[288,1152]{1,0:T(8,128)S(1)} custom-call(bf16[64,128]{1,0:T(8,128)(2,1)S(1)} %total.1.own, bf16[1152,128]{1,0:T(8,128)(2,1)S(1)} %get-tuple-element.16.mid.refs_2_, bf16[128,1152]{1,0:T(8,128)(2,1)S(1)} %copy-done), custom_call_target="tpu_custom_call" | custom-call | flops 84934656 | bytes 1327104 | tf_op jit(solution)/shard_map/inner/pallas_call | solution.py:99
  26.0 1.9 %collective-permute-done.8.far = bf16[64,128]{1,0:T(8,128)(2,1)S(1)} collective-permute-done((bf16[64,128]{1,0:T(8,128)(2,1)S(1)}, bf16[64,128]{1,0:T(8,128)(2,1)S(1)}, u32[]{:S(2)}, u32[]{:S(2)}) %collective-permute-start.8) | collective-permute-done | bytes 16416 | tf_op jit(solution)/shard_map/ppermute | solution.py:415
  27.9 0.0 collective-permute-done.7.near
  27.9 0.0 copy-done.1
  27.9 1.1 %outer.1 = f32[288,1152]{1,0:T(8,128)} custom-call(bf16[64,128]{1,0:T(8,128)(2,1)S(1)} %collective-permute-done.7.near, bf16[64,128]{1,0:T(8,128)(2,1)S(1)} %collective-permute-done.8.far, bf16[144,128]{1,0:T(8,128)(2,1)S(1)} %collective-permute-done.refs_8_.near_pack, bf16[80,128]{1,0:T(8,128)(2,1)S(1)} %collective-permute-done.3.refs_11_.far_edge, ...), custom_call_target="tpu_custom_call" | custom-call | flops 56623104 | bytes 294912 | tf_op jit(solution)/shard_map/outer/pallas_call | solution.py:99
  (5 shorter events, 0.0 us)
Async XLA Ops:
  0.7 7.5 %copy-start.2 = (bf16[4,128,128]{2,1,0:T(8,128)(2,1)S(1)}, bf16[4,128,128]{2,1,0:T(8,128)(2,1)}, u32[]{:S(2)}) copy-start(bf16[4,128,128]{2,1,0:T(8,128)(2,1)} %constant.18.clone.rims) | copy-start | bytes 393220
  2.7 6.5 %collective-permute-start.1 = (bf16[64,128]{1,0:T(8,128)(2,1)S(1)}, bf16[64,128]{1,0:T(8,128)(2,1)S(1)}, u32[]{:S(2)}, u32[]{:S(2)}) collective-permute-start(bf16[64,128]{1,0:T(8,128)(2,1)S(1)} %get-tuple-element.22.refs_7_), channel_id=1, source_target_pairs={{0,2},{1,3},{2,0},{3,1},{4,7},{5,6},{6,5},{7,4},{8,10},{9,11},{10,... | collective-permute-start | bytes 49160 | tf_op jit(solution)/shard_map/ppermute | solution.py:365
  5.4 4.1 %collective-permute-start.3 = (bf16[80,128]{1,0:T(8,128)(2,1)S(1)}, bf16[80,128]{1,0:T(8,128)(2,1)S(1)}, u32[]{:S(2)}, u32[]{:S(2)}) collective-permute-start(bf16[80,128]{1,0:T(8,128)(2,1)S(1)} %get-tuple-element.24), channel_id=1, source_target_pairs={{0,28},{1,29},{2,30},{3,31},{4,8},{5,9},{6,10},{7,11},{8,4},{9,5},... | collective-permute-start | bytes 61448 | tf_op jit(solution)/shard_map/ppermute | solution.py:359
  7.0 3.6 %collective-permute-start = (bf16[144,128]{1,0:T(8,128)(2,1)S(1)}, bf16[144,128]{1,0:T(8,128)(2,1)S(1)}, u32[]{:S(2)}, u32[]{:S(2)}) collective-permute-start(bf16[144,128]{1,0:T(8,128)(2,1)S(1)} %get-tuple-element.23), channel_id=1, source_target_pairs={{0,5},{1,4},{2,7},{3,6},{4,1},{5,0},{6,3},{7,2},{8,13},{9,12},{10,... | collective-permute-start | bytes 110600 | tf_op jit(solution)/shard_map/ppermute | solution.py:360
  8.1 2.4 %copy-start.3 = (s32[288,1152]{1,0:T(8,128)S(1)}, s32[288,1152]{1,0:T(8,128)}, u32[]{:S(2)}) copy-start(s32[288,1152]{1,0:T(8,128)} %refs_1_.1) | copy-start | bytes 3981316
  8.1 2.4 %copy-start.4 = (bf16[9,256,128]{2,1,0:T(8,128)(2,1)S(1)}, bf16[9,256,128]{2,1,0:T(8,128)(2,1)}, u32[]{:S(2)}) copy-start(bf16[9,256,128]{2,1,0:T(8,128)(2,1)} %constant.17.clone.refs_5_) | copy-start | bytes 1769476
  8.1 2.4 %copy-start.5 = (bf16[9,128,256]{2,1,0:T(8,128)(2,1)S(1)}, bf16[9,128,256]{2,1,0:T(8,128)(2,1)}, u32[]{:S(2)}) copy-start(bf16[9,128,256]{2,1,0:T(8,128)(2,1)} %constant.16.clone.refs_4_) | copy-start | bytes 1769476
  9.3 1.2 %collective-permute-start.2 = (bf16[64,128]{1,0:T(8,128)(2,1)S(1)}, bf16[64,128]{1,0:T(8,128)(2,1)S(1)}, u32[]{:S(2)}, u32[]{:S(2)}) collective-permute-start(bf16[64,128]{1,0:T(8,128)(2,1)S(1)} %relay.1), channel_id=1, source_target_pairs={{0,4},{1,5},{2,6},{3,7},{4,0},{5,1},{6,2},{7,3},{8,12},{9,13},{10,... | collective-permute-start | bytes 49160 | tf_op jit(solution)/shard_map/ppermute | solution.py:385
  10.6 14.9 %copy-start = (bf16[128,1152]{1,0:T(8,128)(2,1)S(1)}, bf16[128,1152]{1,0:T(8,128)(2,1)}, u32[]{:S(2)}) copy-start(bf16[128,1152]{1,0:T(8,128)(2,1)} %constant.19.clone.back) | copy-start | bytes 884740
  15.0 12.9 %copy-start.1 = (bf16[4,128,128]{2,1,0:T(8,128)(2,1)S(1)}, bf16[4,128,128]{2,1,0:T(8,128)(2,1)}, u32[]{:S(2)}) copy-start(bf16[4,128,128]{2,1,0:T(8,128)(2,1)} %constant.20.clone.margins) | copy-start | bytes 393220
  15.0 3.8 %collective-permute-start.6 = (bf16[64,128]{1,0:T(8,128)(2,1)S(1)}, bf16[64,128]{1,0:T(8,128)(2,1)S(1)}, u32[]{:S(2)}, u32[]{:S(2)}) collective-permute-start(bf16[64,128]{1,0:T(8,128)(2,1)S(1)} %fields.1.refs_0_), channel_id=1, source_target_pairs={{0,1},{1,0},{2,3},{3,2},{4,7},{5,6},{6,5},{7,4},{8,9},{9,8},{10,11... | collective-permute-start | bytes 49160 | tf_op jit(solution)/shard_map/ppermute | solution.py:411
  15.7 5.5 %collective-permute-start.5 = (bf16[64,128]{1,0:T(8,128)(2,1)S(1)}, bf16[64,128]{1,0:T(8,128)(2,1)S(1)}, u32[]{:S(2)}, u32[]{:S(2)}) collective-permute-start(bf16[64,128]{1,0:T(8,128)(2,1)S(1)} %fields.1.refs_0_), channel_id=1, source_target_pairs={{0,3},{1,2},{2,1},{3,0},{4,6},{5,7},{6,4},{7,5},{8,11},{9,10},{10,... | collective-permute-start | bytes 49160 | tf_op jit(solution)/shard_map/ppermute | solution.py:411
  17.2 4.6 %collective-permute-start.4 = (bf16[64,128]{1,0:T(8,128)(2,1)S(1)}, bf16[64,128]{1,0:T(8,128)(2,1)S(1)}, u32[]{:S(2)}, u32[]{:S(2)}) collective-permute-start(bf16[64,128]{1,0:T(8,128)(2,1)S(1)} %fields.1.refs_0_), channel_id=1, source_target_pairs={{0,2},{1,3},{2,0},{3,1},{4,5},{5,4},{6,7},{7,6},{8,10},{9,11},{10,... | collective-permute-start | bytes 49160 | tf_op jit(solution)/shard_map/ppermute | solution.py:411
  21.9 6.0 %collective-permute-start.8 = (bf16[64,128]{1,0:T(8,128)(2,1)S(1)}, bf16[64,128]{1,0:T(8,128)(2,1)S(1)}, u32[]{:S(2)}, u32[]{:S(2)}) collective-permute-start(bf16[64,128]{1,0:T(8,128)(2,1)S(1)} %total.1.own), channel_id=1, source_target_pairs={{4,8},{8,4},{12,16},{16,12},{20,24},{24,20},{5,9},{9,5},{13,17},{1... | collective-permute-start | bytes 49160 | tf_op jit(solution)/shard_map/ppermute | solution.py:415
  23.8 4.0 %collective-permute-start.7 = (bf16[64,128]{1,0:T(8,128)(2,1)S(1)}, bf16[64,128]{1,0:T(8,128)(2,1)S(1)}, u32[]{:S(2)}, u32[]{:S(2)}) collective-permute-start(bf16[64,128]{1,0:T(8,128)(2,1)S(1)} %total.1.own), channel_id=1, source_target_pairs={{0,4},{4,0},{8,12},{12,8},{16,20},{20,16},{24,28},{28,24},{1,5},{5... | collective-permute-start | bytes 49160 | tf_op jit(solution)/shard_map/ppermute | solution.py:413

commit v4 on v2

--- a/solution.py
+++ b/solution.py
@@ -108,49 +108,43 @@
     )(*args)
 
 
-def edges_body(
-    mask, mid, mid_t, real, imag, weight, flags, mate, other, side, held, tall, table, sides_out, pair, marks, sems
-):
-    odd = lax.rem(lax.axis_index("tile"), 2) == 1
+def pack_body(real, imag, weight, flags, side, sides, pair, marks, sems):
+    copies = [
+        pltpu.make_async_copy(real.at[0], pair.at[0], sems.at[0]),
+        pltpu.make_async_copy(imag.at[0], pair.at[1], sems.at[1]),
+        pltpu.make_async_copy(flags, marks, sems.at[2]),
+    ]
+    for copy in copies:
+        copy.start()
+    for copy in copies:
+        copy.wait()
+    scale = jnp.sqrt(jnp.full((KF, KF), 2.0 * weight[0], F32)) * (1.0 / (NE * KF))
+    side[...] = jnp.concatenate([pair[0] * scale, pair[1] * scale], 1).astype(BF16)
+    row = lax.broadcasted_iota(jnp.int32, (MARKS, LANES), 0)
+    sides[...] = jnp.where(row == 0, marks[0, 0].astype(F32), marks[0, 1].astype(F32)).astype(BF16)
+
+
+def edges_body(mask, mid_t, side, sides, mate, other, table, strips, sems):
     copies = [
         pltpu.make_async_copy(mid_t, table, sems.at[0]),
-        pltpu.make_async_copy(mask.at[:, :LANES], held.at[:, :LANES], sems.at[1]),
-        pltpu.make_async_copy(mask.at[:, N - LANES :], held.at[:, N - LANES :], sems.at[2]),
-        pltpu.make_async_copy(real.at[0], pair.at[0], sems.at[3]),
-        pltpu.make_async_copy(imag.at[0], pair.at[1], sems.at[4]),
-        pltpu.make_async_copy(flags, marks, sems.at[5]),
+        pltpu.make_async_copy(mask.at[:, :LANES], strips.at[:, :LANES], sems.at[1]),
+        pltpu.make_async_copy(mask.at[:, N - LANES :], strips.at[:, LANES:], sems.at[2]),
     ]
-    inner = pltpu.make_async_copy(
-        mask.at[:, LANES : N - LANES], held.at[:, LANES : N - LANES], sems.at[6]
-    )
-    columns = pltpu.make_async_copy(mid, tall, sems.at[7])
     for copy in copies:
         copy.start()
-    inner.start()
-    columns.start()
-    for copy in copies[3:]:
+    odd = lax.rem(lax.axis_index("tile"), 2) == 1
+    mate[EDGE : 2 * EDGE, :] = side[...]
+    mate[2 * EDGE :, :] = sides[...]
+    other[EDGE:, :] = sides[...]
+    for copy in copies:
         copy.wait()
-    scale = jnp.sqrt(jnp.full((KF, KF), 2.0 * weight[0], F32)) * (1.0 / (NE * KF))
-    kernel = jnp.concatenate([pair[0] * scale, pair[1] * scale], 1).astype(BF16)
-    row = lax.broadcasted_iota(jnp.int32, (16, LANES), 0)
-    sides = jnp.where(row == 0, marks[0, 0].astype(F32), marks[0, 1].astype(F32)).astype(BF16)
-    side[...] = kernel
-    mate[EDGE : 2 * EDGE, :] = kernel
-    mate[2 * EDGE :, :] = sides
-    other[EDGE:, :] = sides
-    sides_out[...] = sides
-    for copy in copies[:3]:
-        copy.wait()
-    strips = jnp.concatenate([held[:, :LANES], held[:, N - LANES :]], 1)
-    both = dot(table[...], strips)
+    both = dot(table[...], strips[...])
     left = in_left_half((KF, LANES))
     first, last = both[:, :LANES], both[:, LANES:]
     first = jnp.where(left, first[:KF], swap_halves(first[KF:]))
     last = jnp.where(left, swap_halves(last[:KF]), last[KF:])
     mate[:EDGE, :] = jnp.where(odd, first, last).astype(BF16)
     other[:EDGE, :] = jnp.where(odd, last, first).astype(BF16)
-    inner.wait()
-    columns.wait()
 
 
 def middle_body(row_count, mask, mid, mid_t, marks, rims, out, tables, rows_t):
@@ -315,29 +309,32 @@
     hbm = pl.BlockSpec(memory_space=pltpu.HBM)
     small = jax.ShapeDtypeStruct((KF, PAIR), BF16)
 
-    mate, other, side, held, mid, mid_t, marks = call(
+    side, marks = call(
+        pack_body,
+        "pack",
+        (pltpu.VMEM((KF, PAIR), BF16), pltpu.VMEM((MARKS, LANES), BF16)),
+        (far_off(kernel_real), far_off(kernel_imag), eigen_weights, far_off(orientation)),
+        [hbm, hbm, smem, hbm],
+        scratch=[
+            pltpu.VMEM((2, KF, KF), F32),
+            pltpu.SMEM((1, 2), jnp.int32),
+            pltpu.SemaphoreType.DMA((3,)),
+        ],
+        flops=8 * KF * KF,
+        moved=8 * KF * KF,
+    )
+    held = pltpu.with_memory_space_constraint(mask_pixels, pltpu.VMEM)
+    mate, other, mid_t = call(
         edges_body,
         "edges",
         (
             pltpu.VMEM((2 * EDGE + MARKS, LANES), BF16),
             pltpu.VMEM((EDGE + MARKS, LANES), BF16),
-            pltpu.VMEM((KF, PAIR), BF16),
-            pltpu.VMEM((N, N), BF16),
-            pltpu.VMEM((N, PAIR), BF16),
             pltpu.VMEM((PAIR, N), BF16),
-            pltpu.VMEM((MARKS, LANES), BF16),
         ),
-        (
-            *(far_off(one) for one in (mask_pixels, mid, mid_t, kernel_real, kernel_imag)),
-            eigen_weights,
-            far_off(orientation),
-        ),
-        [hbm] * 5 + [smem, hbm],
-        scratch=[
-            pltpu.VMEM((2, KF, KF), F32),
-            pltpu.SMEM((1, 2), jnp.int32),
-            pltpu.SemaphoreType.DMA((8,)),
-        ],
+        (far_off(mask_pixels), far_off(mid_t), side, marks),
+        [hbm, hbm, vmem, vmem],
+        scratch=[pltpu.VMEM((N, 2 * LANES), BF16), pltpu.SemaphoreType.DMA((3,))],
         flops=2 * N * LANES * PAIR * 2,
         moved=N * LANES * 4,
     )

time: 28.9 us -> 30.4 us (1.052)
  the two profiles are of different devices: /device:TPU:4 before, /device:TPU:12 now
where the time goes in v4:
time: 30.4 us; the launch traced here: 30.2 us
  starting transfers between devices  11.4 us (38%)
  Pallas kernels  9.69 us (32%)
  waiting for transfers between devices  7.44 us (24%)
  local copies, waits for them, and re-layouts  0.94 us (3%)
  between operations  0.75 us (2%)
    pallas_call x8, Pallas kernels, call(): pl.pallas_call(body, name=name, out_shape=outs, in_specs=specs, out_specs...  9.69 us
    ppermute x3, starting transfers between devices, per_device(): parts.append(lax.ppermute(part, both, pairs))  3.85 us
    ppermute x3, waiting for transfers between devices, per_device(): parts.append(lax.ppermute(part, both, pairs))  3.73 us
    ppermute x1, waiting for transfers between devices, per_device(): far = lax.ppermute(own, 'tile', [(t, other_side(t)) for t in inner])  2.86 us
    ppermute x1, starting transfers between devices, per_device(): kernels = [lax.ppermute(side, both, pairs)]  2.65 us
    ppermute x1, starting transfers between devices, per_device(): far = lax.ppermute(own, 'tile', [(t, other_side(t)) for t in inner])  1.92 us
    ppermute x1, starting transfers between devices, per_device(): near_pack = lax.ppermute(mate, both, swapped(chip_mate, 1))  1.65 us
    unnamed x16, local copies, waits for them, and re-layouts  0.94 us
  transfers between devices with their start and end apart: 9, of which 4 were waited for; matrix products, arithmetic and copies ran while one was open for 0% of the time, Pallas kernels for 11%

profile of v4, /device:TPU:12, one launch (start us, length us, event | category | flops | bytes accessed | tf_op | source)
XLA Modules:
  0.0 30.2 jit_solution(17319197286932159538)
XLA Ops:
  0.7 0.9 %pack.1 = (bf16[64,128]{1,0:T(8,128)(2,1)S(1)}, bf16[16,128]{1,0:T(8,128)(2,1)S(1)}) custom-call(f32[1,64,64]{2,1,0:T(8,128)} %real.1, f32[1,64,64]{2,1,0:T(8,128)} %imag.1, f32[1]{0:T(128)S(6)} %copy.14.weight, s32[1,2]{1,0:T(1,128)} %flags.1), custom_call_target="tpu_custom_call" | custom-call | flops 32768 | bytes 32768 | tf_op jit(solution)/shard_map/pack/pallas_call | solution.py:99
  1.6 2.7 %collective-permute-start.1 = (bf16[64,128]{1,0:T(8,128)(2,1)S(1)}, bf16[64,128]{1,0:T(8,128)(2,1)S(1)}, u32[]{:S(2)}, u32[]{:S(2)}) collective-permute-start(bf16[64,128]{1,0:T(8,128)(2,1)S(1)} %get-tuple-element.13.side.refs_7_), channel_id=1, source_target_pairs={{0,2},{1,3},{2,0},{3,1},{4,7},{5,6},{6,5},{7,4},{8,10},{9,11},{10,... | collective-permute-start | bytes 49160 | tf_op jit(solution)/shard_map/ppermute | solution.py:362
  4.2 1.7 %edges.1 = (bf16[144,128]{1,0:T(8,128)(2,1)S(1)}, bf16[80,128]{1,0:T(8,128)(2,1)S(1)}, bf16[128,1152]{1,0:T(8,128)(2,1)S(1)}) custom-call(bf16[1152,1152]{1,0:T(8,128)(2,1)} %mask.3, bf16[128,1152]{1,0:T(8,128)(2,1)} %constant.15.clone.mid_t, bf16[64,128]{1,0:T(8,128)(2,1)S(1)} %get-tuple-element.13.side.refs_7_, ...), custom_call_target="tpu_custom_call" | custom-call | flops 75497472 | bytes 589824 | tf_op jit(solution)/shard_map/edges/pallas_call | solution.py:99
  5.9 0.1 collective-permute-start.3
  6.0 1.6 %collective-permute-start = (bf16[144,128]{1,0:T(8,128)(2,1)S(1)}, bf16[144,128]{1,0:T(8,128)(2,1)S(1)}, u32[]{:S(2)}, u32[]{:S(2)}) collective-permute-start(bf16[144,128]{1,0:T(8,128)(2,1)S(1)} %get-tuple-element.19), channel_id=1, source_target_pairs={{0,5},{1,4},{2,7},{3,6},{4,1},{5,0},{6,3},{7,2},{8,13},{9,12},{10,... | collective-permute-start | bytes 110600 | tf_op jit(solution)/shard_map/ppermute | solution.py:357
  7.6 0.0 copy-done
  7.6 0.0 copy-done.1
  7.6 0.9 %copy-done.4 = bf16[4,128,128]{2,1,0:T(8,128)(2,1)S(1)} copy-done((bf16[4,128,128]{2,1,0:T(8,128)(2,1)S(1)}, bf16[4,128,128]{2,1,0:T(8,128)(2,1)}, u32[]{:S(2)}) %copy-start.4) | copy-done | bytes 131096
  8.5 1.1 %middle.1 = (f32[128,128]{1,0:T(8,128)S(1)}, bf16[2,128,128]{2,1,0:T(8,128)(2,1)S(1)}, bf16[128,288]{1,0:T(8,128)(2,1)S(1)}) custom-call(bf16[1152,1152]{1,0:T(8,128)(2,1)S(1)} %copy-done, bf16[1152,128]{1,0:T(8,128)(2,1)S(1)} %copy-done.1, bf16[128,1152]{1,0:T(8,128)(2,1)S(1)} %get-tuple-element.15.mid_t, ...), custom_call_target="tpu_custom_call" | custom-call | flops 679477248 | bytes 2654208 | tf_op jit(solution)/shard_map/middle/pallas_call | solution.py:99
  9.6 0.0 collective-permute-done.1.value.refs_9_
  9.6 0.6 %collective-permute-start.2 = (bf16[64,128]{1,0:T(8,128)(2,1)S(1)}, bf16[64,128]{1,0:T(8,128)(2,1)S(1)}, u32[]{:S(2)}, u32[]{:S(2)}) collective-permute-start(bf16[64,128]{1,0:T(8,128)(2,1)S(1)} %relay.1), channel_id=1, source_target_pairs={{0,4},{1,5},{2,6},{3,7},{4,0},{5,1},{6,2},{7,3},{8,12},{9,13},{10,... | collective-permute-start | bytes 49160 | tf_op jit(solution)/shard_map/ppermute | solution.py:382
  10.2 0.0 collective-permute-done.3.refs_11_.far_edge
  10.2 0.8 %collective-permute-done.2.refs_10_ = bf16[64,128]{1,0:T(8,128)(2,1)S(1)} collective-permute-done((bf16[64,128]{1,0:T(8,128)(2,1)S(1)}, bf16[64,128]{1,0:T(8,128)(2,1)S(1)}, u32[]{:S(2)}, u32[]{:S(2)}) %collective-permute-start.2) | collective-permute-done | bytes 16416 | tf_op jit(solution)/shard_map/ppermute | solution.py:382
  11.1 0.0 collective-permute-done.refs_8_.near_pack
  11.1 0.0 copy-done.5
  11.1 0.0 copy-done.6
  11.1 0.0 copy-done.7
  11.1 0.0 copy-start.2
  11.1 4.4 %fields.1.refs_0_ = bf16[64,128]{1,0:T(8,128)(2,1)S(1)} custom-call(f32[128,128]{1,0:T(8,128)S(1)} %get-tuple-element.16.ready.refs_0_, s32[288,1152]{1,0:T(8,128)S(1)} %copy-done.5, bf16[1152,128]{1,0:T(8,128)(2,1)S(1)} %copy-done.1, bf16[128,288]{1,0:T(8,128)(2,1)S(1)} %get-tuple-element.17.refs_3_, bf16[9,128,256]{2,1,0:T(8,128)(2,1)S(1)} %copy-done.7, ...), custom_call_target="tpu_custom_call" | custom-call | flops 1358954496 | bytes 1327104 | tf_op jit(solution)/shard_map/fields/pallas_call | solution.py:99
  15.5 0.0 copy-start.3
  15.5 0.4 %collective-permute-start.6 = (bf16[64,128]{1,0:T(8,128)(2,1)S(1)}, bf16[64,128]{1,0:T(8,128)(2,1)S(1)}, u32[]{:S(2)}, u32[]{:S(2)}) collective-permute-start(bf16[64,128]{1,0:T(8,128)(2,1)S(1)} %fields.1.refs_0_), channel_id=1, source_target_pairs={{0,3},{1,2},{2,1},{3,0},{4,5},{5,4},{6,7},{7,6},{8,11},{9,10},{10,... | collective-permute-start | bytes 49160 | tf_op jit(solution)/shard_map/ppermute | solution.py:408
  15.9 3.5 %collective-permute-start.5 = (bf16[64,128]{1,0:T(8,128)(2,1)S(1)}, bf16[64,128]{1,0:T(8,128)(2,1)S(1)}, u32[]{:S(2)}, u32[]{:S(2)}) collective-permute-start(bf16[64,128]{1,0:T(8,128)(2,1)S(1)} %fields.1.refs_0_), channel_id=1, source_target_pairs={{0,2},{1,3},{2,0},{3,1},{4,7},{5,6},{6,5},{7,4},{8,10},{9,11},{10,... | collective-permute-start | bytes 49160 | tf_op jit(solution)/shard_map/ppermute | solution.py:408
  19.3 0.0 collective-permute-start.4
  19.4 0.0 collective-permute-done.6.refs_3_
  19.4 1.9 %collective-permute-done.5.refs_2_ = bf16[64,128]{1,0:T(8,128)(2,1)S(1)} collective-permute-done((bf16[64,128]{1,0:T(8,128)(2,1)S(1)}, bf16[64,128]{1,0:T(8,128)(2,1)S(1)}, u32[]{:S(2)}, u32[]{:S(2)}) %collective-permute-start.5) | collective-permute-done | bytes 16416 | tf_op jit(solution)/shard_map/ppermute | solution.py:408
  21.3 1.8 %collective-permute-done.4.refs_1_ = bf16[64,128]{1,0:T(8,128)(2,1)S(1)} collective-permute-done((bf16[64,128]{1,0:T(8,128)(2,1)S(1)}, bf16[64,128]{1,0:T(8,128)(2,1)S(1)}, u32[]{:S(2)}, u32[]{:S(2)}) %collective-permute-start.4) | collective-permute-done | bytes 16416 | tf_op jit(solution)/shard_map/ppermute | solution.py:408
  23.1 1.9 %collective-permute-start.8 = (bf16[64,128]{1,0:T(8,128)(2,1)S(1)}, bf16[64,128]{1,0:T(8,128)(2,1)S(1)}, u32[]{:S(2)}, u32[]{:S(2)}) collective-permute-start(bf16[64,128]{1,0:T(8,128)(2,1)S(1)} %total.1.own), channel_id=1, source_target_pairs={{4,8},{8,4},{12,16},{16,12},{20,24},{24,20},{5,9},{9,5},{13,17},{1... | collective-permute-start | bytes 49160 | tf_op jit(solution)/shard_map/ppermute | solution.py:412
  25.0 0.6 %collective-permute-start.7 = (bf16[64,128]{1,0:T(8,128)(2,1)S(1)}, bf16[64,128]{1,0:T(8,128)(2,1)S(1)}, u32[]{:S(2)}, u32[]{:S(2)}) collective-permute-start(bf16[64,128]{1,0:T(8,128)(2,1)S(1)} %total.1.own), channel_id=1, source_target_pairs={{0,4},{4,0},{8,12},{12,8},{16,20},{20,16},{24,28},{28,24},{1,5},{5... | collective-permute-start | bytes 49160 | tf_op jit(solution)/shard_map/ppermute | solution.py:410
  25.7 0.5 %inner.1.begun = f32[288,1152]{1,0:T(8,128)S(1)} custom-call(bf16[64,128]{1,0:T(8,128)(2,1)S(1)} %total.1.own, bf16[1152,128]{1,0:T(8,128)(2,1)S(1)} %copy-done.1, bf16[128,1152]{1,0:T(8,128)(2,1)S(1)} %copy-done.2), custom_call_target="tpu_custom_call" | custom-call | flops 84934656 | bytes 1327104 | tf_op jit(solution)/shard_map/inner/pallas_call | solution.py:99
  26.2 2.9 %collective-permute-done.8.far = bf16[64,128]{1,0:T(8,128)(2,1)S(1)} collective-permute-done((bf16[64,128]{1,0:T(8,128)(2,1)S(1)}, bf16[64,128]{1,0:T(8,128)(2,1)S(1)}, u32[]{:S(2)}, u32[]{:S(2)}) %collective-permute-start.8) | collective-permute-done | bytes 16416 | tf_op jit(solution)/shard_map/ppermute | solution.py:412
  29.1 0.0 collective-permute-done.7.near
  29.1 1.1 %outer.1 = f32[288,1152]{1,0:T(8,128)} custom-call(bf16[64,128]{1,0:T(8,128)(2,1)S(1)} %collective-permute-done.7.near, bf16[64,128]{1,0:T(8,128)(2,1)S(1)} %collective-permute-done.8.far, bf16[144,128]{1,0:T(8,128)(2,1)S(1)} %collective-permute-done.refs_8_.near_pack, bf16[80,128]{1,0:T(8,128)(2,1)S(1)} %collective-permute-done.3.refs_11_.far_edge, ...), custom_call_target="tpu_custom_call" | custom-call | flops 56623104 | bytes 294912 | tf_op jit(solution)/shard_map/outer/pallas_call | solution.py:99
  (10 shorter events, 0.0 us)
Async XLA Ops:
  1.6 8.1 %collective-permute-start.1 = (bf16[64,128]{1,0:T(8,128)(2,1)S(1)}, bf16[64,128]{1,0:T(8,128)(2,1)S(1)}, u32[]{:S(2)}, u32[]{:S(2)}) collective-permute-start(bf16[64,128]{1,0:T(8,128)(2,1)S(1)} %get-tuple-element.13.side.refs_7_), channel_id=1, source_target_pairs={{0,2},{1,3},{2,0},{3,1},{4,7},{5,6},{6,5},{7,4},{8,10},{9,11},{10,... | collective-permute-start | bytes 49160 | tf_op jit(solution)/shard_map/ppermute | solution.py:362
  4.2 3.4 %copy-start = (bf16[1152,1152]{1,0:T(8,128)(2,1)S(1)}, bf16[1152,1152]{1,0:T(8,128)(2,1)}, u32[]{:S(2)}) copy-start(bf16[1152,1152]{1,0:T(8,128)(2,1)} %mask.3) | copy-start | bytes 7962628
  4.2 3.4 %copy-start.1 = (bf16[1152,128]{1,0:T(8,128)(2,1)S(1)}, bf16[1152,128]{1,0:T(8,128)(2,1)}, u32[]{:S(2)}) copy-start(bf16[1152,128]{1,0:T(8,128)(2,1)} %constant.14.clone.mid.refs_2_) | copy-start | bytes 884740
  5.9 4.3 %collective-permute-start.3 = (bf16[80,128]{1,0:T(8,128)(2,1)S(1)}, bf16[80,128]{1,0:T(8,128)(2,1)S(1)}, u32[]{:S(2)}, u32[]{:S(2)}) collective-permute-start(bf16[80,128]{1,0:T(8,128)(2,1)S(1)} %get-tuple-element.20), channel_id=1, source_target_pairs={{0,28},{1,29},{2,30},{3,31},{4,8},{5,9},{6,10},{7,11},{8,4},{9,5},... | collective-permute-start | bytes 61448 | tf_op jit(solution)/shard_map/ppermute | solution.py:356
  6.0 5.1 %collective-permute-start = (bf16[144,128]{1,0:T(8,128)(2,1)S(1)}, bf16[144,128]{1,0:T(8,128)(2,1)S(1)}, u32[]{:S(2)}, u32[]{:S(2)}) collective-permute-start(bf16[144,128]{1,0:T(8,128)(2,1)S(1)} %get-tuple-element.19), channel_id=1, source_target_pairs={{0,5},{1,4},{2,7},{3,6},{4,1},{5,0},{6,3},{7,2},{8,13},{9,12},{10,... | collective-permute-start | bytes 110600 | tf_op jit(solution)/shard_map/ppermute | solution.py:357
  7.6 0.9 %copy-start.4 = (bf16[4,128,128]{2,1,0:T(8,128)(2,1)S(1)}, bf16[4,128,128]{2,1,0:T(8,128)(2,1)}, u32[]{:S(2)}) copy-start(bf16[4,128,128]{2,1,0:T(8,128)(2,1)} %constant.18.clone.rims) | copy-start | bytes 393220
  8.5 2.5 %copy-start.5 = (s32[288,1152]{1,0:T(8,128)S(1)}, s32[288,1152]{1,0:T(8,128)}, u32[]{:S(2)}) copy-start(s32[288,1152]{1,0:T(8,128)} %refs_1_.1) | copy-start | bytes 3981316
  8.5 2.5 %copy-start.6 = (bf16[9,256,128]{2,1,0:T(8,128)(2,1)S(1)}, bf16[9,256,128]{2,1,0:T(8,128)(2,1)}, u32[]{:S(2)}) copy-start(bf16[9,256,128]{2,1,0:T(8,128)(2,1)} %constant.17.clone.refs_5_) | copy-start | bytes 1769476
  8.5 2.5 %copy-start.7 = (bf16[9,128,256]{2,1,0:T(8,128)(2,1)S(1)}, bf16[9,128,256]{2,1,0:T(8,128)(2,1)}, u32[]{:S(2)}) copy-start(bf16[9,128,256]{2,1,0:T(8,128)(2,1)} %constant.16.clone.refs_4_) | copy-start | bytes 1769476
  9.6 1.4 %collective-permute-start.2 = (bf16[64,128]{1,0:T(8,128)(2,1)S(1)}, bf16[64,128]{1,0:T(8,128)(2,1)S(1)}, u32[]{:S(2)}, u32[]{:S(2)}) collective-permute-start(bf16[64,128]{1,0:T(8,128)(2,1)S(1)} %relay.1), channel_id=1, source_target_pairs={{0,4},{1,5},{2,6},{3,7},{4,0},{5,1},{6,2},{7,3},{8,12},{9,13},{10,... | collective-permute-start | bytes 49160 | tf_op jit(solution)/shard_map/ppermute | solution.py:382
  11.1 14.6 %copy-start.2 = (bf16[128,1152]{1,0:T(8,128)(2,1)S(1)}, bf16[128,1152]{1,0:T(8,128)(2,1)}, u32[]{:S(2)}) copy-start(bf16[128,1152]{1,0:T(8,128)(2,1)} %constant.19.clone.back) | copy-start | bytes 884740
  15.5 13.6 %copy-start.3 = (bf16[4,128,128]{2,1,0:T(8,128)(2,1)S(1)}, bf16[4,128,128]{2,1,0:T(8,128)(2,1)}, u32[]{:S(2)}) copy-start(bf16[4,128,128]{2,1,0:T(8,128)(2,1)} %constant.20.clone.margins) | copy-start | bytes 393220
  15.5 3.9 %collective-permute-start.6 = (bf16[64,128]{1,0:T(8,128)(2,1)S(1)}, bf16[64,128]{1,0:T(8,128)(2,1)S(1)}, u32[]{:S(2)}, u32[]{:S(2)}) collective-permute-start(bf16[64,128]{1,0:T(8,128)(2,1)S(1)} %fields.1.refs_0_), channel_id=1, source_target_pairs={{0,3},{1,2},{2,1},{3,0},{4,5},{5,4},{6,7},{7,6},{8,11},{9,10},{10,... | collective-permute-start | bytes 49160 | tf_op jit(solution)/shard_map/ppermute | solution.py:408
  15.9 5.4 %collective-permute-start.5 = (bf16[64,128]{1,0:T(8,128)(2,1)S(1)}, bf16[64,128]{1,0:T(8,128)(2,1)S(1)}, u32[]{:S(2)}, u32[]{:S(2)}) collective-permute-start(bf16[64,128]{1,0:T(8,128)(2,1)S(1)} %fields.1.refs_0_), channel_id=1, source_target_pairs={{0,2},{1,3},{2,0},{3,1},{4,7},{5,6},{6,5},{7,4},{8,10},{9,11},{10,... | collective-permute-start | bytes 49160 | tf_op jit(solution)/shard_map/ppermute | solution.py:408
  19.3 3.7 %collective-permute-start.4 = (bf16[64,128]{1,0:T(8,128)(2,1)S(1)}, bf16[64,128]{1,0:T(8,128)(2,1)S(1)}, u32[]{:S(2)}, u32[]{:S(2)}) collective-permute-start(bf16[64,128]{1,0:T(8,128)(2,1)S(1)} %fields.1.refs_0_), channel_id=1, source_target_pairs={{0,1},{1,0},{2,3},{3,2},{4,6},{5,7},{6,4},{7,5},{8,9},{9,8},{10,11... | collective-permute-start | bytes 49160 | tf_op jit(solution)/shard_map/ppermute | solution.py:408
  23.1 6.0 %collective-permute-start.8 = (bf16[64,128]{1,0:T(8,128)(2,1)S(1)}, bf16[64,128]{1,0:T(8,128)(2,1)S(1)}, u32[]{:S(2)}, u32[]{:S(2)}) collective-permute-start(bf16[64,128]{1,0:T(8,128)(2,1)S(1)} %total.1.own), channel_id=1, source_target_pairs={{4,8},{8,4},{12,16},{16,12},{20,24},{24,20},{5,9},{9,5},{13,17},{1... | collective-permute-start | bytes 49160 | tf_op jit(solution)/shard_map/ppermute | solution.py:412
  25.0 4.0 %collective-permute-start.7 = (bf16[64,128]{1,0:T(8,128)(2,1)S(1)}, bf16[64,128]{1,0:T(8,128)(2,1)S(1)}, u32[]{:S(2)}, u32[]{:S(2)}) collective-permute-start(bf16[64,128]{1,0:T(8,128)(2,1)S(1)} %total.1.own), channel_id=1, source_target_pairs={{0,4},{4,0},{8,12},{12,8},{16,20},{20,16},{24,28},{28,24},{1,5},{5... | collective-permute-start | bytes 49160 | tf_op jit(solution)/shard_map/ppermute | solution.py:410

commit v5 on v2

--- a/solution.py
+++ b/solution.py
@@ -109,24 +109,22 @@
 
 
 def edges_body(
-    mask, mid, mid_t, real, imag, weight, flags, mate, other, side, held, tall, table, sides_out, pair, marks, sems
+    mask, mid, mid_t, rims, real, imag, weight, flags, mate, other, side, tall, table, sides_out, rims_out, strips, pair, marks, sems
 ):
     odd = lax.rem(lax.axis_index("tile"), 2) == 1
     copies = [
         pltpu.make_async_copy(mid_t, table, sems.at[0]),
-        pltpu.make_async_copy(mask.at[:, :LANES], held.at[:, :LANES], sems.at[1]),
-        pltpu.make_async_copy(mask.at[:, N - LANES :], held.at[:, N - LANES :], sems.at[2]),
+        pltpu.make_async_copy(mask.at[:, :LANES], strips.at[:, :LANES], sems.at[1]),
+        pltpu.make_async_copy(mask.at[:, N - LANES :], strips.at[:, LANES:], sems.at[2]),
         pltpu.make_async_copy(real.at[0], pair.at[0], sems.at[3]),
         pltpu.make_async_copy(imag.at[0], pair.at[1], sems.at[4]),
         pltpu.make_async_copy(flags, marks, sems.at[5]),
     ]
-    inner = pltpu.make_async_copy(
-        mask.at[:, LANES : N - LANES], held.at[:, LANES : N - LANES], sems.at[6]
-    )
+    turned = pltpu.make_async_copy(rims, rims_out, sems.at[6])
     columns = pltpu.make_async_copy(mid, tall, sems.at[7])
     for copy in copies:
         copy.start()
-    inner.start()
+    turned.start()
     columns.start()
     for copy in copies[3:]:
         copy.wait()
@@ -141,15 +139,14 @@
     sides_out[...] = sides
     for copy in copies[:3]:
         copy.wait()
-    strips = jnp.concatenate([held[:, :LANES], held[:, N - LANES :]], 1)
-    both = dot(table[...], strips)
+    both = dot(table[...], strips[...])
     left = in_left_half((KF, LANES))
     first, last = both[:, :LANES], both[:, LANES:]
     first = jnp.where(left, first[:KF], swap_halves(first[KF:]))
     last = jnp.where(left, swap_halves(last[:KF]), last[KF:])
     mate[:EDGE, :] = jnp.where(odd, first, last).astype(BF16)
     other[:EDGE, :] = jnp.where(odd, last, first).astype(BF16)
-    inner.wait()
+    turned.wait()
     columns.wait()
 
 
@@ -315,25 +312,26 @@
     hbm = pl.BlockSpec(memory_space=pltpu.HBM)
     small = jax.ShapeDtypeStruct((KF, PAIR), BF16)
 
-    mate, other, side, held, mid, mid_t, marks = call(
+    mate, other, side, mid, mid_t, marks, rims = call(
         edges_body,
         "edges",
         (
             pltpu.VMEM((2 * EDGE + MARKS, LANES), BF16),
             pltpu.VMEM((EDGE + MARKS, LANES), BF16),
             pltpu.VMEM((KF, PAIR), BF16),
-            pltpu.VMEM((N, N), BF16),
             pltpu.VMEM((N, PAIR), BF16),
             pltpu.VMEM((PAIR, N), BF16),
             pltpu.VMEM((MARKS, LANES), BF16),
+            pltpu.VMEM((4, LANES, PAIR), BF16),
         ),
         (
-            *(far_off(one) for one in (mask_pixels, mid, mid_t, kernel_real, kernel_imag)),
+            *(far_off(one) for one in (mask_pixels, mid, mid_t, rims, kernel_real, kernel_imag)),
             eigen_weights,
             far_off(orientation),
         ),
-        [hbm] * 5 + [smem, hbm],
+        [hbm] * 6 + [smem, hbm],
         scratch=[
+            pltpu.VMEM((N, 2 * LANES), BF16),
             pltpu.VMEM((2, KF, KF), F32),
             pltpu.SMEM((1, 2), jnp.int32),
             pltpu.SemaphoreType.DMA((8,)),
@@ -374,7 +372,7 @@
             pltpu.VMEM((2, PAIR, PAIR), BF16),
             pltpu.VMEM((PAIR, row_count), BF16),
         ),
-        (held, mid, mid_t, marks, rims),
+        (pltpu.with_memory_space_constraint(mask_pixels, pltpu.VMEM), mid, mid_t, marks, rims),
         [vmem] * 5,
         flops=4 * N * N * PAIR,
         moved=N * N * 2,

time: 28.9 us -> 28.5 us (0.986)
  Pallas kernels: 9.18 us -> 8.85 us
    pallas_call x7, Pallas kernels: 9.18 us -> 8.85 us  [call(): pl.pallas_call(body, name=name, out_shape=outs, in_specs=specs, out_specs...]
where the time goes in v5:
time: 28.5 us; the launch traced here: 28.3 us
  starting transfers between devices  13.6 us (48%)
  Pallas kernels  8.85 us (31%)
  waiting for transfers between devices  5.06 us (18%)
  between operations  0.75 us (3%)
    pallas_call x7, Pallas kernels, call(): pl.pallas_call(body, name=name, out_shape=outs, in_specs=specs, out_specs...  8.85 us
    ppermute x3, starting transfers between devices, per_device(): parts.append(lax.ppermute(part, both, pairs))  4.45 us
    ppermute x1, starting transfers between devices, per_device(): kernels = [lax.ppermute(side, both, pairs)]  2.65 us
    ppermute x1, starting transfers between devices, per_device(): far = lax.ppermute(own, 'tile', [(t, other_side(t)) for t in inner])  2.29 us
    ppermute x3, waiting for transfers between devices, per_device(): parts.append(lax.ppermute(part, both, pairs))  2.01 us
    ppermute x1, waiting for transfers between devices, per_device(): far = lax.ppermute(own, 'tile', [(t, other_side(t)) for t in inner])  1.83 us
    ppermute x1, starting transfers between devices, per_device(): far_edge = lax.ppermute(other, both, swapped(other_side, 0))  1.61 us
    ppermute x1, starting transfers between devices, per_device(): near = lax.ppermute(own, 'tile', [(t, chip_mate(t)) for t in range(tiles)])  1.31 us
  transfers between devices with their start and end apart: 9, of which 5 were waited for; matrix products, arithmetic and copies ran while one was open for 0% of the time, Pallas kernels for 6%

profile of v5, /device:TPU:4, one launch (start us, length us, event | category | flops | bytes accessed | tf_op | source)
XLA Modules:
  0.0 28.3 jit_solution(9434170181473145956)
XLA Ops:
  0.7 0.0 copy-start
  0.7 1.7 %edges.1 = (bf16[144,128]{1,0:T(8,128)(2,1)S(1)}, bf16[80,128]{1,0:T(8,128)(2,1)S(1)}, bf16[64,128]{1,0:T(8,128)(2,1)S(1)}, bf16[1152,128]{1,0:T(8,128)(2,1)S(1)...) custom-call(bf16[1152,1152]{1,0:T(8,128)(2,1)} %mask.3, ...), custom_call_target="tpu_custom_call" | custom-call | flops 75497472 | bytes 589824 | tf_op jit(solution)/shard_map/edges/pallas_call | solution.py:99
  2.4 2.7 %collective-permute-start.1 = (bf16[64,128]{1,0:T(8,128)(2,1)S(1)}, bf16[64,128]{1,0:T(8,128)(2,1)S(1)}, u32[]{:S(2)}, u32[]{:S(2)}) collective-permute-start(bf16[64,128]{1,0:T(8,128)(2,1)S(1)} %get-tuple-element.22.refs_7_), channel_id=1, source_target_pairs={{0,2},{1,3},{2,0},{3,1},{4,7},{5,6},{6,5},{7,4},{8,10},{9,11},{10,... | collective-permute-start | bytes 49160 | tf_op jit(solution)/shard_map/ppermute | solution.py:363
  5.0 1.6 %collective-permute-start.3 = (bf16[80,128]{1,0:T(8,128)(2,1)S(1)}, bf16[80,128]{1,0:T(8,128)(2,1)S(1)}, u32[]{:S(2)}, u32[]{:S(2)}) collective-permute-start(bf16[80,128]{1,0:T(8,128)(2,1)S(1)} %get-tuple-element.24), channel_id=1, source_target_pairs={{0,28},{1,29},{2,30},{3,31},{4,8},{5,9},{6,10},{7,11},{8,4},{9,5},... | collective-permute-start | bytes 61448 | tf_op jit(solution)/shard_map/ppermute | solution.py:357
  6.7 1.2 %collective-permute-start = (bf16[144,128]{1,0:T(8,128)(2,1)S(1)}, bf16[144,128]{1,0:T(8,128)(2,1)S(1)}, u32[]{:S(2)}, u32[]{:S(2)}) collective-permute-start(bf16[144,128]{1,0:T(8,128)(2,1)S(1)} %get-tuple-element.23), channel_id=1, source_target_pairs={{0,5},{1,4},{2,7},{3,6},{4,1},{5,0},{6,3},{7,2},{8,13},{9,12},{10,... | collective-permute-start | bytes 110600 | tf_op jit(solution)/shard_map/ppermute | solution.py:358
  7.8 0.0 copy-done
  7.8 1.1 %middle.1 = (f32[128,128]{1,0:T(8,128)S(1)}, bf16[2,128,128]{2,1,0:T(8,128)(2,1)S(1)}, bf16[128,288]{1,0:T(8,128)(2,1)S(1)}) custom-call(bf16[1152,1152]{1,0:T(8,128)(2,1)S(1)} %copy-done, bf16[1152,128]{1,0:T(8,128)(2,1)S(1)} %get-tuple-element.15.mid.refs_2_, bf16[128,1152]{1,0:T(8,128)(2,1)S(1)} %get-tuple-element.16.mid_t, ...), custom_call_target="tpu_custom_call" | custom-call | flops 679477248 | bytes 2654208 | tf_op jit(solution)/shard_map/middle/pallas_call | solution.py:99
  8.9 0.0 collective-permute-done.1.value.refs_9_
  9.0 0.1 collective-permute-start.2
  9.0 0.1 collective-permute-done.3.refs_11_.far_edge
  9.2 1.0 %collective-permute-done.2.refs_10_ = bf16[64,128]{1,0:T(8,128)(2,1)S(1)} collective-permute-done((bf16[64,128]{1,0:T(8,128)(2,1)S(1)}, bf16[64,128]{1,0:T(8,128)(2,1)S(1)}, u32[]{:S(2)}, u32[]{:S(2)}) %collective-permute-start.2) | collective-permute-done | bytes 16416 | tf_op jit(solution)/shard_map/ppermute | solution.py:383
  10.2 0.0 collective-permute-done.refs_8_.near_pack
  10.3 0.0 copy-done.3
  10.3 0.0 copy-done.4
  10.3 0.0 copy-done.5
  10.3 0.0 copy-start.1
  10.3 4.4 %fields.1.refs_0_ = bf16[64,128]{1,0:T(8,128)(2,1)S(1)} custom-call(f32[128,128]{1,0:T(8,128)S(1)} %get-tuple-element.19.ready.refs_0_, s32[288,1152]{1,0:T(8,128)S(1)} %copy-done.3, bf16[1152,128]{1,0:T(8,128)(2,1)S(1)} %get-tuple-element.15.mid.refs_2_, bf16[128,288]{1,0:T(8,128)(2,1)S(1)} %get-tuple-element.20.refs_3_, ...), custom_call_target="tpu_custom_call" | custom-call | flops 1358954496 | bytes 1327104 | tf_op jit(solution)/shard_map/fields/pallas_call | solution.py:99
  14.7 0.0 copy-start.2
  14.7 1.8 %collective-permute-start.6 = (bf16[64,128]{1,0:T(8,128)(2,1)S(1)}, bf16[64,128]{1,0:T(8,128)(2,1)S(1)}, u32[]{:S(2)}, u32[]{:S(2)}) collective-permute-start(bf16[64,128]{1,0:T(8,128)(2,1)S(1)} %fields.1.refs_0_), channel_id=1, source_target_pairs={{0,3},{1,2},{2,1},{3,0},{4,5},{5,4},{6,7},{7,6},{8,11},{9,10},{10,... | collective-permute-start | bytes 49160 | tf_op jit(solution)/shard_map/ppermute | solution.py:409
  16.5 0.3 collective-permute-start.5
  16.8 2.4 %collective-permute-start.4 = (bf16[64,128]{1,0:T(8,128)(2,1)S(1)}, bf16[64,128]{1,0:T(8,128)(2,1)S(1)}, u32[]{:S(2)}, u32[]{:S(2)}) collective-permute-start(bf16[64,128]{1,0:T(8,128)(2,1)S(1)} %fields.1.refs_0_), channel_id=1, source_target_pairs={{0,1},{1,0},{2,3},{3,2},{4,6},{5,7},{6,4},{7,5},{8,9},{9,8},{10,11... | collective-permute-start | bytes 49160 | tf_op jit(solution)/shard_map/ppermute | solution.py:409
  19.1 1.3 %collective-permute-done.6.refs_3_ = bf16[64,128]{1,0:T(8,128)(2,1)S(1)} collective-permute-done((bf16[64,128]{1,0:T(8,128)(2,1)S(1)}, bf16[64,128]{1,0:T(8,128)(2,1)S(1)}, u32[]{:S(2)}, u32[]{:S(2)}) %collective-permute-start.6) | collective-permute-done | bytes 16416 | tf_op jit(solution)/shard_map/ppermute | solution.py:409
  20.4 0.7 %collective-permute-done.5.refs_2_ = bf16[64,128]{1,0:T(8,128)(2,1)S(1)} collective-permute-done((bf16[64,128]{1,0:T(8,128)(2,1)S(1)}, bf16[64,128]{1,0:T(8,128)(2,1)S(1)}, u32[]{:S(2)}, u32[]{:S(2)}) %collective-permute-start.5) | collective-permute-done | bytes 16416 | tf_op jit(solution)/shard_map/ppermute | solution.py:409
  21.2 0.0 collective-permute-done.4.refs_1_
  21.2 2.3 %collective-permute-start.8 = (bf16[64,128]{1,0:T(8,128)(2,1)S(1)}, bf16[64,128]{1,0:T(8,128)(2,1)S(1)}, u32[]{:S(2)}, u32[]{:S(2)}) collective-permute-start(bf16[64,128]{1,0:T(8,128)(2,1)S(1)} %total.1.own), channel_id=1, source_target_pairs={{4,8},{8,4},{12,16},{16,12},{20,24},{24,20},{5,9},{9,5},{13,17},{1... | collective-permute-start | bytes 49160 | tf_op jit(solution)/shard_map/ppermute | solution.py:413
  23.5 1.3 %collective-permute-start.7 = (bf16[64,128]{1,0:T(8,128)(2,1)S(1)}, bf16[64,128]{1,0:T(8,128)(2,1)S(1)}, u32[]{:S(2)}, u32[]{:S(2)}) collective-permute-start(bf16[64,128]{1,0:T(8,128)(2,1)S(1)} %total.1.own), channel_id=1, source_target_pairs={{0,4},{4,0},{8,12},{12,8},{16,20},{20,16},{24,28},{28,24},{1,5},{5... | collective-permute-start | bytes 49160 | tf_op jit(solution)/shard_map/ppermute | solution.py:411
  24.8 0.0 copy-done.1
  24.8 0.5 %inner.1.begun = f32[288,1152]{1,0:T(8,128)S(1)} custom-call(bf16[64,128]{1,0:T(8,128)(2,1)S(1)} %total.1.own, bf16[1152,128]{1,0:T(8,128)(2,1)S(1)} %get-tuple-element.15.mid.refs_2_, bf16[128,1152]{1,0:T(8,128)(2,1)S(1)} %copy-done.1), custom_call_target="tpu_custom_call" | custom-call | flops 84934656 | bytes 1327104 | tf_op jit(solution)/shard_map/inner/pallas_call | solution.py:99
  25.3 1.8 %collective-permute-done.8.far = bf16[64,128]{1,0:T(8,128)(2,1)S(1)} collective-permute-done((bf16[64,128]{1,0:T(8,128)(2,1)S(1)}, bf16[64,128]{1,0:T(8,128)(2,1)S(1)}, u32[]{:S(2)}, u32[]{:S(2)}) %collective-permute-start.8) | collective-permute-done | bytes 16416 | tf_op jit(solution)/shard_map/ppermute | solution.py:413
  27.1 0.0 collective-permute-done.7.near
  27.1 0.0 copy-done.2
  27.1 1.1 %outer.1 = f32[288,1152]{1,0:T(8,128)} custom-call(bf16[64,128]{1,0:T(8,128)(2,1)S(1)} %collective-permute-done.7.near, bf16[64,128]{1,0:T(8,128)(2,1)S(1)} %collective-permute-done.8.far, bf16[144,128]{1,0:T(8,128)(2,1)S(1)} %collective-permute-done.refs_8_.near_pack, bf16[80,128]{1,0:T(8,128)(2,1)S(1)} %collective-permute-done.3.refs_11_.far_edge, ...), custom_call_target="tpu_custom_call" | custom-call | flops 56623104 | bytes 294912 | tf_op jit(solution)/shard_map/outer/pallas_call | solution.py:99
  (5 shorter events, 0.0 us)
Async XLA Ops:
  0.7 7.2 %copy-start = (bf16[1152,1152]{1,0:T(8,128)(2,1)S(1)}, bf16[1152,1152]{1,0:T(8,128)(2,1)}, u32[]{:S(2)}) copy-start(bf16[1152,1152]{1,0:T(8,128)(2,1)} %mask.3) | copy-start | bytes 7962628
  2.4 6.5 %collective-permute-start.1 = (bf16[64,128]{1,0:T(8,128)(2,1)S(1)}, bf16[64,128]{1,0:T(8,128)(2,1)S(1)}, u32[]{:S(2)}, u32[]{:S(2)}) collective-permute-start(bf16[64,128]{1,0:T(8,128)(2,1)S(1)} %get-tuple-element.22.refs_7_), channel_id=1, source_target_pairs={{0,2},{1,3},{2,0},{3,1},{4,7},{5,6},{6,5},{7,4},{8,10},{9,11},{10,... | collective-permute-start | bytes 49160 | tf_op jit(solution)/shard_map/ppermute | solution.py:363
  5.0 4.1 %collective-permute-start.3 = (bf16[80,128]{1,0:T(8,128)(2,1)S(1)}, bf16[80,128]{1,0:T(8,128)(2,1)S(1)}, u32[]{:S(2)}, u32[]{:S(2)}) collective-permute-start(bf16[80,128]{1,0:T(8,128)(2,1)S(1)} %get-tuple-element.24), channel_id=1, source_target_pairs={{0,28},{1,29},{2,30},{3,31},{4,8},{5,9},{6,10},{7,11},{8,4},{9,5},... | collective-permute-start | bytes 61448 | tf_op jit(solution)/shard_map/ppermute | solution.py:357
  6.7 3.6 %collective-permute-start = (bf16[144,128]{1,0:T(8,128)(2,1)S(1)}, bf16[144,128]{1,0:T(8,128)(2,1)S(1)}, u32[]{:S(2)}, u32[]{:S(2)}) collective-permute-start(bf16[144,128]{1,0:T(8,128)(2,1)S(1)} %get-tuple-element.23), channel_id=1, source_target_pairs={{0,5},{1,4},{2,7},{3,6},{4,1},{5,0},{6,3},{7,2},{8,13},{9,12},{10,... | collective-permute-start | bytes 110600 | tf_op jit(solution)/shard_map/ppermute | solution.py:358
  7.8 2.4 %copy-start.3 = (s32[288,1152]{1,0:T(8,128)S(1)}, s32[288,1152]{1,0:T(8,128)}, u32[]{:S(2)}) copy-start(s32[288,1152]{1,0:T(8,128)} %refs_1_.1) | copy-start | bytes 3981316
  7.8 2.4 %copy-start.4 = (bf16[9,256,128]{2,1,0:T(8,128)(2,1)S(1)}, bf16[9,256,128]{2,1,0:T(8,128)(2,1)}, u32[]{:S(2)}) copy-start(bf16[9,256,128]{2,1,0:T(8,128)(2,1)} %constant.17.clone.refs_5_) | copy-start | bytes 1769476
  7.8 2.4 %copy-start.5 = (bf16[9,128,256]{2,1,0:T(8,128)(2,1)S(1)}, bf16[9,128,256]{2,1,0:T(8,128)(2,1)}, u32[]{:S(2)}) copy-start(bf16[9,128,256]{2,1,0:T(8,128)(2,1)} %constant.16.clone.refs_4_) | copy-start | bytes 1769476
  9.0 1.2 %collective-permute-start.2 = (bf16[64,128]{1,0:T(8,128)(2,1)S(1)}, bf16[64,128]{1,0:T(8,128)(2,1)S(1)}, u32[]{:S(2)}, u32[]{:S(2)}) collective-permute-start(bf16[64,128]{1,0:T(8,128)(2,1)S(1)} %relay.1), channel_id=1, source_target_pairs={{0,4},{1,5},{2,6},{3,7},{4,0},{5,1},{6,2},{7,3},{8,12},{9,13},{10,... | collective-permute-start | bytes 49160 | tf_op jit(solution)/shard_map/ppermute | solution.py:383
  10.3 14.5 %copy-start.1 = (bf16[128,1152]{1,0:T(8,128)(2,1)S(1)}, bf16[128,1152]{1,0:T(8,128)(2,1)}, u32[]{:S(2)}) copy-start(bf16[128,1152]{1,0:T(8,128)(2,1)} %constant.19.clone.back) | copy-start | bytes 884740
  14.7 12.5 %copy-start.2 = (bf16[4,128,128]{2,1,0:T(8,128)(2,1)S(1)}, bf16[4,128,128]{2,1,0:T(8,128)(2,1)}, u32[]{:S(2)}) copy-start(bf16[4,128,128]{2,1,0:T(8,128)(2,1)} %constant.20.clone.margins) | copy-start | bytes 393220
  14.7 5.7 %collective-permute-start.6 = (bf16[64,128]{1,0:T(8,128)(2,1)S(1)}, bf16[64,128]{1,0:T(8,128)(2,1)S(1)}, u32[]{:S(2)}, u32[]{:S(2)}) collective-permute-start(bf16[64,128]{1,0:T(8,128)(2,1)S(1)} %fields.1.refs_0_), channel_id=1, source_target_pairs={{0,3},{1,2},{2,1},{3,0},{4,5},{5,4},{6,7},{7,6},{8,11},{9,10},{10,... | collective-permute-start | bytes 49160 | tf_op jit(solution)/shard_map/ppermute | solution.py:409
  16.5 4.6 %collective-permute-start.5 = (bf16[64,128]{1,0:T(8,128)(2,1)S(1)}, bf16[64,128]{1,0:T(8,128)(2,1)S(1)}, u32[]{:S(2)}, u32[]{:S(2)}) collective-permute-start(bf16[64,128]{1,0:T(8,128)(2,1)S(1)} %fields.1.refs_0_), channel_id=1, source_target_pairs={{0,2},{1,3},{2,0},{3,1},{4,7},{5,6},{6,5},{7,4},{8,10},{9,11},{10,... | collective-permute-start | bytes 49160 | tf_op jit(solution)/shard_map/ppermute | solution.py:409
  16.8 4.4 %collective-permute-start.4 = (bf16[64,128]{1,0:T(8,128)(2,1)S(1)}, bf16[64,128]{1,0:T(8,128)(2,1)S(1)}, u32[]{:S(2)}, u32[]{:S(2)}) collective-permute-start(bf16[64,128]{1,0:T(8,128)(2,1)S(1)} %fields.1.refs_0_), channel_id=1, source_target_pairs={{0,1},{1,0},{2,3},{3,2},{4,6},{5,7},{6,4},{7,5},{8,9},{9,8},{10,11... | collective-permute-start | bytes 49160 | tf_op jit(solution)/shard_map/ppermute | solution.py:409
  21.2 6.0 %collective-permute-start.8 = (bf16[64,128]{1,0:T(8,128)(2,1)S(1)}, bf16[64,128]{1,0:T(8,128)(2,1)S(1)}, u32[]{:S(2)}, u32[]{:S(2)}) collective-permute-start(bf16[64,128]{1,0:T(8,128)(2,1)S(1)} %total.1.own), channel_id=1, source_target_pairs={{4,8},{8,4},{12,16},{16,12},{20,24},{24,20},{5,9},{9,5},{13,17},{1... | collective-permute-start | bytes 49160 | tf_op jit(solution)/shard_map/ppermute | solution.py:413
  23.5 3.7 %collective-permute-start.7 = (bf16[64,128]{1,0:T(8,128)(2,1)S(1)}, bf16[64,128]{1,0:T(8,128)(2,1)S(1)}, u32[]{:S(2)}, u32[]{:S(2)}) collective-permute-start(bf16[64,128]{1,0:T(8,128)(2,1)S(1)} %total.1.own), channel_id=1, source_target_pairs={{0,4},{4,0},{8,12},{12,8},{16,20},{20,16},{24,28},{28,24},{1,5},{5... | collective-permute-start | bytes 49160 | tf_op jit(solution)/shard_map/ppermute | solution.py:411

commit v6 on v5

--- a/solution.py
+++ b/solution.py
@@ -174,11 +174,7 @@
     return jnp.where(left, pair, other), jnp.where(left, other, pair)
 
 
-def fields_body(count, row_count, *refs):
-    (middle, target, mid, rows_t, to_columns, from_columns, tables, own) = refs[:8]
-    near_pack, *others, far_edge = refs[8 : 8 + count]
-    out, a_ref, field_a, field_b, bent_a, bent_b, u_ref = refs[8 + count :]
-    fields, bent = (field_a, field_b), (bent_a, bent_b)
+def spectrum_body(middle, tables, near_pack, far_edge, out):
     left = in_left_half((KF, PAIR))
     blocks = middle[...]
     for pack, table in ((near_pack, tables[0]), (far_edge, tables[1])):
@@ -189,6 +185,16 @@
     spectrum = jnp.where(left, top - bottom, -(top + bottom))
     turned = swap_halves(spectrum)
     turned = jnp.where(left, -turned, turned)
+    out[0], out[1] = spectrum, turned
+
+
+def fields_body(count, row_count, *refs):
+    (spectra, target, mid, rows_t, to_columns, from_columns, own) = refs[:7]
+    near_pack, *others = refs[7 : 6 + count]
+    out, a_ref, field_a, field_b, bent_a, bent_b, u_ref = refs[6 + count :]
+    fields, bent = (field_a, field_b), (bent_a, bent_b)
+    left = in_left_half((KF, PAIR))
+    spectrum, turned = spectra[0], spectra[1]
     kernels = [own[...].astype(F32)]
     kernels.append(near_pack[EDGE : 2 * EDGE, :].astype(F32))
     kernels += [one[...].astype(F32) for one in others]
@@ -382,12 +388,19 @@
         relayed = call(relay_body, "relay", small, (kernels[0], middle), [vmem] * 2)
         kernels.append(lax.ppermute(relayed, both, swapped(chip_mate, 0)))
 
+    spectra = call(
+        spectrum_body,
+        "spectrum",
+        pltpu.VMEM((2, KF, PAIR), F32),
+        (middle, edge_tables, near_pack, far_edge),
+        [vmem] * 4,
+    )
     part = call(
         functools.partial(fields_body, count, row_count),
         "fields",
         small,
-        (middle, target_pattern, mid, rows_t, to_columns, from_columns, edge_tables, side, near_pack, *kernels, far_edge),
-        [vmem] * (8 + count),
+        (spectra, target_pattern, mid, rows_t, to_columns, from_columns, side, near_pack, *kernels),
+        [vmem] * (6 + count),
         scratch=[
             pltpu.VMEM((count * row_count, PAIR), BF16),
             pltpu.VMEM((count * row_count, 2 * LANES), F32),

time: 28.5 us -> 28.7 us (level)
  starting transfers between devices: 13.6 us -> 13.3 us
    ppermute x1, waiting for transfers between devices: 0.05 us -> 1.09 us  [per_device(): near_pack = lax.ppermute(mate, both, swapped(chip_mate, 1))]
    ppermute x1, waiting for transfers between devices: 1.04 us -> 0.01 us  [per_device(): kernels.append(lax.ppermute(relayed, both, swapped(chip_mate, 0)))]
    pallas_call x7 -> x8, Pallas kernels: 8.85 us -> 8.94 us  [call(): pl.pallas_call(body, name=name, out_shape=outs, in_specs=specs, out_specs...]
  transfers between devices with their start and end apart: 9 -> 9, of which waited for: 5 -> 5; matrix products, arithmetic and copies ran while one was open for 0% -> 0% of each run, Pallas kernels for 6% -> 7%
where the time goes in v6:
time: 28.7 us; the launch traced here: 28.3 us
  starting transfers between devices  13.3 us (46%)
  Pallas kernels  8.94 us (31%)
  waiting for transfers between devices  5.2 us (18%)
  between operations  0.79 us (3%)
    pallas_call x8, Pallas kernels, call(): pl.pallas_call(body, name=name, out_shape=outs, in_specs=specs, out_specs...  8.94 us
    ppermute x3, starting transfers between devices, per_device(): parts.append(lax.ppermute(part, both, pairs))  4.45 us
    ppermute x1, starting transfers between devices, per_device(): kernels = [lax.ppermute(side, both, pairs)]  2.65 us
    ppermute x1, starting transfers between devices, per_device(): far = lax.ppermute(own, 'tile', [(t, other_side(t)) for t in inner])  2.16 us
    ppermute x1, waiting for transfers between devices, per_device(): far = lax.ppermute(own, 'tile', [(t, other_side(t)) for t in inner])  2.08 us
    ppermute x3, waiting for transfers between devices, per_device(): parts.append(lax.ppermute(part, both, pairs))  1.89 us
    ppermute x1, starting transfers between devices, per_device(): far_edge = lax.ppermute(other, both, swapped(other_side, 0))  1.61 us
    ppermute x1, starting transfers between devices, per_device(): near = lax.ppermute(own, 'tile', [(t, chip_mate(t)) for t in range(tiles)])  1.18 us
  transfers between devices with their start and end apart: 9, of which 5 were waited for; matrix products, arithmetic and copies ran while one was open for 0% of the time, Pallas kernels for 7%

profile of v6, /device:TPU:4, one launch (start us, length us, event | category | flops | bytes accessed | tf_op | source)
XLA Modules:
  0.0 28.3 jit_solution(12817853421174985674)
XLA Ops:
  0.7 0.0 copy-start
  0.7 1.7 %edges.1 = (bf16[144,128]{1,0:T(8,128)(2,1)S(1)}, bf16[80,128]{1,0:T(8,128)(2,1)S(1)}, bf16[64,128]{1,0:T(8,128)(2,1)S(1)}, bf16[1152,128]{1,0:T(8,128)(2,1)S(1)...) custom-call(bf16[1152,1152]{1,0:T(8,128)(2,1)} %mask.3, ...), custom_call_target="tpu_custom_call" | custom-call | flops 75497472 | bytes 589824 | tf_op jit(solution)/shard_map/edges/pallas_call | solution.py:99
  2.4 2.7 %collective-permute-start.2 = (bf16[64,128]{1,0:T(8,128)(2,1)S(1)}, bf16[64,128]{1,0:T(8,128)(2,1)S(1)}, u32[]{:S(2)}, u32[]{:S(2)}) collective-permute-start(bf16[64,128]{1,0:T(8,128)(2,1)S(1)} %get-tuple-element.24.refs_6_), channel_id=1, source_target_pairs={{0,2},{1,3},{2,0},{3,1},{4,7},{5,6},{6,5},{7,4},{8,10},{9,11},{10,... | collective-permute-start | bytes 49160 | tf_op jit(solution)/shard_map/ppermute | solution.py:369
  5.0 1.6 %collective-permute-start.1 = (bf16[80,128]{1,0:T(8,128)(2,1)S(1)}, bf16[80,128]{1,0:T(8,128)(2,1)S(1)}, u32[]{:S(2)}, u32[]{:S(2)}) collective-permute-start(bf16[80,128]{1,0:T(8,128)(2,1)S(1)} %get-tuple-element.22), channel_id=1, source_target_pairs={{0,28},{1,29},{2,30},{3,31},{4,8},{5,9},{6,10},{7,11},{8,4},{9,5},... | collective-permute-start | bytes 61448 | tf_op jit(solution)/shard_map/ppermute | solution.py:363
  6.7 1.2 %collective-permute-start = (bf16[144,128]{1,0:T(8,128)(2,1)S(1)}, bf16[144,128]{1,0:T(8,128)(2,1)S(1)}, u32[]{:S(2)}, u32[]{:S(2)}) collective-permute-start(bf16[144,128]{1,0:T(8,128)(2,1)S(1)} %get-tuple-element.21), channel_id=1, source_target_pairs={{0,5},{1,4},{2,7},{3,6},{4,1},{5,0},{6,3},{7,2},{8,13},{9,12},{10,... | collective-permute-start | bytes 110600 | tf_op jit(solution)/shard_map/ppermute | solution.py:364
  7.8 0.0 copy-done
  7.8 1.1 %middle.1 = (f32[128,128]{1,0:T(8,128)S(1)}, bf16[2,128,128]{2,1,0:T(8,128)(2,1)S(1)}, bf16[128,288]{1,0:T(8,128)(2,1)S(1)}) custom-call(bf16[1152,1152]{1,0:T(8,128)(2,1)S(1)} %copy-done, bf16[1152,128]{1,0:T(8,128)(2,1)S(1)} %get-tuple-element.15.mid.refs_2_, bf16[128,1152]{1,0:T(8,128)(2,1)S(1)} %get-tuple-element.16.mid_t, ...), custom_call_target="tpu_custom_call" | custom-call | flops 679477248 | bytes 2654208 | tf_op jit(solution)/shard_map/middle/pallas_call | solution.py:99
  8.9 0.0 collective-permute-done.2.value.refs_8_
  9.0 0.1 collective-permute-start.3
  9.0 0.1 collective-permute-done.1.far_edge
  9.2 1.1 %collective-permute-done.near_pack.refs_7_ = bf16[144,128]{1,0:T(8,128)(2,1)S(1)} collective-permute-done((bf16[144,128]{1,0:T(8,128)(2,1)S(1)}, bf16[144,128]{1,0:T(8,128)(2,1)S(1)}, u32[]{:S(2)}, u32[]{:S(2)}) %collective-permute-start) | collective-permute-done | bytes 36896 | tf_op jit(solution)/shard_map/ppermute | solution.py:364
  10.3 0.3 %spectrum.1.refs_0_ = f32[2,64,128]{2,1,0:T(8,128)S(1)} custom-call(f32[128,128]{1,0:T(8,128)S(1)} %get-tuple-element.19.middle.ready, bf16[2,128,128]{2,1,0:T(8,128)(2,1)S(1)} %get-tuple-element.20.tables, bf16[144,128]{1,0:T(8,128)(2,1)S(1)} %collective-permute-done.near_pack.refs_7_, bf16[80,128]{1,0:T(8,128)(2,1)S(1)} %collective-permute-done.1.far_edge), custom_call_target="tpu_custom_call" | custom-call | tf_op jit(solution)/shard_map/spectrum/pallas_call | solution.py:99
  10.6 0.0 collective-permute-done.3.refs_9_
  10.6 0.0 copy-done.3
  10.6 0.0 copy-done.4
  10.6 0.0 copy-done.5
  10.6 0.0 copy-start.1
  10.6 4.2 %fields.1.refs_0_ = bf16[64,128]{1,0:T(8,128)(2,1)S(1)} custom-call(f32[2,64,128]{2,1,0:T(8,128)S(1)} %spectrum.1.refs_0_, s32[288,1152]{1,0:T(8,128)S(1)} %copy-done.3, bf16[1152,128]{1,0:T(8,128)(2,1)S(1)} %get-tuple-element.15.mid.refs_2_, bf16[128,288]{1,0:T(8,128)(2,1)S(1)} %get-tuple-element.23.refs_3_, bf16[9,128,256]{2,1,0:T(8,128)(2,1)S(1)} %copy-done.5, ...), custom_call_target="tpu_custom_call" | custom-call | flops 1358954496 | bytes 1327104 | tf_op jit(solution)/shard_map/fields/pallas_call | solution.py:99
  14.8 0.0 copy-start.2
  14.8 1.4 %collective-permute-start.6 = (bf16[64,128]{1,0:T(8,128)(2,1)S(1)}, bf16[64,128]{1,0:T(8,128)(2,1)S(1)}, u32[]{:S(2)}, u32[]{:S(2)}) collective-permute-start(bf16[64,128]{1,0:T(8,128)(2,1)S(1)} %fields.1.refs_0_), channel_id=1, source_target_pairs={{0,3},{1,2},{2,1},{3,0},{4,5},{5,4},{6,7},{7,6},{8,11},{9,10},{10,... | collective-permute-start | bytes 49160 | tf_op jit(solution)/shard_map/ppermute | solution.py:422
  16.3 0.6 %collective-permute-start.5 = (bf16[64,128]{1,0:T(8,128)(2,1)S(1)}, bf16[64,128]{1,0:T(8,128)(2,1)S(1)}, u32[]{:S(2)}, u32[]{:S(2)}) collective-permute-start(bf16[64,128]{1,0:T(8,128)(2,1)S(1)} %fields.1.refs_0_), channel_id=1, source_target_pairs={{0,2},{1,3},{2,0},{3,1},{4,7},{5,6},{6,5},{7,4},{8,10},{9,11},{10,... | collective-permute-start | bytes 49160 | tf_op jit(solution)/shard_map/ppermute | solution.py:422
  16.8 2.4 %collective-permute-start.4 = (bf16[64,128]{1,0:T(8,128)(2,1)S(1)}, bf16[64,128]{1,0:T(8,128)(2,1)S(1)}, u32[]{:S(2)}, u32[]{:S(2)}) collective-permute-start(bf16[64,128]{1,0:T(8,128)(2,1)S(1)} %fields.1.refs_0_), channel_id=1, source_target_pairs={{0,1},{1,0},{2,3},{3,2},{4,6},{5,7},{6,4},{7,5},{8,9},{9,8},{10,11... | collective-permute-start | bytes 49160 | tf_op jit(solution)/shard_map/ppermute | solution.py:422
  19.3 1.2 %collective-permute-done.6.refs_3_ = bf16[64,128]{1,0:T(8,128)(2,1)S(1)} collective-permute-done((bf16[64,128]{1,0:T(8,128)(2,1)S(1)}, bf16[64,128]{1,0:T(8,128)(2,1)S(1)}, u32[]{:S(2)}, u32[]{:S(2)}) %collective-permute-start.6) | collective-permute-done | bytes 16416 | tf_op jit(solution)/shard_map/ppermute | solution.py:422
  20.5 0.7 %collective-permute-done.5.refs_2_ = bf16[64,128]{1,0:T(8,128)(2,1)S(1)} collective-permute-done((bf16[64,128]{1,0:T(8,128)(2,1)S(1)}, bf16[64,128]{1,0:T(8,128)(2,1)S(1)}, u32[]{:S(2)}, u32[]{:S(2)}) %collective-permute-start.5) | collective-permute-done | bytes 16416 | tf_op jit(solution)/shard_map/ppermute | solution.py:422
  21.2 0.0 collective-permute-done.4.refs_1_
  21.2 2.2 %collective-permute-start.8 = (bf16[64,128]{1,0:T(8,128)(2,1)S(1)}, bf16[64,128]{1,0:T(8,128)(2,1)S(1)}, u32[]{:S(2)}, u32[]{:S(2)}) collective-permute-start(bf16[64,128]{1,0:T(8,128)(2,1)S(1)} %total.1.own), channel_id=1, source_target_pairs={{4,8},{8,4},{12,16},{16,12},{20,24},{24,20},{5,9},{9,5},{13,17},{1... | collective-permute-start | bytes 49160 | tf_op jit(solution)/shard_map/ppermute | solution.py:426
  23.3 1.2 %collective-permute-start.7 = (bf16[64,128]{1,0:T(8,128)(2,1)S(1)}, bf16[64,128]{1,0:T(8,128)(2,1)S(1)}, u32[]{:S(2)}, u32[]{:S(2)}) collective-permute-start(bf16[64,128]{1,0:T(8,128)(2,1)S(1)} %total.1.own), channel_id=1, source_target_pairs={{0,4},{4,0},{8,12},{12,8},{16,20},{20,16},{24,28},{28,24},{1,5},{5... | collective-permute-start | bytes 49160 | tf_op jit(solution)/shard_map/ppermute | solution.py:424
  24.5 0.0 copy-done.1
  24.5 0.5 %inner.1.begun = f32[288,1152]{1,0:T(8,128)S(1)} custom-call(bf16[64,128]{1,0:T(8,128)(2,1)S(1)} %total.1.own, bf16[1152,128]{1,0:T(8,128)(2,1)S(1)} %get-tuple-element.15.mid.refs_2_, bf16[128,1152]{1,0:T(8,128)(2,1)S(1)} %copy-done.1), custom_call_target="tpu_custom_call" | custom-call | flops 84934656 | bytes 1327104 | tf_op jit(solution)/shard_map/inner/pallas_call | solution.py:99
  25.1 2.1 %collective-permute-done.8.far = bf16[64,128]{1,0:T(8,128)(2,1)S(1)} collective-permute-done((bf16[64,128]{1,0:T(8,128)(2,1)S(1)}, bf16[64,128]{1,0:T(8,128)(2,1)S(1)}, u32[]{:S(2)}, u32[]{:S(2)}) %collective-permute-start.8) | collective-permute-done | bytes 16416 | tf_op jit(solution)/shard_map/ppermute | solution.py:426
  27.1 0.0 collective-permute-done.7.near
  27.1 1.1 %outer.1 = f32[288,1152]{1,0:T(8,128)} custom-call(bf16[64,128]{1,0:T(8,128)(2,1)S(1)} %collective-permute-done.7.near, bf16[64,128]{1,0:T(8,128)(2,1)S(1)} %collective-permute-done.8.far, bf16[144,128]{1,0:T(8,128)(2,1)S(1)} %collective-permute-done.near_pack.refs_7_, bf16[80,128]{1,0:T(8,128)(2,1)S(1)} %collective-permute-done.1.far_edge, ...), custom_call_target="tpu_custom_call" | custom-call | flops 56623104 | bytes 294912 | tf_op jit(solution)/shard_map/outer/pallas_call | solution.py:99
  (6 shorter events, 0.0 us)
Async XLA Ops:
  0.7 7.2 %copy-start = (bf16[1152,1152]{1,0:T(8,128)(2,1)S(1)}, bf16[1152,1152]{1,0:T(8,128)(2,1)}, u32[]{:S(2)}) copy-start(bf16[1152,1152]{1,0:T(8,128)(2,1)} %mask.3) | copy-start | bytes 7962628
  2.4 6.5 %collective-permute-start.2 = (bf16[64,128]{1,0:T(8,128)(2,1)S(1)}, bf16[64,128]{1,0:T(8,128)(2,1)S(1)}, u32[]{:S(2)}, u32[]{:S(2)}) collective-permute-start(bf16[64,128]{1,0:T(8,128)(2,1)S(1)} %get-tuple-element.24.refs_6_), channel_id=1, source_target_pairs={{0,2},{1,3},{2,0},{3,1},{4,7},{5,6},{6,5},{7,4},{8,10},{9,11},{10,... | collective-permute-start | bytes 49160 | tf_op jit(solution)/shard_map/ppermute | solution.py:369
  5.0 4.1 %collective-permute-start.1 = (bf16[80,128]{1,0:T(8,128)(2,1)S(1)}, bf16[80,128]{1,0:T(8,128)(2,1)S(1)}, u32[]{:S(2)}, u32[]{:S(2)}) collective-permute-start(bf16[80,128]{1,0:T(8,128)(2,1)S(1)} %get-tuple-element.22), channel_id=1, source_target_pairs={{0,28},{1,29},{2,30},{3,31},{4,8},{5,9},{6,10},{7,11},{8,4},{9,5},... | collective-permute-start | bytes 61448 | tf_op jit(solution)/shard_map/ppermute | solution.py:363
  6.7 3.6 %collective-permute-start = (bf16[144,128]{1,0:T(8,128)(2,1)S(1)}, bf16[144,128]{1,0:T(8,128)(2,1)S(1)}, u32[]{:S(2)}, u32[]{:S(2)}) collective-permute-start(bf16[144,128]{1,0:T(8,128)(2,1)S(1)} %get-tuple-element.21), channel_id=1, source_target_pairs={{0,5},{1,4},{2,7},{3,6},{4,1},{5,0},{6,3},{7,2},{8,13},{9,12},{10,... | collective-permute-start | bytes 110600 | tf_op jit(solution)/shard_map/ppermute | solution.py:364
  7.8 2.8 %copy-start.3 = (s32[288,1152]{1,0:T(8,128)S(1)}, s32[288,1152]{1,0:T(8,128)}, u32[]{:S(2)}) copy-start(s32[288,1152]{1,0:T(8,128)} %refs_1_.1) | copy-start | bytes 3981316
  7.8 2.8 %copy-start.4 = (bf16[9,256,128]{2,1,0:T(8,128)(2,1)S(1)}, bf16[9,256,128]{2,1,0:T(8,128)(2,1)}, u32[]{:S(2)}) copy-start(bf16[9,256,128]{2,1,0:T(8,128)(2,1)} %constant.17.clone.refs_5_) | copy-start | bytes 1769476
  7.8 2.8 %copy-start.5 = (bf16[9,128,256]{2,1,0:T(8,128)(2,1)S(1)}, bf16[9,128,256]{2,1,0:T(8,128)(2,1)}, u32[]{:S(2)}) copy-start(bf16[9,128,256]{2,1,0:T(8,128)(2,1)} %constant.16.clone.refs_4_) | copy-start | bytes 1769476
  9.0 1.6 %collective-permute-start.3 = (bf16[64,128]{1,0:T(8,128)(2,1)S(1)}, bf16[64,128]{1,0:T(8,128)(2,1)S(1)}, u32[]{:S(2)}, u32[]{:S(2)}) collective-permute-start(bf16[64,128]{1,0:T(8,128)(2,1)S(1)} %relay.1), channel_id=1, source_target_pairs={{0,4},{1,5},{2,6},{3,7},{4,0},{5,1},{6,2},{7,3},{8,12},{9,13},{10,... | collective-permute-start | bytes 49160 | tf_op jit(solution)/shard_map/ppermute | solution.py:389
  10.6 13.9 %copy-start.1 = (bf16[128,1152]{1,0:T(8,128)(2,1)S(1)}, bf16[128,1152]{1,0:T(8,128)(2,1)}, u32[]{:S(2)}) copy-start(bf16[128,1152]{1,0:T(8,128)(2,1)} %constant.19.clone.back) | copy-start | bytes 884740
  14.8 12.3 %copy-start.2 = (bf16[4,128,128]{2,1,0:T(8,128)(2,1)S(1)}, bf16[4,128,128]{2,1,0:T(8,128)(2,1)}, u32[]{:S(2)}) copy-start(bf16[4,128,128]{2,1,0:T(8,128)(2,1)} %constant.20.clone.margins) | copy-start | bytes 393220
  14.8 5.7 %collective-permute-start.6 = (bf16[64,128]{1,0:T(8,128)(2,1)S(1)}, bf16[64,128]{1,0:T(8,128)(2,1)S(1)}, u32[]{:S(2)}, u32[]{:S(2)}) collective-permute-start(bf16[64,128]{1,0:T(8,128)(2,1)S(1)} %fields.1.refs_0_), channel_id=1, source_target_pairs={{0,3},{1,2},{2,1},{3,0},{4,5},{5,4},{6,7},{7,6},{8,11},{9,10},{10,... | collective-permute-start | bytes 49160 | tf_op jit(solution)/shard_map/ppermute | solution.py:422
  16.3 4.9 %collective-permute-start.5 = (bf16[64,128]{1,0:T(8,128)(2,1)S(1)}, bf16[64,128]{1,0:T(8,128)(2,1)S(1)}, u32[]{:S(2)}, u32[]{:S(2)}) collective-permute-start(bf16[64,128]{1,0:T(8,128)(2,1)S(1)} %fields.1.refs_0_), channel_id=1, source_target_pairs={{0,2},{1,3},{2,0},{3,1},{4,7},{5,6},{6,5},{7,4},{8,10},{9,11},{10,... | collective-permute-start | bytes 49160 | tf_op jit(solution)/shard_map/ppermute | solution.py:422
  16.8 4.3 %collective-permute-start.4 = (bf16[64,128]{1,0:T(8,128)(2,1)S(1)}, bf16[64,128]{1,0:T(8,128)(2,1)S(1)}, u32[]{:S(2)}, u32[]{:S(2)}) collective-permute-start(bf16[64,128]{1,0:T(8,128)(2,1)S(1)} %fields.1.refs_0_), channel_id=1, source_target_pairs={{0,1},{1,0},{2,3},{3,2},{4,6},{5,7},{6,4},{7,5},{8,9},{9,8},{10,11... | collective-permute-start | bytes 49160 | tf_op jit(solution)/shard_map/ppermute | solution.py:422
  21.2 6.0 %collective-permute-start.8 = (bf16[64,128]{1,0:T(8,128)(2,1)S(1)}, bf16[64,128]{1,0:T(8,128)(2,1)S(1)}, u32[]{:S(2)}, u32[]{:S(2)}) collective-permute-start(bf16[64,128]{1,0:T(8,128)(2,1)S(1)} %total.1.own), channel_id=1, source_target_pairs={{4,8},{8,4},{12,16},{16,12},{20,24},{24,20},{5,9},{9,5},{13,17},{1... | collective-permute-start | bytes 49160 | tf_op jit(solution)/shard_map/ppermute | solution.py:426
  23.3 3.8 %collective-permute-start.7 = (bf16[64,128]{1,0:T(8,128)(2,1)S(1)}, bf16[64,128]{1,0:T(8,128)(2,1)S(1)}, u32[]{:S(2)}, u32[]{:S(2)}) collective-permute-start(bf16[64,128]{1,0:T(8,128)(2,1)S(1)} %total.1.own), channel_id=1, source_target_pairs={{0,4},{4,0},{8,12},{12,8},{16,20},{20,16},{24,28},{28,24},{1,5},{5... | collective-permute-start | bytes 49160 | tf_op jit(solution)/shard_map/ppermute | solution.py:424

commit v7 on v5

--- a/solution.py
+++ b/solution.py
@@ -204,7 +204,7 @@
     waves = dot(rows, jnp.concatenate(stacks, 1)).astype(BF16)
     for index in range(count):
         a_ref[index * row_count : (index + 1) * row_count, :] = waves[:, index * PAIR : (index + 1) * PAIR]
-    step = 32 if row_count % 32 == 0 else 16
+    step = 16
     halves = (slice(0, LANES), slice(LANES, 2 * LANES))
     fields[0][...] = dot(a_ref[...], to_columns[0])
     for block in range(BLOCKS + 1):

time: 28.5 us -> 28.5 us (level)
  no operation moved by 1% of the time
where the time goes in v7:
time: 28.5 us; the launch traced here: 28.3 us
  starting transfers between devices  13.6 us (48%)
  Pallas kernels  8.85 us (31%)
  waiting for transfers between devices  5.06 us (18%)
  between operations  0.75 us (3%)
    pallas_call x7, Pallas kernels, call(): pl.pallas_call(body, name=name, out_shape=outs, in_specs=specs, out_specs...  8.85 us
    ppermute x3, starting transfers between devices, per_device(): parts.append(lax.ppermute(part, both, pairs))  4.45 us
    ppermute x1, starting transfers between devices, per_device(): kernels = [lax.ppermute(side, both, pairs)]  2.65 us
    ppermute x1, starting transfers between devices, per_device(): far = lax.ppermute(own, 'tile', [(t, other_side(t)) for t in inner])  2.29 us
    ppermute x3, waiting for transfers between devices, per_device(): parts.append(lax.ppermute(part, both, pairs))  2.01 us
    ppermute x1, waiting for transfers between devices, per_device(): far = lax.ppermute(own, 'tile', [(t, other_side(t)) for t in inner])  1.83 us
    ppermute x1, starting transfers between devices, per_device(): far_edge = lax.ppermute(other, both, swapped(other_side, 0))  1.61 us
    ppermute x1, starting transfers between devices, per_device(): near = lax.ppermute(own, 'tile', [(t, chip_mate(t)) for t in range(tiles)])  1.31 us
  transfers between devices with their start and end apart: 9, of which 5 were waited for; matrix products, arithmetic and copies ran while one was open for 0% of the time, Pallas kernels for 6%

profile of v7, /device:TPU:4, one launch (start us, length us, event | category | flops | bytes accessed | tf_op | source)
XLA Modules:
  0.0 28.3 jit_solution(9434170181473145956)
XLA Ops:
  0.7 0.0 copy-start
  0.7 1.7 %edges.1 = (bf16[144,128]{1,0:T(8,128)(2,1)S(1)}, bf16[80,128]{1,0:T(8,128)(2,1)S(1)}, bf16[64,128]{1,0:T(8,128)(2,1)S(1)}, bf16[1152,128]{1,0:T(8,128)(2,1)S(1)...) custom-call(bf16[1152,1152]{1,0:T(8,128)(2,1)} %mask.3, ...), custom_call_target="tpu_custom_call" | custom-call | flops 75497472 | bytes 589824 | tf_op jit(solution)/shard_map/edges/pallas_call | solution.py:99
  2.4 2.7 %collective-permute-start.1 = (bf16[64,128]{1,0:T(8,128)(2,1)S(1)}, bf16[64,128]{1,0:T(8,128)(2,1)S(1)}, u32[]{:S(2)}, u32[]{:S(2)}) collective-permute-start(bf16[64,128]{1,0:T(8,128)(2,1)S(1)} %get-tuple-element.22.refs_7_), channel_id=1, source_target_pairs={{0,2},{1,3},{2,0},{3,1},{4,7},{5,6},{6,5},{7,4},{8,10},{9,11},{10,... | collective-permute-start | bytes 49160 | tf_op jit(solution)/shard_map/ppermute | solution.py:363
  5.0 1.6 %collective-permute-start.3 = (bf16[80,128]{1,0:T(8,128)(2,1)S(1)}, bf16[80,128]{1,0:T(8,128)(2,1)S(1)}, u32[]{:S(2)}, u32[]{:S(2)}) collective-permute-start(bf16[80,128]{1,0:T(8,128)(2,1)S(1)} %get-tuple-element.24), channel_id=1, source_target_pairs={{0,28},{1,29},{2,30},{3,31},{4,8},{5,9},{6,10},{7,11},{8,4},{9,5},... | collective-permute-start | bytes 61448 | tf_op jit(solution)/shard_map/ppermute | solution.py:357
  6.7 1.2 %collective-permute-start = (bf16[144,128]{1,0:T(8,128)(2,1)S(1)}, bf16[144,128]{1,0:T(8,128)(2,1)S(1)}, u32[]{:S(2)}, u32[]{:S(2)}) collective-permute-start(bf16[144,128]{1,0:T(8,128)(2,1)S(1)} %get-tuple-element.23), channel_id=1, source_target_pairs={{0,5},{1,4},{2,7},{3,6},{4,1},{5,0},{6,3},{7,2},{8,13},{9,12},{10,... | collective-permute-start | bytes 110600 | tf_op jit(solution)/shard_map/ppermute | solution.py:358
  7.8 0.0 copy-done
  7.8 1.1 %middle.1 = (f32[128,128]{1,0:T(8,128)S(1)}, bf16[2,128,128]{2,1,0:T(8,128)(2,1)S(1)}, bf16[128,288]{1,0:T(8,128)(2,1)S(1)}) custom-call(bf16[1152,1152]{1,0:T(8,128)(2,1)S(1)} %copy-done, bf16[1152,128]{1,0:T(8,128)(2,1)S(1)} %get-tuple-element.15.mid.refs_2_, bf16[128,1152]{1,0:T(8,128)(2,1)S(1)} %get-tuple-element.16.mid_t, ...), custom_call_target="tpu_custom_call" | custom-call | flops 679477248 | bytes 2654208 | tf_op jit(solution)/shard_map/middle/pallas_call | solution.py:99
  8.9 0.0 collective-permute-done.1.value.refs_9_
  9.0 0.1 collective-permute-start.2
  9.0 0.1 collective-permute-done.3.refs_11_.far_edge
  9.2 1.0 %collective-permute-done.2.refs_10_ = bf16[64,128]{1,0:T(8,128)(2,1)S(1)} collective-permute-done((bf16[64,128]{1,0:T(8,128)(2,1)S(1)}, bf16[64,128]{1,0:T(8,128)(2,1)S(1)}, u32[]{:S(2)}, u32[]{:S(2)}) %collective-permute-start.2) | collective-permute-done | bytes 16416 | tf_op jit(solution)/shard_map/ppermute | solution.py:383
  10.2 0.0 collective-permute-done.refs_8_.near_pack
  10.3 0.0 copy-done.3
  10.3 0.0 copy-done.4
  10.3 0.0 copy-done.5
  10.3 0.0 copy-start.1
  10.3 4.4 %fields.1.refs_0_ = bf16[64,128]{1,0:T(8,128)(2,1)S(1)} custom-call(f32[128,128]{1,0:T(8,128)S(1)} %get-tuple-element.19.ready.refs_0_, s32[288,1152]{1,0:T(8,128)S(1)} %copy-done.3, bf16[1152,128]{1,0:T(8,128)(2,1)S(1)} %get-tuple-element.15.mid.refs_2_, bf16[128,288]{1,0:T(8,128)(2,1)S(1)} %get-tuple-element.20.refs_3_, ...), custom_call_target="tpu_custom_call" | custom-call | flops 1358954496 | bytes 1327104 | tf_op jit(solution)/shard_map/fields/pallas_call | solution.py:99
  14.7 0.0 copy-start.2
  14.7 1.8 %collective-permute-start.6 = (bf16[64,128]{1,0:T(8,128)(2,1)S(1)}, bf16[64,128]{1,0:T(8,128)(2,1)S(1)}, u32[]{:S(2)}, u32[]{:S(2)}) collective-permute-start(bf16[64,128]{1,0:T(8,128)(2,1)S(1)} %fields.1.refs_0_), channel_id=1, source_target_pairs={{0,3},{1,2},{2,1},{3,0},{4,5},{5,4},{6,7},{7,6},{8,11},{9,10},{10,... | collective-permute-start | bytes 49160 | tf_op jit(solution)/shard_map/ppermute | solution.py:409
  16.5 0.3 collective-permute-start.5
  16.8 2.4 %collective-permute-start.4 = (bf16[64,128]{1,0:T(8,128)(2,1)S(1)}, bf16[64,128]{1,0:T(8,128)(2,1)S(1)}, u32[]{:S(2)}, u32[]{:S(2)}) collective-permute-start(bf16[64,128]{1,0:T(8,128)(2,1)S(1)} %fields.1.refs_0_), channel_id=1, source_target_pairs={{0,1},{1,0},{2,3},{3,2},{4,6},{5,7},{6,4},{7,5},{8,9},{9,8},{10,11... | collective-permute-start | bytes 49160 | tf_op jit(solution)/shard_map/ppermute | solution.py:409
  19.1 1.3 %collective-permute-done.6.refs_3_ = bf16[64,128]{1,0:T(8,128)(2,1)S(1)} collective-permute-done((bf16[64,128]{1,0:T(8,128)(2,1)S(1)}, bf16[64,128]{1,0:T(8,128)(2,1)S(1)}, u32[]{:S(2)}, u32[]{:S(2)}) %collective-permute-start.6) | collective-permute-done | bytes 16416 | tf_op jit(solution)/shard_map/ppermute | solution.py:409
  20.4 0.7 %collective-permute-done.5.refs_2_ = bf16[64,128]{1,0:T(8,128)(2,1)S(1)} collective-permute-done((bf16[64,128]{1,0:T(8,128)(2,1)S(1)}, bf16[64,128]{1,0:T(8,128)(2,1)S(1)}, u32[]{:S(2)}, u32[]{:S(2)}) %collective-permute-start.5) | collective-permute-done | bytes 16416 | tf_op jit(solution)/shard_map/ppermute | solution.py:409
  21.2 0.0 collective-permute-done.4.refs_1_
  21.2 2.3 %collective-permute-start.8 = (bf16[64,128]{1,0:T(8,128)(2,1)S(1)}, bf16[64,128]{1,0:T(8,128)(2,1)S(1)}, u32[]{:S(2)}, u32[]{:S(2)}) collective-permute-start(bf16[64,128]{1,0:T(8,128)(2,1)S(1)} %total.1.own), channel_id=1, source_target_pairs={{4,8},{8,4},{12,16},{16,12},{20,24},{24,20},{5,9},{9,5},{13,17},{1... | collective-permute-start | bytes 49160 | tf_op jit(solution)/shard_map/ppermute | solution.py:413
  23.5 1.3 %collective-permute-start.7 = (bf16[64,128]{1,0:T(8,128)(2,1)S(1)}, bf16[64,128]{1,0:T(8,128)(2,1)S(1)}, u32[]{:S(2)}, u32[]{:S(2)}) collective-permute-start(bf16[64,128]{1,0:T(8,128)(2,1)S(1)} %total.1.own), channel_id=1, source_target_pairs={{0,4},{4,0},{8,12},{12,8},{16,20},{20,16},{24,28},{28,24},{1,5},{5... | collective-permute-start | bytes 49160 | tf_op jit(solution)/shard_map/ppermute | solution.py:411
  24.8 0.0 copy-done.1
  24.8 0.5 %inner.1.begun = f32[288,1152]{1,0:T(8,128)S(1)} custom-call(bf16[64,128]{1,0:T(8,128)(2,1)S(1)} %total.1.own, bf16[1152,128]{1,0:T(8,128)(2,1)S(1)} %get-tuple-element.15.mid.refs_2_, bf16[128,1152]{1,0:T(8,128)(2,1)S(1)} %copy-done.1), custom_call_target="tpu_custom_call" | custom-call | flops 84934656 | bytes 1327104 | tf_op jit(solution)/shard_map/inner/pallas_call | solution.py:99
  25.3 1.8 %collective-permute-done.8.far = bf16[64,128]{1,0:T(8,128)(2,1)S(1)} collective-permute-done((bf16[64,128]{1,0:T(8,128)(2,1)S(1)}, bf16[64,128]{1,0:T(8,128)(2,1)S(1)}, u32[]{:S(2)}, u32[]{:S(2)}) %collective-permute-start.8) | collective-permute-done | bytes 16416 | tf_op jit(solution)/shard_map/ppermute | solution.py:413
  27.1 0.0 collective-permute-done.7.near
  27.1 0.0 copy-done.2
  27.1 1.1 %outer.1 = f32[288,1152]{1,0:T(8,128)} custom-call(bf16[64,128]{1,0:T(8,128)(2,1)S(1)} %collective-permute-done.7.near, bf16[64,128]{1,0:T(8,128)(2,1)S(1)} %collective-permute-done.8.far, bf16[144,128]{1,0:T(8,128)(2,1)S(1)} %collective-permute-done.refs_8_.near_pack, bf16[80,128]{1,0:T(8,128)(2,1)S(1)} %collective-permute-done.3.refs_11_.far_edge, ...), custom_call_target="tpu_custom_call" | custom-call | flops 56623104 | bytes 294912 | tf_op jit(solution)/shard_map/outer/pallas_call | solution.py:99
  (5 shorter events, 0.0 us)
Async XLA Ops:
  0.7 7.2 %copy-start = (bf16[1152,1152]{1,0:T(8,128)(2,1)S(1)}, bf16[1152,1152]{1,0:T(8,128)(2,1)}, u32[]{:S(2)}) copy-start(bf16[1152,1152]{1,0:T(8,128)(2,1)} %mask.3) | copy-start | bytes 7962628
  2.4 6.5 %collective-permute-start.1 = (bf16[64,128]{1,0:T(8,128)(2,1)S(1)}, bf16[64,128]{1,0:T(8,128)(2,1)S(1)}, u32[]{:S(2)}, u32[]{:S(2)}) collective-permute-start(bf16[64,128]{1,0:T(8,128)(2,1)S(1)} %get-tuple-element.22.refs_7_), channel_id=1, source_target_pairs={{0,2},{1,3},{2,0},{3,1},{4,7},{5,6},{6,5},{7,4},{8,10},{9,11},{10,... | collective-permute-start | bytes 49160 | tf_op jit(solution)/shard_map/ppermute | solution.py:363
  5.0 4.1 %collective-permute-start.3 = (bf16[80,128]{1,0:T(8,128)(2,1)S(1)}, bf16[80,128]{1,0:T(8,128)(2,1)S(1)}, u32[]{:S(2)}, u32[]{:S(2)}) collective-permute-start(bf16[80,128]{1,0:T(8,128)(2,1)S(1)} %get-tuple-element.24), channel_id=1, source_target_pairs={{0,28},{1,29},{2,30},{3,31},{4,8},{5,9},{6,10},{7,11},{8,4},{9,5},... | collective-permute-start | bytes 61448 | tf_op jit(solution)/shard_map/ppermute | solution.py:357
  6.7 3.6 %collective-permute-start = (bf16[144,128]{1,0:T(8,128)(2,1)S(1)}, bf16[144,128]{1,0:T(8,128)(2,1)S(1)}, u32[]{:S(2)}, u32[]{:S(2)}) collective-permute-start(bf16[144,128]{1,0:T(8,128)(2,1)S(1)} %get-tuple-element.23), channel_id=1, source_target_pairs={{0,5},{1,4},{2,7},{3,6},{4,1},{5,0},{6,3},{7,2},{8,13},{9,12},{10,... | collective-permute-start | bytes 110600 | tf_op jit(solution)/shard_map/ppermute | solution.py:358
  7.8 2.4 %copy-start.3 = (s32[288,1152]{1,0:T(8,128)S(1)}, s32[288,1152]{1,0:T(8,128)}, u32[]{:S(2)}) copy-start(s32[288,1152]{1,0:T(8,128)} %refs_1_.1) | copy-start | bytes 3981316
  7.8 2.4 %copy-start.4 = (bf16[9,256,128]{2,1,0:T(8,128)(2,1)S(1)}, bf16[9,256,128]{2,1,0:T(8,128)(2,1)}, u32[]{:S(2)}) copy-start(bf16[9,256,128]{2,1,0:T(8,128)(2,1)} %constant.17.clone.refs_5_) | copy-start | bytes 1769476
  7.8 2.4 %copy-start.5 = (bf16[9,128,256]{2,1,0:T(8,128)(2,1)S(1)}, bf16[9,128,256]{2,1,0:T(8,128)(2,1)}, u32[]{:S(2)}) copy-start(bf16[9,128,256]{2,1,0:T(8,128)(2,1)} %constant.16.clone.refs_4_) | copy-start | bytes 1769476
  9.0 1.2 %collective-permute-start.2 = (bf16[64,128]{1,0:T(8,128)(2,1)S(1)}, bf16[64,128]{1,0:T(8,128)(2,1)S(1)}, u32[]{:S(2)}, u32[]{:S(2)}) collective-permute-start(bf16[64,128]{1,0:T(8,128)(2,1)S(1)} %relay.1), channel_id=1, source_target_pairs={{0,4},{1,5},{2,6},{3,7},{4,0},{5,1},{6,2},{7,3},{8,12},{9,13},{10,... | collective-permute-start | bytes 49160 | tf_op jit(solution)/shard_map/ppermute | solution.py:383
  10.3 14.5 %copy-start.1 = (bf16[128,1152]{1,0:T(8,128)(2,1)S(1)}, bf16[128,1152]{1,0:T(8,128)(2,1)}, u32[]{:S(2)}) copy-start(bf16[128,1152]{1,0:T(8,128)(2,1)} %constant.19.clone.back) | copy-start | bytes 884740
  14.7 12.5 %copy-start.2 = (bf16[4,128,128]{2,1,0:T(8,128)(2,1)S(1)}, bf16[4,128,128]{2,1,0:T(8,128)(2,1)}, u32[]{:S(2)}) copy-start(bf16[4,128,128]{2,1,0:T(8,128)(2,1)} %constant.20.clone.margins) | copy-start | bytes 393220
  14.7 5.7 %collective-permute-start.6 = (bf16[64,128]{1,0:T(8,128)(2,1)S(1)}, bf16[64,128]{1,0:T(8,128)(2,1)S(1)}, u32[]{:S(2)}, u32[]{:S(2)}) collective-permute-start(bf16[64,128]{1,0:T(8,128)(2,1)S(1)} %fields.1.refs_0_), channel_id=1, source_target_pairs={{0,3},{1,2},{2,1},{3,0},{4,5},{5,4},{6,7},{7,6},{8,11},{9,10},{10,... | collective-permute-start | bytes 49160 | tf_op jit(solution)/shard_map/ppermute | solution.py:409
  16.5 4.6 %collective-permute-start.5 = (bf16[64,128]{1,0:T(8,128)(2,1)S(1)}, bf16[64,128]{1,0:T(8,128)(2,1)S(1)}, u32[]{:S(2)}, u32[]{:S(2)}) collective-permute-start(bf16[64,128]{1,0:T(8,128)(2,1)S(1)} %fields.1.refs_0_), channel_id=1, source_target_pairs={{0,2},{1,3},{2,0},{3,1},{4,7},{5,6},{6,5},{7,4},{8,10},{9,11},{10,... | collective-permute-start | bytes 49160 | tf_op jit(solution)/shard_map/ppermute | solution.py:409
  16.8 4.4 %collective-permute-start.4 = (bf16[64,128]{1,0:T(8,128)(2,1)S(1)}, bf16[64,128]{1,0:T(8,128)(2,1)S(1)}, u32[]{:S(2)}, u32[]{:S(2)}) collective-permute-start(bf16[64,128]{1,0:T(8,128)(2,1)S(1)} %fields.1.refs_0_), channel_id=1, source_target_pairs={{0,1},{1,0},{2,3},{3,2},{4,6},{5,7},{6,4},{7,5},{8,9},{9,8},{10,11... | collective-permute-start | bytes 49160 | tf_op jit(solution)/shard_map/ppermute | solution.py:409
  21.2 6.0 %collective-permute-start.8 = (bf16[64,128]{1,0:T(8,128)(2,1)S(1)}, bf16[64,128]{1,0:T(8,128)(2,1)S(1)}, u32[]{:S(2)}, u32[]{:S(2)}) collective-permute-start(bf16[64,128]{1,0:T(8,128)(2,1)S(1)} %total.1.own), channel_id=1, source_target_pairs={{4,8},{8,4},{12,16},{16,12},{20,24},{24,20},{5,9},{9,5},{13,17},{1... | collective-permute-start | bytes 49160 | tf_op jit(solution)/shard_map/ppermute | solution.py:413
  23.5 3.7 %collective-permute-start.7 = (bf16[64,128]{1,0:T(8,128)(2,1)S(1)}, bf16[64,128]{1,0:T(8,128)(2,1)S(1)}, u32[]{:S(2)}, u32[]{:S(2)}) collective-permute-start(bf16[64,128]{1,0:T(8,128)(2,1)S(1)} %total.1.own), channel_id=1, source_target_pairs={{0,4},{4,0},{8,12},{12,8},{16,20},{20,16},{24,28},{28,24},{1,5},{5... | collective-permute-start | bytes 49160 | tf_op jit(solution)/shard_map/ppermute | solution.py:411

commit v8 on v7

--- a/solution.py
+++ b/solution.py
@@ -83,7 +83,7 @@
 
 
 def sum_step(step, tile, count):
-    return (step, (2, 3, 1)[step - 1])[tile % 2] if count == 4 else step
+    return (step, count - step)[tile % 2] if count == 4 else step
 
 
 def destination(k, step, count):

time: 28.5 us -> 28.6 us (level)
    ppermute x1, starting transfers between devices: 2.29 us -> 2.93 us  [per_device(): far = lax.ppermute(own, 'tile', [(t, other_side(t)) for t in inner])]
    ppermute x1, starting transfers between devices: 1.31 us -> 0.67 us  [per_device(): near = lax.ppermute(own, 'tile', [(t, chip_mate(t)) for t in range(tiles)])]
where the time goes in v8:
time: 28.6 us; the launch traced here: 28.3 us
  starting transfers between devices  13.6 us (48%)
  Pallas kernels  8.85 us (31%)
  waiting for transfers between devices  5.07 us (18%)
  between operations  0.75 us (3%)
    pallas_call x7, Pallas kernels, call(): pl.pallas_call(body, name=name, out_shape=outs, in_specs=specs, out_specs...  8.85 us
    ppermute x3, starting transfers between devices, per_device(): parts.append(lax.ppermute(part, both, pairs))  4.45 us
    ppermute x1, starting transfers between devices, per_device(): far = lax.ppermute(own, 'tile', [(t, other_side(t)) for t in inner])  2.93 us
    ppermute x1, starting transfers between devices, per_device(): kernels = [lax.ppermute(side, both, pairs)]  2.65 us
    ppermute x3, waiting for transfers between devices, per_device(): parts.append(lax.ppermute(part, both, pairs))  2.02 us
    ppermute x1, waiting for transfers between devices, per_device(): far = lax.ppermute(own, 'tile', [(t, other_side(t)) for t in inner])  1.83 us
    ppermute x1, starting transfers between devices, per_device(): far_edge = lax.ppermute(other, both, swapped(other_side, 0))  1.61 us
    ppermute x1, starting transfers between devices, per_device(): near_pack = lax.ppermute(mate, both, swapped(chip_mate, 1))  1.18 us
  transfers between devices with their start and end apart: 9, of which 5 were waited for; matrix products, arithmetic and copies ran while one was open for 0% of the time, Pallas kernels for 6%

profile of v8, /device:TPU:4, one launch (start us, length us, event | category | flops | bytes accessed | tf_op | source)
XLA Modules:
  0.0 28.3 jit_solution(11737603127173937260)
XLA Ops:
  0.7 0.0 copy-start
  0.7 1.7 %edges.1 = (bf16[144,128]{1,0:T(8,128)(2,1)S(1)}, bf16[80,128]{1,0:T(8,128)(2,1)S(1)}, bf16[64,128]{1,0:T(8,128)(2,1)S(1)}, bf16[1152,128]{1,0:T(8,128)(2,1)S(1)...) custom-call(bf16[1152,1152]{1,0:T(8,128)(2,1)} %mask.3, ...), custom_call_target="tpu_custom_call" | custom-call | flops 75497472 | bytes 589824 | tf_op jit(solution)/shard_map/edges/pallas_call | solution.py:99
  2.4 2.7 %collective-permute-start.1 = (bf16[64,128]{1,0:T(8,128)(2,1)S(1)}, bf16[64,128]{1,0:T(8,128)(2,1)S(1)}, u32[]{:S(2)}, u32[]{:S(2)}) collective-permute-start(bf16[64,128]{1,0:T(8,128)(2,1)S(1)} %get-tuple-element.22.refs_7_), channel_id=1, source_target_pairs={{0,2},{1,3},{2,0},{3,1},{4,7},{5,6},{6,5},{7,4},{8,10},{9,11},{10,... | collective-permute-start | bytes 49160 | tf_op jit(solution)/shard_map/ppermute | solution.py:363
  5.0 1.6 %collective-permute-start.3 = (bf16[80,128]{1,0:T(8,128)(2,1)S(1)}, bf16[80,128]{1,0:T(8,128)(2,1)S(1)}, u32[]{:S(2)}, u32[]{:S(2)}) collective-permute-start(bf16[80,128]{1,0:T(8,128)(2,1)S(1)} %get-tuple-element.24), channel_id=1, source_target_pairs={{0,28},{1,29},{2,30},{3,31},{4,8},{5,9},{6,10},{7,11},{8,4},{9,5},... | collective-permute-start | bytes 61448 | tf_op jit(solution)/shard_map/ppermute | solution.py:357
  6.7 1.2 %collective-permute-start = (bf16[144,128]{1,0:T(8,128)(2,1)S(1)}, bf16[144,128]{1,0:T(8,128)(2,1)S(1)}, u32[]{:S(2)}, u32[]{:S(2)}) collective-permute-start(bf16[144,128]{1,0:T(8,128)(2,1)S(1)} %get-tuple-element.23), channel_id=1, source_target_pairs={{0,5},{1,4},{2,7},{3,6},{4,1},{5,0},{6,3},{7,2},{8,13},{9,12},{10,... | collective-permute-start | bytes 110600 | tf_op jit(solution)/shard_map/ppermute | solution.py:358
  7.8 0.0 copy-done
  7.8 1.1 %middle.1 = (f32[128,128]{1,0:T(8,128)S(1)}, bf16[2,128,128]{2,1,0:T(8,128)(2,1)S(1)}, bf16[128,288]{1,0:T(8,128)(2,1)S(1)}) custom-call(bf16[1152,1152]{1,0:T(8,128)(2,1)S(1)} %copy-done, bf16[1152,128]{1,0:T(8,128)(2,1)S(1)} %get-tuple-element.15.mid.refs_2_, bf16[128,1152]{1,0:T(8,128)(2,1)S(1)} %get-tuple-element.16.mid_t, ...), custom_call_target="tpu_custom_call" | custom-call | flops 679477248 | bytes 2654208 | tf_op jit(solution)/shard_map/middle/pallas_call | solution.py:99
  8.9 0.0 collective-permute-done.1.value.refs_9_
  9.0 0.1 collective-permute-start.2
  9.0 0.1 collective-permute-done.3.refs_11_.far_edge
  9.2 1.0 %collective-permute-done.2.refs_10_ = bf16[64,128]{1,0:T(8,128)(2,1)S(1)} collective-permute-done((bf16[64,128]{1,0:T(8,128)(2,1)S(1)}, bf16[64,128]{1,0:T(8,128)(2,1)S(1)}, u32[]{:S(2)}, u32[]{:S(2)}) %collective-permute-start.2) | collective-permute-done | bytes 16416 | tf_op jit(solution)/shard_map/ppermute | solution.py:383
  10.2 0.0 collective-permute-done.refs_8_.near_pack
  10.3 0.0 copy-done.3
  10.3 0.0 copy-done.4
  10.3 0.0 copy-done.5
  10.3 0.0 copy-start.1
  10.3 4.4 %fields.1.refs_0_ = bf16[64,128]{1,0:T(8,128)(2,1)S(1)} custom-call(f32[128,128]{1,0:T(8,128)S(1)} %get-tuple-element.19.ready.refs_0_, s32[288,1152]{1,0:T(8,128)S(1)} %copy-done.3, bf16[1152,128]{1,0:T(8,128)(2,1)S(1)} %get-tuple-element.15.mid.refs_2_, bf16[128,288]{1,0:T(8,128)(2,1)S(1)} %get-tuple-element.20.refs_3_, ...), custom_call_target="tpu_custom_call" | custom-call | flops 1358954496 | bytes 1327104 | tf_op jit(solution)/shard_map/fields/pallas_call | solution.py:99
  14.7 0.0 copy-start.2
  14.7 1.8 %collective-permute-start.6 = (bf16[64,128]{1,0:T(8,128)(2,1)S(1)}, bf16[64,128]{1,0:T(8,128)(2,1)S(1)}, u32[]{:S(2)}, u32[]{:S(2)}) collective-permute-start(bf16[64,128]{1,0:T(8,128)(2,1)S(1)} %fields.1.refs_0_), channel_id=1, source_target_pairs={{0,3},{1,2},{2,1},{3,0},{4,5},{5,4},{6,7},{7,6},{8,11},{9,10},{10,... | collective-permute-start | bytes 49160 | tf_op jit(solution)/shard_map/ppermute | solution.py:409
  16.5 0.3 collective-permute-start.5
  16.8 2.4 %collective-permute-start.4 = (bf16[64,128]{1,0:T(8,128)(2,1)S(1)}, bf16[64,128]{1,0:T(8,128)(2,1)S(1)}, u32[]{:S(2)}, u32[]{:S(2)}) collective-permute-start(bf16[64,128]{1,0:T(8,128)(2,1)S(1)} %fields.1.refs_0_), channel_id=1, source_target_pairs={{0,1},{1,0},{2,3},{3,2},{4,7},{5,6},{6,5},{7,4},{8,9},{9,8},{10,11... | collective-permute-start | bytes 49160 | tf_op jit(solution)/shard_map/ppermute | solution.py:409
  19.1 1.1 %collective-permute-done.6.refs_3_ = bf16[64,128]{1,0:T(8,128)(2,1)S(1)} collective-permute-done((bf16[64,128]{1,0:T(8,128)(2,1)S(1)}, bf16[64,128]{1,0:T(8,128)(2,1)S(1)}, u32[]{:S(2)}, u32[]{:S(2)}) %collective-permute-start.6) | collective-permute-done | bytes 16416 | tf_op jit(solution)/shard_map/ppermute | solution.py:409
  20.3 0.9 %collective-permute-done.5.refs_2_ = bf16[64,128]{1,0:T(8,128)(2,1)S(1)} collective-permute-done((bf16[64,128]{1,0:T(8,128)(2,1)S(1)}, bf16[64,128]{1,0:T(8,128)(2,1)S(1)}, u32[]{:S(2)}, u32[]{:S(2)}) %collective-permute-start.5) | collective-permute-done | bytes 16416 | tf_op jit(solution)/shard_map/ppermute | solution.py:409
  21.2 0.0 collective-permute-done.4.refs_1_
  21.2 2.9 %collective-permute-start.8 = (bf16[64,128]{1,0:T(8,128)(2,1)S(1)}, bf16[64,128]{1,0:T(8,128)(2,1)S(1)}, u32[]{:S(2)}, u32[]{:S(2)}) collective-permute-start(bf16[64,128]{1,0:T(8,128)(2,1)S(1)} %total.1.own), channel_id=1, source_target_pairs={{4,8},{8,4},{12,16},{16,12},{20,24},{24,20},{5,9},{9,5},{13,17},{1... | collective-permute-start | bytes 49160 | tf_op jit(solution)/shard_map/ppermute | solution.py:413
  24.1 0.7 %collective-permute-start.7 = (bf16[64,128]{1,0:T(8,128)(2,1)S(1)}, bf16[64,128]{1,0:T(8,128)(2,1)S(1)}, u32[]{:S(2)}, u32[]{:S(2)}) collective-permute-start(bf16[64,128]{1,0:T(8,128)(2,1)S(1)} %total.1.own), channel_id=1, source_target_pairs={{0,4},{4,0},{8,12},{12,8},{16,20},{20,16},{24,28},{28,24},{1,5},{5... | collective-permute-start | bytes 49160 | tf_op jit(solution)/shard_map/ppermute | solution.py:411
  24.8 0.0 copy-done.1
  24.8 0.5 %inner.1.begun = f32[288,1152]{1,0:T(8,128)S(1)} custom-call(bf16[64,128]{1,0:T(8,128)(2,1)S(1)} %total.1.own, bf16[1152,128]{1,0:T(8,128)(2,1)S(1)} %get-tuple-element.15.mid.refs_2_, bf16[128,1152]{1,0:T(8,128)(2,1)S(1)} %copy-done.1), custom_call_target="tpu_custom_call" | custom-call | flops 84934656 | bytes 1327104 | tf_op jit(solution)/shard_map/inner/pallas_call | solution.py:99
  25.3 1.8 %collective-permute-done.8.far = bf16[64,128]{1,0:T(8,128)(2,1)S(1)} collective-permute-done((bf16[64,128]{1,0:T(8,128)(2,1)S(1)}, bf16[64,128]{1,0:T(8,128)(2,1)S(1)}, u32[]{:S(2)}, u32[]{:S(2)}) %collective-permute-start.8) | collective-permute-done | bytes 16416 | tf_op jit(solution)/shard_map/ppermute | solution.py:413
  27.1 0.0 collective-permute-done.7.near
  27.1 0.0 copy-done.2
  27.1 1.1 %outer.1 = f32[288,1152]{1,0:T(8,128)} custom-call(bf16[64,128]{1,0:T(8,128)(2,1)S(1)} %collective-permute-done.7.near, bf16[64,128]{1,0:T(8,128)(2,1)S(1)} %collective-permute-done.8.far, bf16[144,128]{1,0:T(8,128)(2,1)S(1)} %collective-permute-done.refs_8_.near_pack, bf16[80,128]{1,0:T(8,128)(2,1)S(1)} %collective-permute-done.3.refs_11_.far_edge, ...), custom_call_target="tpu_custom_call" | custom-call | flops 56623104 | bytes 294912 | tf_op jit(solution)/shard_map/outer/pallas_call | solution.py:99
  (5 shorter events, 0.0 us)
Async XLA Ops:
  0.7 7.2 %copy-start = (bf16[1152,1152]{1,0:T(8,128)(2,1)S(1)}, bf16[1152,1152]{1,0:T(8,128)(2,1)}, u32[]{:S(2)}) copy-start(bf16[1152,1152]{1,0:T(8,128)(2,1)} %mask.3) | copy-start | bytes 7962628
  2.4 6.5 %collective-permute-start.1 = (bf16[64,128]{1,0:T(8,128)(2,1)S(1)}, bf16[64,128]{1,0:T(8,128)(2,1)S(1)}, u32[]{:S(2)}, u32[]{:S(2)}) collective-permute-start(bf16[64,128]{1,0:T(8,128)(2,1)S(1)} %get-tuple-element.22.refs_7_), channel_id=1, source_target_pairs={{0,2},{1,3},{2,0},{3,1},{4,7},{5,6},{6,5},{7,4},{8,10},{9,11},{10,... | collective-permute-start | bytes 49160 | tf_op jit(solution)/shard_map/ppermute | solution.py:363
  5.0 4.1 %collective-permute-start.3 = (bf16[80,128]{1,0:T(8,128)(2,1)S(1)}, bf16[80,128]{1,0:T(8,128)(2,1)S(1)}, u32[]{:S(2)}, u32[]{:S(2)}) collective-permute-start(bf16[80,128]{1,0:T(8,128)(2,1)S(1)} %get-tuple-element.24), channel_id=1, source_target_pairs={{0,28},{1,29},{2,30},{3,31},{4,8},{5,9},{6,10},{7,11},{8,4},{9,5},... | collective-permute-start | bytes 61448 | tf_op jit(solution)/shard_map/ppermute | solution.py:357
  6.7 3.6 %collective-permute-start = (bf16[144,128]{1,0:T(8,128)(2,1)S(1)}, bf16[144,128]{1,0:T(8,128)(2,1)S(1)}, u32[]{:S(2)}, u32[]{:S(2)}) collective-permute-start(bf16[144,128]{1,0:T(8,128)(2,1)S(1)} %get-tuple-element.23), channel_id=1, source_target_pairs={{0,5},{1,4},{2,7},{3,6},{4,1},{5,0},{6,3},{7,2},{8,13},{9,12},{10,... | collective-permute-start | bytes 110600 | tf_op jit(solution)/shard_map/ppermute | solution.py:358
  7.8 2.4 %copy-start.3 = (s32[288,1152]{1,0:T(8,128)S(1)}, s32[288,1152]{1,0:T(8,128)}, u32[]{:S(2)}) copy-start(s32[288,1152]{1,0:T(8,128)} %refs_1_.1) | copy-start | bytes 3981316
  7.8 2.4 %copy-start.4 = (bf16[9,256,128]{2,1,0:T(8,128)(2,1)S(1)}, bf16[9,256,128]{2,1,0:T(8,128)(2,1)}, u32[]{:S(2)}) copy-start(bf16[9,256,128]{2,1,0:T(8,128)(2,1)} %constant.17.clone.refs_5_) | copy-start | bytes 1769476
  7.8 2.4 %copy-start.5 = (bf16[9,128,256]{2,1,0:T(8,128)(2,1)S(1)}, bf16[9,128,256]{2,1,0:T(8,128)(2,1)}, u32[]{:S(2)}) copy-start(bf16[9,128,256]{2,1,0:T(8,128)(2,1)} %constant.16.clone.refs_4_) | copy-start | bytes 1769476
  9.0 1.2 %collective-permute-start.2 = (bf16[64,128]{1,0:T(8,128)(2,1)S(1)}, bf16[64,128]{1,0:T(8,128)(2,1)S(1)}, u32[]{:S(2)}, u32[]{:S(2)}) collective-permute-start(bf16[64,128]{1,0:T(8,128)(2,1)S(1)} %relay.1), channel_id=1, source_target_pairs={{0,4},{1,5},{2,6},{3,7},{4,0},{5,1},{6,2},{7,3},{8,12},{9,13},{10,... | collective-permute-start | bytes 49160 | tf_op jit(solution)/shard_map/ppermute | solution.py:383
  10.3 14.5 %copy-start.1 = (bf16[128,1152]{1,0:T(8,128)(2,1)S(1)}, bf16[128,1152]{1,0:T(8,128)(2,1)}, u32[]{:S(2)}) copy-start(bf16[128,1152]{1,0:T(8,128)(2,1)} %constant.19.clone.back) | copy-start | bytes 884740
  14.7 12.5 %copy-start.2 = (bf16[4,128,128]{2,1,0:T(8,128)(2,1)S(1)}, bf16[4,128,128]{2,1,0:T(8,128)(2,1)}, u32[]{:S(2)}) copy-start(bf16[4,128,128]{2,1,0:T(8,128)(2,1)} %constant.20.clone.margins) | copy-start | bytes 393220
  14.7 5.6 %collective-permute-start.6 = (bf16[64,128]{1,0:T(8,128)(2,1)S(1)}, bf16[64,128]{1,0:T(8,128)(2,1)S(1)}, u32[]{:S(2)}, u32[]{:S(2)}) collective-permute-start(bf16[64,128]{1,0:T(8,128)(2,1)S(1)} %fields.1.refs_0_), channel_id=1, source_target_pairs={{0,3},{1,2},{2,1},{3,0},{4,5},{5,4},{6,7},{7,6},{8,11},{9,10},{10,... | collective-permute-start | bytes 49160 | tf_op jit(solution)/shard_map/ppermute | solution.py:409
  16.5 4.6 %collective-permute-start.5 = (bf16[64,128]{1,0:T(8,128)(2,1)S(1)}, bf16[64,128]{1,0:T(8,128)(2,1)S(1)}, u32[]{:S(2)}, u32[]{:S(2)}) collective-permute-start(bf16[64,128]{1,0:T(8,128)(2,1)S(1)} %fields.1.refs_0_), channel_id=1, source_target_pairs={{0,2},{1,3},{2,0},{3,1},{4,6},{5,7},{6,4},{7,5},{8,10},{9,11},{10,... | collective-permute-start | bytes 49160 | tf_op jit(solution)/shard_map/ppermute | solution.py:409
  16.8 4.4 %collective-permute-start.4 = (bf16[64,128]{1,0:T(8,128)(2,1)S(1)}, bf16[64,128]{1,0:T(8,128)(2,1)S(1)}, u32[]{:S(2)}, u32[]{:S(2)}) collective-permute-start(bf16[64,128]{1,0:T(8,128)(2,1)S(1)} %fields.1.refs_0_), channel_id=1, source_target_pairs={{0,1},{1,0},{2,3},{3,2},{4,7},{5,6},{6,5},{7,4},{8,9},{9,8},{10,11... | collective-permute-start | bytes 49160 | tf_op jit(solution)/shard_map/ppermute | solution.py:409
  21.2 6.0 %collective-permute-start.8 = (bf16[64,128]{1,0:T(8,128)(2,1)S(1)}, bf16[64,128]{1,0:T(8,128)(2,1)S(1)}, u32[]{:S(2)}, u32[]{:S(2)}) collective-permute-start(bf16[64,128]{1,0:T(8,128)(2,1)S(1)} %total.1.own), channel_id=1, source_target_pairs={{4,8},{8,4},{12,16},{16,12},{20,24},{24,20},{5,9},{9,5},{13,17},{1... | collective-permute-start | bytes 49160 | tf_op jit(solution)/shard_map/ppermute | solution.py:413
  24.1 3.0 %collective-permute-start.7 = (bf16[64,128]{1,0:T(8,128)(2,1)S(1)}, bf16[64,128]{1,0:T(8,128)(2,1)S(1)}, u32[]{:S(2)}, u32[]{:S(2)}) collective-permute-start(bf16[64,128]{1,0:T(8,128)(2,1)S(1)} %total.1.own), channel_id=1, source_target_pairs={{0,4},{4,0},{8,12},{12,8},{16,20},{20,16},{24,28},{28,24},{1,5},{5... | collective-permute-start | bytes 49160 | tf_op jit(solution)/shard_map/ppermute | solution.py:411
